TPU v7x, 128 devices: a whole 4x4x4 slice. The times are simulated.
128 devices in a mesh: dp: 4 (over y), ha: 4 (over z), wa: 8 (over x, core).
Axes of the slice: x: 4, y: 4, z: 4, core: 2. Of those that a mesh axis runs over, the one named last changes fastest.
Arguments:
- left_feat: bfloat16 [4, 32, 192, 128], P('dp', 'ha', 'wa'), may hold values from -512 to 512
- right_feat: bfloat16 [4, 32, 192, 128], P('dp', 'ha', 'wa'), may hold values from -512 to 512
- conv_weight: float32 [8, 3, 3, 3], replicated, may hold values from -1.6 to 1.6
- disparity_gt: int32 [4, 32, 192], P('dp', 'ha', 'wa'), may hold values from 0 to 191
- valid_mask: int32 [4, 32, 192], P('dp', 'ha', 'wa'), may hold values 0 or 1
Outputs:
- loss: float32 [], replicated
- grad_left: float32 [4, 32, 192, 128], P('dp', 'ha', 'wa')
- grad_right: float32 [4, 32, 192, 128], P('dp', 'ha', 'wa')
- grad_weight: float32 [8, 3, 3, 3], replicated
All inputs are finite; a program needn't handle non-finite values. No bound on the sum of `valid_mask` on one device may be relied on, other than what follows from the above.
Results may differ from a plain program's by a relative error of at most 0.009.
Values may be sent and summed in bfloat16 or wider, within the bound.
No kernel may reach another device: no remote copies, remote signals or barrier semaphores. Data moves between devices by JAX's collectives and lax.ppermute only.
A program may use at most 256 MiB of HBM per device.

v0:
```python
import jax
import jax.numpy as jnp
from jax import lax
from jax.sharding import PartitionSpec as P

D = 192


precise = lax.Precision.HIGHEST


def passed_along(value, axis, by):
    count = lax.axis_size(axis)
    pairs = [(i, i + by) for i in range(count) if 0 <= i + by < count]
    return lax.ppermute(value, axis, pairs)


def extended_2(value, sides, width):
    for axis, dim in sides:
        count, length = (lax.axis_size(axis), value.shape[dim])
        up = [(i, (i + 1) % count) for i in range(count - 1)]
        down = [(j, i) for i, j in up]
        last = lax.slice_in_dim(value, length - width, length, axis=dim)
        initial = lax.slice_in_dim(value, 0, width, axis=dim)
        before = lax.ppermute(last, axis, up)
        after = lax.ppermute(initial, axis, down)
        value = jnp.concatenate([before, value, after], axis=dim)
    return value


def skew_levels(products, tile_width, ext_width, levels):
    flipped = products[..., ::-1]
    lead = flipped.shape[:-2]
    flat = flipped.reshape(lead + (tile_width * ext_width,))
    start = tile_width - 1
    window = flat[..., start : start + tile_width * (ext_width - 1)]
    return window.reshape(lead + (tile_width, ext_width - 1))[..., :levels]


def unskew_levels(values, tile_width, ext_width, levels):
    lead = values.shape[:-2]
    padded = jnp.pad(values, [(0, 0)] * len(lead) + [(0, 0), (0, ext_width - 1 - levels)])
    flat = padded.reshape(lead + (tile_width * (ext_width - 1),))
    flat = jnp.pad(flat, [(0, 0)] * len(lead) + [(tile_width - 1, 1)])
    return flat.reshape(lead + (tile_width, ext_width))[..., ::-1]


def taps_forward(padded, weight, row_count, col_count, levels):
    padded = jnp.pad(padded, ((0, 0), (0, 0), (0, 0), (1, 1)))
    running = jnp.zeros((row_count, col_count, levels), jnp.float32)
    for row_tap in range(3):
        for col_tap in range(3):
            window = padded[row_tap : row_tap + row_count, col_tap : col_tap + col_count]
            stacked = jnp.stack([window[..., lev_tap : lev_tap + levels] for lev_tap in range(3)])
            running = running + jnp.einsum(
                "ehwgd,ge->hwd", stacked, weight[:, row_tap, col_tap, :], precision=precise
            )
    return running


def taps_weight(padded, upstream, row_count, col_count, levels):
    padded = jnp.pad(padded, ((0, 0), (0, 0), (0, 0), (1, 1)))
    results = []
    for row_tap in range(3):
        for col_tap in range(3):
            window = padded[row_tap : row_tap + row_count, col_tap : col_tap + col_count]
            stacked = jnp.stack([window[..., lev_tap : lev_tap + levels] for lev_tap in range(3)])
            results.append(jnp.einsum("hwd,ehwgd->ge", upstream, stacked, precision=precise))
    merged = jnp.stack(results, axis=1)
    return merged.reshape(merged.shape[0], 3, 3, 3)


def taps_back(padded, weight, row_count, col_count, levels):
    padded = jnp.pad(padded, ((0, 0), (0, 0), (1, 1)))
    running = jnp.zeros((row_count, col_count, weight.shape[0], levels), jnp.float32)
    for row_tap in range(3):
        for col_tap in range(3):
            window = padded[
                2 - row_tap : 2 - row_tap + row_count, 2 - col_tap : 2 - col_tap + col_count
            ]
            stacked = jnp.stack(
                [window[..., 2 - lev_tap : 2 - lev_tap + levels] for lev_tap in range(3)]
            )
            running = running + jnp.einsum(
                "ehwd,ge->hwgd", stacked, weight[:, row_tap, col_tap, :], precision=precise
            )
    return running


def shards(left_feat, right_feat, conv_weight, disparity_gt, valid_mask):
    left_tile = left_feat[0]
    right_tile = right_feat[0]
    row_count, tile_width, channels = left_tile.shape
    groups = conv_weight.shape[0]
    per_group = channels // groups
    levels = D
    hop_count = (levels + tile_width - 2) // tile_width
    ext_width = (hop_count + 1) * tile_width
    tile_index = lax.axis_index("wa")
    inverse = 1.0 / per_group
    pieces = [right_tile]
    current = right_tile
    for hop_step in range(hop_count):
        current = passed_along(current, "wa", 1)
        pieces.insert(0, current)
    extended = jnp.concatenate(pieces, axis=1)
    left_groups = left_tile.reshape(row_count, tile_width, groups, per_group)
    right_groups = extended.reshape(row_count, ext_width, groups, per_group)
    products = jnp.einsum(
        "hwgc,hjgc->hgwj", left_groups, right_groups, preferred_element_type=jnp.float32
    )
    skewed = skew_levels(products, tile_width, ext_width, levels)
    cost_volume = jnp.transpose(skewed, (0, 2, 1, 3)) * inverse
    cost_padded = extended_2(cost_volume, (("ha", 0), ("wa", 1)), 1)
    logits = taps_forward(cost_padded, conv_weight, row_count, tile_width, levels)
    shifted = logits - jnp.max(logits, axis=-1, keepdims=True)
    weights_exp = jnp.exp(shifted)
    probability = weights_exp / jnp.sum(weights_exp, axis=-1, keepdims=True)
    level_values = jnp.arange(levels, dtype=jnp.float32)
    estimate = jnp.sum(probability * level_values, axis=-1)
    columns = tile_index * tile_width + lax.broadcasted_iota(jnp.int32, (row_count, tile_width), 1)
    usable = (valid_mask[0] * (disparity_gt[0] <= columns).astype(jnp.int32)).astype(jnp.float32)
    residual = estimate - disparity_gt[0].astype(jnp.float32)
    smooth_loss = jnp.where(
        jnp.abs(residual) < 1.0, 0.5 * residual * residual, jnp.abs(residual) - 0.5
    )
    count_local = jnp.sum(usable)
    loss_local = jnp.sum(usable * smooth_loss)
    residual_grad = jnp.clip(residual, -1.0, 1.0) * usable
    count_total = lax.psum(count_local, ("dp", "ha", "wa"))
    upstream = probability * (level_values - estimate[..., None]) * residual_grad[..., None]
    upstream_padded = extended_2(upstream, (("ha", 0), ("wa", 1)), 1)
    grad_cost = taps_back(upstream_padded, conv_weight, row_count, tile_width, levels)
    kernel_local = taps_weight(cost_padded, upstream, row_count, tile_width, levels)
    gcost_low = (grad_cost * inverse).astype(jnp.bfloat16)
    grad_products = unskew_levels(
        jnp.transpose(gcost_low, (0, 2, 1, 3)), tile_width, ext_width, levels
    )
    grad_left = jnp.einsum(
        "hgwj,hjgc->hwgc", grad_products, right_groups, preferred_element_type=jnp.float32
    )
    grad_left = grad_left.reshape(row_count, tile_width, channels)
    grad_ext = jnp.einsum(
        "hgwj,hwgc->hjgc", grad_products, left_groups, preferred_element_type=jnp.float32
    )
    grad_ext = grad_ext.reshape(row_count, ext_width, channels)
    grad_tiles = [
        grad_ext[:, hop_step * tile_width : (hop_step + 1) * tile_width]
        for hop_step in range(hop_count + 1)
    ]
    grad_right = grad_tiles[0]
    for hop_step in range(1, hop_count + 1):
        grad_right = (
            passed_along(grad_right.astype(jnp.bfloat16), "wa", -1).astype(grad_right.dtype)
            + grad_tiles[hop_step]
        )
    loss_total, kernel_total = lax.psum((loss_local, kernel_local), ("dp", "ha", "wa"))
    normaliser = 1.0 / jnp.maximum(count_total, 1.0)
    loss = loss_total * normaliser
    grad_weight = kernel_total * normaliser
    grad_left = grad_left * normaliser
    grad_right = grad_right * normaliser
    return (loss, grad_left[None], grad_right[None], grad_weight)


def solution(mesh):
    placed = (
        P("dp", "ha", "wa", None),
        P("dp", "ha", "wa", None),
        P(),
        P("dp", "ha", "wa"),
        P("dp", "ha", "wa"),
    )
    return jax.shard_map(
        shards,
        mesh=mesh,
        in_specs=placed,
        out_specs=(P(), P("dp", "ha", "wa", None), P("dp", "ha", "wa", None), P()),
        check_vma=False,
    )
```

profile of v0, /device:TPU:1, one launch (start us, length us, event | category | flops | bytes accessed | tf_op | source)
XLA Modules:
  0.0 542.2 jit_solution(3020413413336192321)
XLA Ops:
  0.6 4.5 collective-permute-start
  6.6 4.1 collective-permute-start.1
  11.9 4.2 collective-permute-start.2
  17.3 4.2 collective-permute-start.3
  22.7 4.2 collective-permute-start.4
  28.1 4.2 collective-permute-start.5
  33.5 4.2 collective-permute-start.6
  38.9 4.2 collective-permute-start.7
  46.6 4.0 concatenate.75
  66.1 4.1 collective-permute-done.9
  70.4 4.4 collective-permute-start.10
  85.9 11.7 %slice_bitcast_fusion.23 = (f32[1,8,24,8,192]{4,2,3,1,0:T(8,128)}, f32[1,8,24,8,192]{4,2,3,1,0:T(8,128)}, f32[1,8,24,8,192]{4,2,3,1,0:T(8,128)}, f32[1,8,24,8,19...) fusion(f32[10,26,8,194]{3,1,2,0:T(8,128)S(1)} %select_maximum_f, ...), kind=kLoop, calls=%fused_computation.83 | loop fusion | bytes 42467328 | tf_op jit(solution)/shard_map/stack | solution.py:54
  97.7 3.9 slice_bitcast_fusion.17
  141.2 3.9 fusion.20
  146.2 28.1 %fusion.2 = f32[1,3,8,1,1]{2,0,4,3,1:T(1,128)} fusion(f32[3,8,24,8,192]{4,2,3,1,0:T(8,128)} %copy-done.2, f32[8,24,192,1,1]{2,1,0,3,4:T(8,128)S(1)} %fusion.126), kind=kOutput, calls=%fused_computation.11 | convolution fusion | flops 10616832 | bytes 3686496 | tf_op jit(solution)/shard_map/hwd,ehwgd->ge/dot_general | solution.py:68
  174.4 28.5 %fusion.4 = f32[1,3,8,1,1]{2,0,4,3,1:T(1,128)} fusion(f32[3,8,24,8,192]{4,2,3,1,0:T(8,128)} %copy-done.11, f32[8,24,192,1,1]{2,1,0,3,4:T(8,128)S(1)} %fusion.126), kind=kOutput, calls=%fused_computation.13 | convolution fusion | flops 10616832 | bytes 3686496 | tf_op jit(solution)/shard_map/hwd,ehwgd->ge/dot_general | solution.py:68
  202.9 26.4 %fusion.6 = f32[1,3,8,1,1]{2,0,4,3,1:T(1,128)} fusion(f32[3,8,24,8,192]{4,2,3,1,0:T(8,128)S(1)} %copy-done.10, f32[8,24,192,1,1]{2,1,0,3,4:T(8,128)S(1)} %fusion.126), kind=kOutput, calls=%fused_computation.15 | convolution fusion | flops 10616832 | bytes 3686496 | tf_op jit(solution)/shard_map/hwd,ehwgd->ge/dot_general | solution.py:68
  229.3 28.3 %fusion.8 = f32[1,3,8,1,1]{2,0,4,3,1:T(1,128)} fusion(f32[3,8,24,8,192]{4,2,3,1,0:T(8,128)} %copy-done.8, f32[8,24,192,1,1]{2,1,0,3,4:T(8,128)S(1)} %fusion.126), kind=kOutput, calls=%fused_computation.17 | convolution fusion | flops 10616832 | bytes 3686496 | tf_op jit(solution)/shard_map/hwd,ehwgd->ge/dot_general | solution.py:68
  257.6 26.6 %fusion.10 = f32[1,3,8,1,1]{2,0,4,3,1:T(1,128)} fusion(f32[3,8,24,8,192]{4,2,3,1,0:T(8,128)S(1)} %bitcast.375, f32[8,24,192,1,1]{2,1,0,3,4:T(8,128)S(1)} %fusion.126), kind=kOutput, calls=%fused_computation.19 | convolution fusion | flops 10616832 | bytes 3686496 | tf_op jit(solution)/shard_map/hwd,ehwgd->ge/dot_general | solution.py:68
  284.2 25.8 %fusion.12 = f32[1,3,8,1,1]{2,0,4,3,1:T(1,128)S(1)} fusion(f32[3,8,24,8,192]{4,2,3,1,0:T(8,128)S(1)} %bitcast.373, f32[8,24,192,1,1]{2,1,0,3,4:T(8,128)S(1)} %fusion.126), kind=kOutput, calls=%fused_computation.21 | convolution fusion | flops 10616832 | bytes 3686496 | tf_op jit(solution)/shard_map/hwd,ehwgd->ge/dot_general | solution.py:68
  310.0 25.8 %fusion.14 = f32[1,3,8,1,1]{2,0,4,3,1:T(1,128)S(1)} fusion(f32[3,8,24,8,192]{4,2,3,1,0:T(8,128)S(1)} %bitcast.371, f32[8,24,192,1,1]{2,1,0,3,4:T(8,128)S(1)} %fusion.126), kind=kOutput, calls=%fused_computation.23 | convolution fusion | flops 10616832 | bytes 3686496 | tf_op jit(solution)/shard_map/hwd,ehwgd->ge/dot_general | solution.py:68
  335.8 26.0 %fusion.16 = f32[1,3,8,1,1]{2,0,4,3,1:T(1,128)S(1)} fusion(f32[3,8,24,8,192]{4,2,3,1,0:T(8,128)S(1)} %bitcast.369, f32[8,24,192,1,1]{2,1,0,3,4:T(8,128)S(1)} %fusion.126), kind=kOutput, calls=%fused_computation.25 | convolution fusion | flops 10616832 | bytes 3686496 | tf_op jit(solution)/shard_map/hwd,ehwgd->ge/dot_general | solution.py:68
  361.8 26.2 %fusion.18 = f32[1,3,8,1,1]{2,0,4,3,1:T(1,128)S(1)} fusion(f32[3,8,24,8,192]{4,2,3,1,0:T(8,128)S(1)} %bitcast.367, f32[8,24,192,1,1]{2,1,0,3,4:T(8,128)S(1)} %fusion.126), kind=kOutput, calls=%fused_computation.27 | convolution fusion | flops 10616832 | bytes 3686496 | tf_op jit(solution)/shard_map/hwd,ehwgd->ge/dot_general | solution.py:68
  463.4 65.1 %all-reduce.4 = (f32[]{:T(128)}, f32[]{:T(128)}, f32[8,3,3,3]{0,3,2,1:T(4,128)S(1)}) all-reduce(f32[]{:T(128)} %get-tuple-element.13, f32[]{:T(128)} %get-tuple-element.12, f32[8,3,3,3]{0,3,2,1:T(4,128)} %bitcast.393), channel_id=1, replica_groups=mesh['dp'=4,'ha'=4,'wa'=8] {'dp','ha','wa'}, use_global_device_ids=true, to_apply=%region_4.5 | all-reduce | flops 218 | bytes 1744 | tf_op jit(solution)/shard_map/psum | solution.py:157
  (258 shorter events, 164.7 us)
Async XLA Ops:
  0.6 6.0 %collective-permute-start = (bf16[8,24,128]{2,1,0:T(8,128)(2,1)}, bf16[8,24,128]{2,1,0:T(8,128)(2,1)S(1)}, u32[]{:S(2)}, u32[]{:S(2)}) collective-permute-start(bf16[8,24,128]{2,1,0:T(8,128)(2,1)} %bitcast.392), channel_id=1, source_target_pairs={{0,1},{1,2},{2,3},{3,4},{4,5},{5,6},{6,7},{8,9},{9,10},{10,11},{11... | collective-permute-start | bytes 147464 | tf_op jit(solution)/shard_map/ppermute | solution.py:15
  6.6 5.3 collective-permute-start.1
  11.9 5.4 collective-permute-start.2
  17.3 5.4 collective-permute-start.3
  22.7 5.4 collective-permute-start.4
  28.1 5.4 collective-permute-start.5
  33.5 5.4 collective-permute-start.6
  38.9 7.5 %collective-permute-start.7 = (bf16[8,24,128]{2,1,0:T(8,128)(2,1)S(1)}, bf16[8,24,128]{2,1,0:T(8,128)(2,1)S(1)}, u32[]{:S(2)}, u32[]{:S(2)}) collective-permute-start(bf16[8,24,128]{2,1,0:T(8,128)(2,1)S(1)} %collective-permute-done.6), channel_id=1, source_target_pairs={{0,1},{1,2},{2,3},{3,4},{4,5},{5,6},{6,7},{8,9},{9,10},{10,11},{11... | collective-permute-start | bytes 147464 | tf_op jit(solution)/shard_map/ppermute | solution.py:15
  59.3 6.9 %collective-permute-start.8 = (f32[1,24,8,192]{3,1,2,0:T(8,128)S(1)}, f32[1,24,8,192]{3,1,2,0:T(8,128)S(1)}, u32[]{:S(2)}, u32[]{:S(2)}) collective-permute-start(f32[1,24,8,192]{3,1,2,0:T(8,128)S(1)} %get-tuple-element.49), channel_id=1, source_target_pairs={{0,8},{8,16},{16,24},{1,9},{9,17},{17,25},{2,10},{10,18},{18,26},{... | collective-permute-start | bytes 442376 | tf_op jit(solution)/shard_map/ppermute | solution.py:25
  62.8 7.4 %collective-permute-start.9 = (f32[1,24,8,192]{3,1,2,0:T(8,128)S(1)}, f32[1,24,8,192]{3,1,2,0:T(8,128)S(1)}, u32[]{:S(2)}, u32[]{:S(2)}) collective-permute-start(f32[1,24,8,192]{3,1,2,0:T(8,128)S(1)} %get-tuple-element.50), channel_id=1, source_target_pairs={{8,0},{16,8},{24,16},{9,1},{17,9},{25,17},{10,2},{18,10},{26,18},{... | collective-permute-start | bytes 442376 | tf_op jit(solution)/shard_map/ppermute | solution.py:26
  70.4 8.3 %collective-permute-start.10 = (f32[10,1,8,192]{3,1,2,0:T(1,128)S(1)}, f32[10,1,8,192]{3,1,2,0:T(1,128)S(1)}, u32[]{:S(2)}, u32[]{:S(2)}) collective-permute-start(f32[10,1,8,192]{3,1,2,0:T(1,128)S(1)} %get-tuple-element.43), channel_id=1, source_target_pairs={{0,1},{1,2},{2,3},{3,4},{4,5},{5,6},{6,7},{8,9},{9,10},{10,11},{11... | collective-permute-start | bytes 184328 | tf_op jit(solution)/shard_map/ppermute | solution.py:25
  74.7 5.8 %collective-permute-start.11 = (f32[10,1,8,192]{3,1,2,0:T(1,128)S(1)}, f32[10,1,8,192]{3,1,2,0:T(1,128)S(1)}, u32[]{:S(2)}, u32[]{:S(2)}) collective-permute-start(f32[10,1,8,192]{3,1,2,0:T(1,128)S(1)} %get-tuple-element.44), channel_id=1, source_target_pairs={{1,0},{2,1},{3,2},{4,3},{5,4},{6,5},{7,6},{9,8},{10,9},{11,10},{12... | collective-permute-start | bytes 184328 | tf_op jit(solution)/shard_map/ppermute | solution.py:26
  388.3 5.1 collective-permute-start.12
  392.0 4.6 collective-permute-start.13
  396.6 5.3 collective-permute-start.14
  399.9 5.0 collective-permute-start.15
  428.2 5.8 %collective-permute-start.16 = (bf16[8,24,128]{2,1,0:T(8,128)(2,1)S(1)}, bf16[8,24,128]{2,1,0:T(8,128)(2,1)}, u32[]{:S(2)}, u32[]{:S(2)}) collective-permute-start(bf16[8,24,128]{2,1,0:T(8,128)(2,1)S(1)} %copy.129), channel_id=1, source_target_pairs={{1,0},{2,1},{3,2},{4,3},{5,4},{6,5},{7,6},{9,8},{10,9},{11,10},{12... | collective-permute-start | bytes 147464 | tf_op jit(solution)/shard_map/ppermute | solution.py:15
  434.8 5.5 %collective-permute-start.17 = (bf16[8,24,128]{2,1,0:T(8,128)(2,1)S(1)}, bf16[8,24,128]{2,1,0:T(8,128)(2,1)}, u32[]{:S(2)}, u32[]{:S(2)}) collective-permute-start(bf16[8,24,128]{2,1,0:T(8,128)(2,1)S(1)} %add_convert_fusion.6), channel_id=1, source_target_pairs={{1,0},{2,1},{3,2},{4,3},{5,4},{6,5},{7,6},{9,8},{10,9},{11,10},{12... | collective-permute-start | bytes 147464 | tf_op jit(solution)/shard_map/ppermute | solution.py:15
  441.2 5.5 %collective-permute-start.18 = (bf16[8,24,128]{2,1,0:T(8,128)(2,1)S(1)}, bf16[8,24,128]{2,1,0:T(8,128)(2,1)}, u32[]{:S(2)}, u32[]{:S(2)}) collective-permute-start(bf16[8,24,128]{2,1,0:T(8,128)(2,1)S(1)} %add_convert_fusion.5), channel_id=1, source_target_pairs={{1,0},{2,1},{3,2},{4,3},{5,4},{6,5},{7,6},{9,8},{10,9},{11,10},{12... | collective-permute-start | bytes 147464 | tf_op jit(solution)/shard_map/ppermute | solution.py:15
  447.5 5.5 %collective-permute-start.19 = (bf16[8,24,128]{2,1,0:T(8,128)(2,1)S(1)}, bf16[8,24,128]{2,1,0:T(8,128)(2,1)}, u32[]{:S(2)}, u32[]{:S(2)}) collective-permute-start(bf16[8,24,128]{2,1,0:T(8,128)(2,1)S(1)} %add_convert_fusion.4), channel_id=1, source_target_pairs={{1,0},{2,1},{3,2},{4,3},{5,4},{6,5},{7,6},{9,8},{10,9},{11,10},{12... | collective-permute-start | bytes 147464 | tf_op jit(solution)/shard_map/ppermute | solution.py:15
  453.8 5.5 %collective-permute-start.20 = (bf16[8,24,128]{2,1,0:T(8,128)(2,1)S(1)}, bf16[8,24,128]{2,1,0:T(8,128)(2,1)}, u32[]{:S(2)}, u32[]{:S(2)}) collective-permute-start(bf16[8,24,128]{2,1,0:T(8,128)(2,1)S(1)} %add_convert_fusion.3), channel_id=1, source_target_pairs={{1,0},{2,1},{3,2},{4,3},{5,4},{6,5},{7,6},{9,8},{10,9},{11,10},{12... | collective-permute-start | bytes 147464 | tf_op jit(solution)/shard_map/ppermute | solution.py:15
  460.2 69.2 %collective-permute-start.21 = (bf16[8,24,128]{2,1,0:T(8,128)(2,1)S(1)}, bf16[8,24,128]{2,1,0:T(8,128)(2,1)S(1)}, u32[]{:S(2)}, u32[]{:S(2)}) collective-permute-start(bf16[8,24,128]{2,1,0:T(8,128)(2,1)S(1)} %add_convert_fusion.2), channel_id=1, source_target_pairs={{1,0},{2,1},{3,2},{4,3},{5,4},{6,5},{7,6},{9,8},{10,9},{11,10},{12... | collective-permute-start | bytes 147464 | tf_op jit(solution)/shard_map/ppermute | solution.py:15
  529.4 5.4 collective-permute-start.22
  534.8 5.4 collective-permute-start.23
  (53 other events, 1302.2 us)
where the time goes:
time: 550 us; the launch traced here: 542 us
  matrix products  293 us (53%)
  starting transfers between devices  71.4 us (13%)
  blocking collectives  65.1 us (12%)
  local copies, waits for them, and re-layouts  56.2 us (10%)
  waiting for transfers between devices  31.6 us (6%)
  other arithmetic  19.7 us (4%)
    dot_general x9, matrix products, taps_weight(): jnp.einsum('hwd,ehwgd->ge', upstream, stacked, precision=precise)  242 us
    psum x1, blocking collectives, shards(): lax.psum((loss_local, kernel_local), ('dp', 'ha', 'wa'))  65.1 us
    ppermute x16, starting transfers between devices, passed_along(): return lax.ppermute(value, axis, pairs)  50 us
    dot_general x9, matrix products, taps_forward(): jnp.einsum('ehwgd,ge->hwd', stacked, weight[:, row_tap, col_tap, :], prec...  33.6 us
    unnamed x129, local copies, waits for them, and re-layouts  19.8 us
    another operation x3, local copies, waits for them, and re-layouts, taps_forward(): jnp.stack([window[..., lev_tap:lev_tap + levels] for lev_tap in range(3)])  17.8 us
    ppermute x16, waiting for transfers between devices, passed_along(): return lax.ppermute(value, axis, pairs)  17.4 us
    dot_general x9, matrix products, taps_back(): jnp.einsum('ehwd,ge->hwgd', stacked, weight[:, row_tap, col_tap, :], prec...  17 us
  transfers between devices with their start and end apart: 24, of which 18 were waited for; matrix products, arithmetic and copies ran while one was open for 4% of the time, Pallas kernels for 0%

commit v1 on v0

v1 whole, which is shorter than its diff:
```python
import jax
import jax.numpy as jnp
from jax import lax
from jax.experimental import pallas as pl
from jax.experimental.pallas import tpu as pltpu
from jax.sharding import PartitionSpec as P

F32 = jnp.float32
BF16 = jnp.bfloat16
ROWS, TILE, CH = 8, 24, 128
WA = 8
WT = 192
JP = 256
GT_LANE, VALID_LANE = 0, 16
LOSS_LANE, COUNT_LANE = 9, 10
VMEM = pltpu.CompilerParams(vmem_limit_bytes=48 * 1024 * 1024)
NT = (((1,), (1,)), ((), ()))
NN = (((1,), (0,)), ((), ()))
TN = (((0,), (0,)), ((), ()))


def dot(lhs, rhs, dims=NN, precision=None):
    return lax.dot_general(lhs, rhs, dims, precision=precision, preferred_element_type=F32)


def meta_block(gt, valid, first, count, lane_of_first):
    row = lax.broadcasted_iota(jnp.int32, (ROWS, CH), 0)
    lane = lax.broadcasted_iota(jnp.int32, (ROWS, CH), 1)
    chosen = (row >= first) & (row < first + count)
    at = row - first + lane_of_first
    pick_gt = (chosen & (lane == at + GT_LANE)).astype(F32)
    pick_valid = (chosen & (lane == at + VALID_LANE)).astype(F32)
    return dot(gt, pick_gt, TN) + dot(valid, pick_valid, TN)


def halo_kernel(left_ref, right_ref, gt_ref, valid_ref, up_ref, down_ref):
    gt = gt_ref[...].astype(F32)
    valid = valid_ref[...].astype(F32)
    for i in range(2):
        up_ref[i] = left_ref[ROWS - 2 + i]
        up_ref[2 + i] = right_ref[ROWS - 2 + i]
        down_ref[i] = left_ref[i]
        down_ref[2 + i] = right_ref[i]
    up_ref[4] = meta_block(gt, valid, ROWS - 2, 2, 0).astype(BF16)
    down_ref[4] = meta_block(gt, valid, 0, 2, ROWS + 2).astype(BF16)


def pack_kernel(left_ref, right_ref, gt_ref, valid_ref, prev_ref, next_ref, out_ref):
    gt = gt_ref[...].astype(F32)
    valid = valid_ref[...].astype(F32)
    meta = meta_block(gt, valid, 0, ROWS, 2)
    meta = meta + prev_ref[4].astype(F32) + next_ref[4].astype(F32)
    for side, ref in ((0, left_ref), (1, right_ref)):
        for ext in range(ROWS + 4):
            if ext < 2:
                block = prev_ref[2 * side + ext]
            elif ext < ROWS + 2:
                block = ref[ext - 2]
            else:
                block = next_ref[2 * side + ext - ROWS - 2]
            for k in range(max(0, ext - 4), min(WA - 1, ext) + 1):
                out_ref[k, 5 * side + ext - k] = block
    for k in range(WA):
        rolled = meta if k == 0 else pltpu.roll(meta, CH - k, 1)
        out_ref[k, 10] = rolled.astype(BF16)


def split3(value):
    high = value.astype(BF16)
    rest = value - high.astype(F32)
    middle = rest.astype(BF16)
    low = (rest - middle.astype(F32)).astype(BF16)
    return high, middle, low


def main_kernel(recv_ref, wc_ref, out_ref, ls, rs, rb, lb, ab, ub, utb, xs, ys, zs, ks):
    ks[...] = jnp.zeros(ks.shape, F32)
    xs[...] = jnp.zeros(xs.shape, F32)
    ys[...] = jnp.zeros(ys.shape, F32)
    zs[...] = jnp.zeros(zs.shape, F32)

    @pl.loop(0, 5)
    def fill(rho):
        ls[rho, 0:8] = jnp.zeros((8, CH), F32)
        ls[rho, 8 + WT :] = jnp.zeros((8, CH), F32)
        rs[rho, 0:8] = jnp.zeros((8, CH), F32)
        rs[rho, 8 + WT :] = jnp.zeros((72, CH), F32)
        for src in range(WA):
            at = 8 + TILE * src
            ls[rho, at : at + TILE] = recv_ref[src, rho].astype(F32)
            rs[rho, at : at + TILE] = recv_ref[src, rho + 5].astype(F32)
        for si in range(5):
            rb[rho, :, si * CH : (si + 1) * CH] = rs[rho, 4 + si : 4 + si + JP].astype(BF16)

    lb[WT:] = jnp.zeros((JP - WT, 3 * CH), BF16)
    for b in range(3):
        lb[0:WT, b * CH : (b + 1) * CH] = ls[2, 7 + b : 7 + b + WT].astype(BF16)

    meta = jnp.concatenate([recv_ref[src, 10].astype(F32) for src in range(WA)], axis=0)
    lane = lax.broadcasted_iota(jnp.int32, (WT, CH), 1)
    ww = lax.broadcasted_iota(jnp.int32, (WT, JP), 0)
    jj = lax.broadcasted_iota(jnp.int32, (WT, JP), 1)
    level = (ww - jj + 2).astype(F32)
    inside = (jj <= ww + 2) & (jj >= ww - (WT - 3))
    on_diag = jj == ww + 2
    wcol = lax.broadcasted_iota(jnp.int32, (WT, 1), 0).astype(F32)
    zeros_count = jnp.maximum(float(WT - 3) - wcol, 0.0)
    zeros_mean = (wcol + float(WT + 2)) * 0.5

    def step(q, carry):
        loss_sum, count_sum = carry
        acc = None
        diag = jnp.zeros((WT, CH), F32)
        for a in range(3):
            rho = q + a
            shifted = [ls[rho, 7 + b : 7 + b + WT] for b in range(3)]
            for si in range(5):
                s = si - 2
                value = None
                for b in range(3):
                    e = b - s
                    if 0 <= e <= 2:
                        term = wc_ref[a, 3 * b + e : 3 * b + e + 1] * shifted[b]
                        value = term if value is None else value + term
                for i, part in enumerate(split3(value)):
                    ab[i * WT : (i + 1) * WT, (a * 5 + si) * CH : (a * 5 + si + 1) * CH] = part
            for b in range(3):
                diag = diag + wc_ref[a, 3 * b : 3 * b + 1] * shifted[b] * rs[rho, 8 + b : 8 + b + WT]
            part = dot(ab[:, a * 5 * CH : (a + 1) * 5 * CH], rb[rho], NT)
            acc = part if acc is None else acc + part
        diag_col = jnp.sum(diag, axis=1, keepdims=True)
        logits = acc[0:WT] + acc[WT : 2 * WT] + acc[2 * WT : 3 * WT]
        logits = logits - jnp.where(on_diag, diag_col, 0.0)
        top = jnp.max(jnp.where(inside, logits, -3e38), axis=1, keepdims=True)
        top = jnp.where(zeros_count > 0.0, jnp.maximum(top, 0.0), top)
        expd = jnp.where(inside, jnp.exp(logits - top), 0.0)
        zero_exp = jnp.where(zeros_count > 0.0, zeros_count * jnp.exp(-top), 0.0)
        denom = jnp.sum(expd, axis=1, keepdims=True) + zero_exp
        first = jnp.sum(expd * level, axis=1, keepdims=True) + zero_exp * zeros_mean
        inv = 1.0 / denom
        estimate = first * inv
        target = jnp.sum(jnp.where(lane == GT_LANE + 1 + q, meta, 0.0), axis=1, keepdims=True)
        valid = jnp.sum(jnp.where(lane == VALID_LANE + 1 + q, meta, 0.0), axis=1, keepdims=True)
        usable = jnp.where(target <= wcol, valid, 0.0)
        resid = estimate - target
        size = jnp.abs(resid)
        smooth = jnp.where(size < 1.0, 0.5 * resid * resid, size - 0.5)
        own = jnp.where(q == 1, 1.0, 0.0)
        loss_sum = loss_sum + own * jnp.sum(usable * smooth, axis=0, keepdims=True)
        count_sum = count_sum + own * jnp.sum(usable, axis=0, keepdims=True)
        factor = jnp.clip(resid, -1.0, 1.0) * usable * inv
        up = expd * (level - estimate) * factor
        up_diag = jnp.sum(jnp.where(on_diag, up, 0.0), axis=1, keepdims=True)
        high = up.astype(BF16)
        ub[0:WT] = high
        ub[WT : 2 * WT] = (up - high.astype(F32)).astype(BF16)
        flipped = jnp.concatenate([up, jnp.zeros((JP - WT, JP), F32)], axis=0).T
        high = flipped.astype(BF16)
        utb[0:JP] = high
        utb[JP : 2 * JP] = (flipped - high.astype(F32)).astype(BF16)
        left_terms = dot(ub[...], rb[2])
        left_terms = left_terms[0:WT] + left_terms[WT : 2 * WT]
        right_terms = dot(utb[...], lb[...])
        right_terms = right_terms[0:JP] + right_terms[JP : 2 * JP]
        a = 2 - q
        taps = [[wc_ref[a, 3 * b + e : 3 * b + e + 1] for e in range(3)] for b in range(3)]
        for b in range(3):
            own_left = ls[2, 7 + b : 7 + b + WT]
            lost = up_diag * rs[2, 8 + b : 8 + b + WT]
            total = None
            for e in range(3):
                si = b - e + 2
                value = left_terms[:, si * CH : (si + 1) * CH]
                if e == 0:
                    value = value - lost
                term = taps[b][e] * value
                total = term if total is None else total + term
                ks[a, 3 * b + e : 3 * b + e + 1] = jnp.sum(own_left * value, axis=0, keepdims=True)
            xs[b, 8 : 8 + WT] += total
            zs[b, 8 : 8 + WT] += taps[b][0] * up_diag * own_left
        for si in range(5):
            s = si - 2
            total = None
            for b in range(3):
                e = b - s
                if 0 <= e <= 2:
                    term = taps[b][e] * right_terms[:, b * CH : (b + 1) * CH]
                    total = term if total is None else total + term
            ys[si] += total
        return loss_sum, count_sum

    zero = jnp.zeros((1, 1), F32)
    loss_sum, count_sum = lax.fori_loop(0, 3, step, (zero, zero))

    grad_left = xs[0, 9 : 9 + WT] + xs[1, 8 : 8 + WT] + xs[2, 7 : 7 + WT]
    grad_right = ys[0, 4 : 4 + WT]
    for si in range(1, 5):
        grad_right = grad_right + ys[si, 4 - si : 4 - si + WT]
    for b in range(3):
        grad_right = grad_right - zs[b, 8 - b : 8 - b + WT]
    for dst in range(WA):
        out_ref[dst, 0] = grad_left[TILE * dst : TILE * (dst + 1)].astype(BF16)
        out_ref[dst, 1] = grad_right[TILE * dst : TILE * (dst + 1)].astype(BF16)

    group = lax.broadcasted_iota(jnp.int32, (8, CH), 0)
    channel = lax.broadcasted_iota(jnp.int32, (8, CH), 1)
    member = (channel // 16 == group).astype(F32)
    by_tap = jnp.concatenate([ks[0], ks[1], ks[2], jnp.zeros((CH - 48, CH), F32)], axis=0)
    sums = dot(member, by_tap, NT, precision=lax.Precision.HIGHEST) * (1.0 / 16.0)
    sums = jnp.where(channel == LOSS_LANE, loss_sum, sums)
    sums = jnp.where(channel == COUNT_LANE, count_sum, sums)
    high, middle, low = split3(sums)
    packed = jnp.concatenate([high.astype(F32), middle.astype(F32), low.astype(F32)], axis=0).astype(BF16)
    for dst in range(WA):
        out_ref[dst, 2] = packed


def partial_kernel(recv_ref, out_ref):
    total = recv_ref[0, 2].astype(F32)
    for src in range(1, WA):
        total = total + recv_ref[src, 2].astype(F32)
    total = total[0:8] + total[8:16] + total[16:24]
    for i in range(out_ref.shape[0]):
        out_ref[i] = total


def finish_kernel(recv_ref, sums_ref, left_ref, right_ref, weight_ref, loss_ref):
    total = sums_ref[0]
    for i in range(1, sums_ref.shape[0]):
        total = total + sums_ref[i]
    norm = 1.0 / jnp.maximum(total[0:1, COUNT_LANE : COUNT_LANE + 1], 1.0)
    for src in range(WA):
        left_ref[src] = recv_ref[src, 0].astype(F32) * norm
        right_ref[src] = recv_ref[src, 1].astype(F32) * norm
    weight_ref[...] = total * norm
    loss_ref[...] = total[0:1, LOSS_LANE : LOSS_LANE + 1] * norm


def call(kernel, out_shape, *args, scratch=()):
    return pl.pallas_call(kernel, out_shape=out_shape, scratch_shapes=list(scratch), compiler_params=VMEM)(*args)


def shards(left_feat, right_feat, conv_weight, disparity_gt, valid_mask):
    left, right = left_feat[0], right_feat[0]
    gt, valid = disparity_gt[0], valid_mask[0]
    ha_count = lax.axis_size("ha")
    halo = jax.ShapeDtypeStruct((5, TILE, CH), BF16)
    up, down = call(halo_kernel, (halo, halo), left, right, gt, valid)
    before = lax.ppermute(up, "ha", [(i, i + 1) for i in range(ha_count - 1)])
    after = lax.ppermute(down, "ha", [(i + 1, i) for i in range(ha_count - 1)])
    taps = jnp.repeat(conv_weight.reshape(8, 27).T, 16, axis=1) * (1.0 / 16.0)
    taps = jnp.pad(taps.reshape(3, 9, CH), ((0, 0), (0, 7), (0, 0)))
    packed = call(
        pack_kernel, jax.ShapeDtypeStruct((WA, 11, TILE, CH), BF16), left, right, gt, valid, before, after
    )
    rows = lax.all_to_all(packed, "wa", 0, 0, tiled=True)
    grads = call(
        main_kernel,
        jax.ShapeDtypeStruct((WA, 3, TILE, CH), BF16),
        rows,
        taps,
        scratch=(
            pltpu.VMEM((5, WT + 16, CH), F32),
            pltpu.VMEM((5, WT + 80, CH), F32),
            pltpu.VMEM((5, JP, 5 * CH), BF16),
            pltpu.VMEM((JP, 3 * CH), BF16),
            pltpu.VMEM((3 * WT, 15 * CH), BF16),
            pltpu.VMEM((2 * WT, JP), BF16),
            pltpu.VMEM((2 * JP, JP), BF16),
            pltpu.VMEM((3, WT + 16, CH), F32),
            pltpu.VMEM((5, JP, CH), F32),
            pltpu.VMEM((3, WT + 16, CH), F32),
            pltpu.VMEM((3, 16, CH), F32),
        ),
    )
    back = lax.all_to_all(grads, "wa", 0, 0, tiled=True)
    others = lax.axis_size("dp") * ha_count
    partial = call(partial_kernel, jax.ShapeDtypeStruct((others, 8, CH), F32), back)
    sums = lax.all_to_all(partial, ("dp", "ha"), 0, 0, tiled=True)
    tile = jax.ShapeDtypeStruct((ROWS, TILE, CH), F32)
    grad_left, grad_right, weight, loss = call(
        finish_kernel,
        (tile, tile, jax.ShapeDtypeStruct((8, CH), F32), jax.ShapeDtypeStruct((1, 1), F32)),
        back,
        sums,
    )
    grad_weight = weight[:, :48].reshape(8, 3, 16)[:, :, :9].reshape(8, 3, 3, 3)
    return (loss[0, 0], grad_left[None], grad_right[None], grad_weight)


def solution(mesh):
    placed = (
        P("dp", "ha", "wa", None),
        P("dp", "ha", "wa", None),
        P(),
        P("dp", "ha", "wa"),
        P("dp", "ha", "wa"),
    )
    return jax.shard_map(
        shards,
        mesh=mesh,
        in_specs=placed,
        out_specs=(P(), P("dp", "ha", "wa", None), P("dp", "ha", "wa", None), P()),
        check_vma=False,
    )
```

time: 550 us -> 62.4 us (0.11)
  the two profiles are of different devices: /device:TPU:1 before, /device:TPU:0 now
where the time goes in v1:
time: 62.4 us; the launch traced here: 61.9 us
  blocking collectives  23.8 us (38%)
  waiting for transfers between devices  14.8 us (24%)
  starting transfers between devices  9.63 us (15%)
  Pallas kernels  9.04 us (14%)
  local copies, waits for them, and re-layouts  3.97 us (6%)
  between operations  0.73 us (1%)
    all_to_all x1, blocking collectives, shards(): sums = lax.all_to_all(partial, ('dp', 'ha'), 0, 0, tiled=True)  15.1 us
    all_to_all x1, waiting for transfers between devices, shards(): rows = lax.all_to_all(packed, 'wa', 0, 0, tiled=True)  10.3 us
    pallas_call x5, Pallas kernels, call(): pl.pallas_call(kernel, out_shape=out_shape, scratch_shapes=list(scratch),...  9.04 us
    all_to_all x1, blocking collectives, shards(): back = lax.all_to_all(grads, 'wa', 0, 0, tiled=True)  8.7 us
    all_to_all x1, starting transfers between devices, shards(): rows = lax.all_to_all(packed, 'wa', 0, 0, tiled=True)  4.43 us
    ppermute x1, waiting for transfers between devices, shards(): after = lax.ppermute(down, 'ha', [(i + 1, i) for i in range(ha_count - 1)])  4.23 us
    ppermute x1, starting transfers between devices, shards(): before = lax.ppermute(up, 'ha', [(i, i + 1) for i in range(ha_count - 1)])  3.9 us
    unnamed x11, local copies, waits for them, and re-layouts  3.58 us
  transfers between devices with their start and end apart: 3, of which 3 were waited for; matrix products, arithmetic and copies ran while one was open for 0% of the time, Pallas kernels for 0%

profile of v1, /device:TPU:0, one launch (start us, length us, event | category | flops | bytes accessed | tf_op | source)
XLA Modules:
  0.0 61.9 jit_solution(12676933635975176720)
XLA Ops:
  0.6 0.0 copy-start.2
  0.6 0.7 %copy-done.2 = s32[1,8,24]{2,1,0:T(8,128)S(1)} copy-done((s32[1,8,24]{2,1,0:T(8,128)S(1)}, s32[1,8,24]{2,1,0:T(8,128)}, u32[]{:S(2)}) %copy-start.2) | copy-done | bytes 792
  1.3 0.0 copy-start
  1.3 0.8 %copy-done = bf16[1,8,24,128]{3,2,1,0:T(8,128)(2,1)S(1)} copy-done((bf16[1,8,24,128]{3,2,1,0:T(8,128)(2,1)S(1)}, bf16[1,8,24,128]{3,2,1,0:T(8,128)(2,1)}, u32[]{:S(2)}) %copy-start) | copy-done | bytes 49176
  2.1 0.8 %copy-done.1 = bf16[1,8,24,128]{3,2,1,0:T(8,128)(2,1)S(1)} copy-done((bf16[1,8,24,128]{3,2,1,0:T(8,128)(2,1)S(1)}, bf16[1,8,24,128]{3,2,1,0:T(8,128)(2,1)}, u32[]{:S(2)}) %copy-start.1) | copy-done | bytes 49176
  2.9 0.7 %copy-done.3 = s32[1,8,24]{2,1,0:T(8,128)S(1)} copy-done((s32[1,8,24]{2,1,0:T(8,128)S(1)}, s32[1,8,24]{2,1,0:T(8,128)}, u32[]{:S(2)}) %copy-start.3) | copy-done | bytes 792
  3.6 0.2 shard_map.84
  3.8 3.9 %collective-permute-start = (bf16[5,24,128]{2,1,0:T(8,128)(2,1)S(1)}, bf16[5,24,128]{2,1,0:T(8,128)(2,1)S(1)}, u32[]{:S(2)}, u32[]{:S(2)}) collective-permute-start(bf16[5,24,128]{2,1,0:T(8,128)(2,1)S(1)} %get-tuple-element.10), channel_id=1, source_target_pairs={{0,8},{8,16},{16,24},{1,9},{9,17},{17,25},{2,10},{10,18},{18,26},{... | collective-permute-start | bytes 92168 | tf_op jit(solution)/shard_map/ppermute | solution.py:249
  7.7 1.3 %collective-permute-start.1 = (bf16[5,24,128]{2,1,0:T(8,128)(2,1)S(1)}, bf16[5,24,128]{2,1,0:T(8,128)(2,1)S(1)}, u32[]{:S(2)}, u32[]{:S(2)}) collective-permute-start(bf16[5,24,128]{2,1,0:T(8,128)(2,1)S(1)} %get-tuple-element.11), channel_id=1, source_target_pairs={{8,0},{16,8},{24,16},{9,1},{17,9},{25,17},{10,2},{18,10},{26,18},{... | collective-permute-start | bytes 92168 | tf_op jit(solution)/shard_map/ppermute | solution.py:250
  9.0 0.3 collective-permute-done.prev_ref
  9.3 4.2 %collective-permute-done.1.next_ref = bf16[5,24,128]{2,1,0:T(8,128)(2,1)S(1)} collective-permute-done((bf16[5,24,128]{2,1,0:T(8,128)(2,1)S(1)}, bf16[5,24,128]{2,1,0:T(8,128)(2,1)S(1)}, u32[]{:S(2)}, u32[]{:S(2)}) %collective-permute-start.1) | collective-permute-done | bytes 30752 | tf_op jit(solution)/shard_map/ppermute | solution.py:250
  13.5 1.1 %shard_map.85 = bf16[8,11,24,128]{3,2,1,0:T(8,128)(2,1)} custom-call(bf16[8,24,128]{2,1,0:T(8,128)(2,1)S(1)} %bitcast.14, bf16[8,24,128]{2,1,0:T(8,128)(2,1)S(1)} %bitcast.16, s32[8,24]{1,0:T(8,128)S(1)} %bitcast.18, s32[8,24]{1,0:T(8,128)S(1)} %bitcast.20, bf16[5,24,128]{2,1,0:T(8,128)(2,1)S(1)} %collective-permute-done.prev_ref, ...), custom_call_target="tpu_custom_call" | custom-call | tf_op jit(solution)/shard_map/pallas_call | solution.py:240
  14.6 4.4 %all-to-all-start = ((bf16[8,11,24,128]{3,2,1,0:T(8,128)(2,1)}), bf16[8,11,24,128]{3,2,1,0:T(8,128)(2,1)S(1)}, u32[]{:S(2)}, u32[]{:S(2)}) async-start(bf16[8,11,24,128]{3,2,1,0:T(8,128)(2,1)} %shard_map.85), calls=%async_computation | async-start | bytes 1081344 | tf_op jit(solution)/shard_map/all_to_all | solution.py:256
  19.0 0.0 copy-done.4
  19.0 0.1 broadcast_in_dim.9
  19.1 0.1 mul.21
  19.3 10.3 %all-to-all-done.recv_ref = bf16[8,11,24,128]{3,2,1,0:T(8,128)(2,1)S(1)} async-done(((bf16[8,11,24,128]{3,2,1,0:T(8,128)(2,1)}), bf16[8,11,24,128]{3,2,1,0:T(8,128)(2,1)S(1)}, u32[]{:S(2)}, u32[]{:S(2)}) %all-to-all-start) | async-done | bytes 540704 | tf_op jit(solution)/shard_map/all_to_all | solution.py:256
  29.5 6.9 %shard_map.86 = bf16[8,3,24,128]{3,2,1,0:T(8,128)(2,1)S(1)} custom-call(bf16[8,11,24,128]{3,2,1,0:T(8,128)(2,1)S(1)} %all-to-all-done.recv_ref, f32[3,16,128]{2,1,0:T(8,128)S(1)} %pad.4.wc_ref), custom_call_target="tpu_custom_call" | custom-call | tf_op jit(solution)/shard_map/pallas_call | solution.py:240
  36.5 8.7 %all_to_all.15.recv_ref = bf16[8,3,24,128]{3,2,1,0:T(8,128)(2,1)S(1)} all-to-all(bf16[8,3,24,128]{3,2,1,0:T(8,128)(2,1)S(1)} %shard_map.86), channel_id=1, replica_groups=mesh['dp'=4,'ha'=4,'wa'=8] {'wa'}, dimensions={0} | all-to-all | bytes 294912 | tf_op jit(solution)/shard_map/all_to_all | solution.py:276
  45.2 15.1 %all_to_all.16.sums_ref = f32[16,8,128]{2,1,0:T(8,128)S(1)} all-to-all(f32[16,8,128]{2,1,0:T(8,128)S(1)} %shard_map.87), channel_id=1, replica_groups=mesh['dp'=4,'ha'=4,'wa'=8] {'dp','ha'}, dimensions={0} | all-to-all | bytes 131072 | tf_op jit(solution)/shard_map/all_to_all | solution.py:279
  60.3 0.8 %shard_map.88 = (f32[8,24,128]{2,1,0:T(8,128)}, f32[8,24,128]{2,1,0:T(8,128)}, f32[8,128]{1,0:T(8,128)S(1)}, f32[1,1]{1,0:T(1,128)}) custom-call(bf16[8,3,24,128]{3,2,1,0:T(8,128)(2,1)S(1)} %all_to_all.15.recv_ref, f32[16,8,128]{2,1,0:T(8,128)S(1)} %all_to_all.16.sums_ref), custom_call_target="tpu_custom_call" | custom-call | tf_op jit(solution)/shard_map/pallas_call | solution.py:240
  61.1 0.1 reshape.22
  61.2 0.1 copy.10
  61.3 0.6 copy.11
  (7 shorter events, 0.0 us)
Async XLA Ops:
  0.6 0.7 %copy-start.2 = (s32[1,8,24]{2,1,0:T(8,128)S(1)}, s32[1,8,24]{2,1,0:T(8,128)}, u32[]{:S(2)}) copy-start(s32[1,8,24]{2,1,0:T(8,128)} %param.8) | copy-start | bytes 2308
  1.3 0.8 %copy-start = (bf16[1,8,24,128]{3,2,1,0:T(8,128)(2,1)S(1)}, bf16[1,8,24,128]{3,2,1,0:T(8,128)(2,1)}, u32[]{:S(2)}) copy-start(bf16[1,8,24,128]{3,2,1,0:T(8,128)(2,1)} %param.5) | copy-start | bytes 147460
  2.1 0.8 %copy-start.1 = (bf16[1,8,24,128]{3,2,1,0:T(8,128)(2,1)S(1)}, bf16[1,8,24,128]{3,2,1,0:T(8,128)(2,1)}, u32[]{:S(2)}) copy-start(bf16[1,8,24,128]{3,2,1,0:T(8,128)(2,1)} %param.6) | copy-start | bytes 147460
  2.9 0.7 %copy-start.3 = (s32[1,8,24]{2,1,0:T(8,128)S(1)}, s32[1,8,24]{2,1,0:T(8,128)}, u32[]{:S(2)}) copy-start(s32[1,8,24]{2,1,0:T(8,128)} %param.9) | copy-start | bytes 2308
  3.8 5.5 %collective-permute-start = (bf16[5,24,128]{2,1,0:T(8,128)(2,1)S(1)}, bf16[5,24,128]{2,1,0:T(8,128)(2,1)S(1)}, u32[]{:S(2)}, u32[]{:S(2)}) collective-permute-start(bf16[5,24,128]{2,1,0:T(8,128)(2,1)S(1)} %get-tuple-element.10), channel_id=1, source_target_pairs={{0,8},{8,16},{16,24},{1,9},{9,17},{17,25},{2,10},{10,18},{18,26},{... | collective-permute-start | bytes 92168 | tf_op jit(solution)/shard_map/ppermute | solution.py:249
  7.7 5.8 %collective-permute-start.1 = (bf16[5,24,128]{2,1,0:T(8,128)(2,1)S(1)}, bf16[5,24,128]{2,1,0:T(8,128)(2,1)S(1)}, u32[]{:S(2)}, u32[]{:S(2)}) collective-permute-start(bf16[5,24,128]{2,1,0:T(8,128)(2,1)S(1)} %get-tuple-element.11), channel_id=1, source_target_pairs={{8,0},{16,8},{24,16},{9,1},{17,9},{25,17},{10,2},{18,10},{26,18},{... | collective-permute-start | bytes 92168 | tf_op jit(solution)/shard_map/ppermute | solution.py:250
  14.6 4.4 %copy-start.4 = (f32[8,3,3,3]{0,3,2,1:T(4,128)S(1)}, f32[8,3,3,3]{0,3,2,1:T(4,128)}, u32[]{:S(2)}) copy-start(f32[8,3,3,3]{0,3,2,1:T(4,128)} %param.7) | copy-start | bytes 2596
  14.6 15.0 %all-to-all-start = ((bf16[8,11,24,128]{3,2,1,0:T(8,128)(2,1)}), bf16[8,11,24,128]{3,2,1,0:T(8,128)(2,1)S(1)}, u32[]{:S(2)}, u32[]{:S(2)}) async-start(bf16[8,11,24,128]{3,2,1,0:T(8,128)(2,1)} %shard_map.85), calls=%async_computation | async-start | bytes 1081344 | tf_op jit(solution)/shard_map/all_to_all | solution.py:256

commit v2 on v1

v2 whole, which is shorter than its diff:
```python
import jax
import jax.numpy as jnp
from jax import lax
from jax.experimental import pallas as pl
from jax.experimental.pallas import tpu as pltpu
from jax.sharding import PartitionSpec as P

F32 = jnp.float32
BF16 = jnp.bfloat16
ROWS, TILE, CH = 8, 24, 128
WA, CHIPS = 8, 4
WT = 192
JP = 256
GT_LANE, VALID_LANE = 0, 16
LOSS_LANE, COUNT_LANE = 9, 10
VMEM = pltpu.CompilerParams(vmem_limit_bytes=48 * 1024 * 1024)
FIRST = pltpu.CompilerParams(vmem_limit_bytes=60 * 1024 * 1024)
NT = (((1,), (1,)), ((), ()))
NN = (((1,), (0,)), ((), ()))
TN = (((0,), (0,)), ((), ()))


def dot(lhs, rhs, dims=NN, precision=None):
    return lax.dot_general(lhs, rhs, dims, precision=precision, preferred_element_type=F32)


def meta_block(gt, valid, first, count, lane_of_first):
    row = lax.broadcasted_iota(jnp.int32, (ROWS, CH), 0)
    lane = lax.broadcasted_iota(jnp.int32, (ROWS, CH), 1)
    chosen = (row >= first) & (row < first + count)
    at = row - first + lane_of_first
    pick_gt = (chosen & (lane == at + GT_LANE)).astype(F32)
    pick_valid = (chosen & (lane == at + VALID_LANE)).astype(F32)
    return dot(gt, pick_gt, TN) + dot(valid, pick_valid, TN)


def halo_kernel(left_ref, right_ref, gt_ref, valid_ref, up_ref, down_ref):
    gt = gt_ref[...].astype(F32)
    valid = valid_ref[...].astype(F32)
    for i in range(2):
        up_ref[i] = left_ref[ROWS - 2 + i]
        up_ref[2 + i] = right_ref[ROWS - 2 + i]
        down_ref[i] = left_ref[i]
        down_ref[2 + i] = right_ref[i]
    up_ref[4] = meta_block(gt, valid, ROWS - 2, 2, 0).astype(BF16)
    down_ref[4] = meta_block(gt, valid, 0, 2, ROWS + 2).astype(BF16)


def position():
    index = lax.axis_index("wa")
    return lax.shift_right_logical(index, 1), index & 1


def pack_kernel(left_ref, right_ref, gt_ref, valid_ref, prev_ref, next_ref, *refs):
    outs, ext = refs[:CHIPS], refs[CHIPS]
    chip, _ = position()
    gt = gt_ref[...].astype(F32)
    valid = valid_ref[...].astype(F32)
    meta = meta_block(gt, valid, 0, ROWS, 2)
    meta = (meta + prev_ref[4].astype(F32) + next_ref[4].astype(F32)).astype(BF16)
    for side, ref in ((0, left_ref), (1, right_ref)):
        for i in range(2):
            ext[12 * side + i] = prev_ref[2 * side + i]
            ext[12 * side + ROWS + 2 + i] = next_ref[2 * side + i]
        for i in range(ROWS):
            ext[12 * side + 2 + i] = ref[i]
    for hop in range(CHIPS):
        first = 2 * ((chip + hop) & (CHIPS - 1))
        for i in range(6):
            outs[hop][i] = ext[first + i]
            outs[hop][6 + i] = ext[first + 12 + i]
        outs[hop][12] = meta


def split3(value):
    high = value.astype(BF16)
    rest = value - high.astype(F32)
    middle = rest.astype(BF16)
    low = (rest - middle.astype(F32)).astype(BF16)
    return high, middle, low


def fill(refs, first, count, ls, rs, rb):
    chip, core = position()
    tiles = []
    for hop in range(CHIPS):
        tile = 2 * ((chip - hop) & (CHIPS - 1))
        tiles.append((refs[hop], pl.multiple_of(8 + TILE * (tile + core), 8)))
        tiles.append((refs[CHIPS + hop], pl.multiple_of(8 + TILE * (tile + 1 - core), 8)))

    @pl.loop(first, first + count)
    def row(rho):
        ls[rho, 0:8] = jnp.zeros((8, CH), F32)
        ls[rho, 8 + WT :] = jnp.zeros((8, CH), F32)
        rs[rho, 0:8] = jnp.zeros((8, CH), F32)
        rs[rho, 8 + WT :] = jnp.zeros((72, CH), F32)
        for ref, at in tiles:
            ls[rho, pl.ds(at, TILE)] = ref[core + rho].astype(F32)
            rs[rho, pl.ds(at, TILE)] = ref[6 + core + rho].astype(F32)
        for si in range(5):
            rb[rho, :, si * CH : (si + 1) * CH] = rs[rho, 4 + si : 4 + si + JP].astype(BF16)

    return tiles


def fill_meta(tiles, ms):
    for ref, at in tiles:
        ms[pl.ds(at - 8, TILE)] = ref[12].astype(F32)


def row_gradient(q, wc_ref, ls, rs, rb, ab, ms):
    lane = lax.broadcasted_iota(jnp.int32, (WT, CH), 1)
    ww = lax.broadcasted_iota(jnp.int32, (WT, JP), 0)
    jj = lax.broadcasted_iota(jnp.int32, (WT, JP), 1)
    level = (ww - jj + 2).astype(F32)
    inside = (jj <= ww + 2) & (jj >= ww - (WT - 3))
    on_diag = jj == ww + 2
    wcol = lax.broadcasted_iota(jnp.int32, (WT, 1), 0).astype(F32)
    zeros_count = jnp.maximum(float(WT - 3) - wcol, 0.0)
    zeros_mean = (wcol + float(WT + 2)) * 0.5
    acc = None
    diag = jnp.zeros((WT, CH), F32)
    for a in range(3):
        rho = q + a
        shifted = [ls[rho, 7 + b : 7 + b + WT] for b in range(3)]
        for si in range(5):
            value = None
            for b in range(3):
                e = b - (si - 2)
                if 0 <= e <= 2:
                    term = wc_ref[a, 3 * b + e : 3 * b + e + 1] * shifted[b]
                    value = term if value is None else value + term
            for i, part in enumerate(split3(value)):
                ab[i * WT : (i + 1) * WT, (a * 5 + si) * CH : (a * 5 + si + 1) * CH] = part
        for b in range(3):
            diag = diag + wc_ref[a, 3 * b : 3 * b + 1] * shifted[b] * rs[rho, 8 + b : 8 + b + WT]
        part = dot(ab[:, a * 5 * CH : (a + 1) * 5 * CH], rb[rho], NT)
        acc = part if acc is None else acc + part
    diag_col = jnp.sum(diag, axis=1, keepdims=True)
    logits = acc[0:WT] + acc[WT : 2 * WT] + acc[2 * WT : 3 * WT]
    logits = logits - jnp.where(on_diag, diag_col, 0.0)
    top = jnp.max(jnp.where(inside, logits, -3e38), axis=1, keepdims=True)
    top = jnp.where(zeros_count > 0.0, jnp.maximum(top, 0.0), top)
    expd = jnp.where(inside, jnp.exp(logits - top), 0.0)
    zero_exp = jnp.where(zeros_count > 0.0, zeros_count * jnp.exp(-top), 0.0)
    denom = jnp.sum(expd, axis=1, keepdims=True) + zero_exp
    first = jnp.sum(expd * level, axis=1, keepdims=True) + zero_exp * zeros_mean
    inv = 1.0 / denom
    estimate = first * inv
    ext = lax.axis_index("wa") + 1 + q
    meta = ms[...]
    target = jnp.sum(jnp.where(lane == GT_LANE + ext, meta, 0.0), axis=1, keepdims=True)
    valid = jnp.sum(jnp.where(lane == VALID_LANE + ext, meta, 0.0), axis=1, keepdims=True)
    usable = jnp.where(target <= wcol, valid, 0.0)
    resid = estimate - target
    factor = jnp.clip(resid, -1.0, 1.0) * usable * inv
    up = expd * (level - estimate) * factor
    up_diag = jnp.sum(jnp.where(on_diag, up, 0.0), axis=1, keepdims=True)
    return up, up_diag, resid, usable


def split2(value):
    high = value.astype(BF16)
    return high, (value - high.astype(F32)).astype(BF16)


def sums_kernel(*refs):
    recv, (wc_ref, out_ref, ls, rs, rb, ab, ms, ub, ks) = refs[:8], refs[8:]
    fill_meta(fill(recv, 1, 3, ls, rs, rb), ms)
    ks[...] = jnp.zeros(ks.shape, F32)
    up, up_diag, resid, usable = row_gradient(1, wc_ref, ls, rs, rb, ab, ms)
    size = jnp.abs(resid)
    smooth = jnp.where(size < 1.0, 0.5 * resid * resid, size - 0.5)
    loss_sum = jnp.sum(usable * smooth, axis=0, keepdims=True)
    count_sum = jnp.sum(usable, axis=0, keepdims=True)
    ub[0:WT], ub[WT : 2 * WT] = split2(up)
    for a in range(3):
        terms = dot(ub[...], rb[1 + a])
        terms = terms[0:WT] + terms[WT : 2 * WT]
        for b in range(3):
            left = ls[1 + a, 7 + b : 7 + b + WT]
            for e in range(3):
                si = b - e + 2
                value = terms[:, si * CH : (si + 1) * CH]
                if e == 0:
                    value = value - up_diag * rs[1 + a, 8 + b : 8 + b + WT]
                at = 16 * a + 3 * b + e
                ks[at : at + 1] = jnp.sum(left * value, axis=0, keepdims=True)
    group = lax.broadcasted_iota(jnp.int32, (8, CH), 0)
    channel = lax.broadcasted_iota(jnp.int32, (8, CH), 1)
    member = (channel // 16 == group).astype(F32)
    sums = dot(member, ks[...], NT, precision=lax.Precision.HIGHEST) * (1.0 / 16.0)
    sums = jnp.where(channel == LOSS_LANE, loss_sum, sums)
    sums = jnp.where(channel == COUNT_LANE, count_sum, sums)
    for i in range(out_ref.shape[0]):
        out_ref[i] = sums


def grads_kernel(*refs):
    recv, (wc_ref, out_ref, ls, rs, rb, ab, ms, ub, utb, lb, xs, ys, zs) = refs[:8], refs[8:]
    fill_meta(fill(recv, 0, 5, ls, rs, rb), ms)
    xs[...] = jnp.zeros(xs.shape, F32)
    ys[...] = jnp.zeros(ys.shape, F32)
    zs[...] = jnp.zeros(zs.shape, F32)
    lb[WT:] = jnp.zeros((JP - WT, 3 * CH), BF16)
    for b in range(3):
        lb[0:WT, b * CH : (b + 1) * CH] = ls[2, 7 + b : 7 + b + WT].astype(BF16)

    @pl.loop(0, 3)
    def step(q):
        up, up_diag, _, _ = row_gradient(q, wc_ref, ls, rs, rb, ab, ms)
        ub[0:WT], ub[WT : 2 * WT] = split2(up)
        flipped = jnp.concatenate([up, jnp.zeros((JP - WT, JP), F32)], axis=0).T
        utb[0:JP], utb[JP : 2 * JP] = split2(flipped)
        left_terms = dot(ub[...], rb[2])
        left_terms = left_terms[0:WT] + left_terms[WT : 2 * WT]
        right_terms = dot(utb[...], lb[...])
        right_terms = right_terms[0:JP] + right_terms[JP : 2 * JP]
        a = 2 - q
        taps = [[wc_ref[a, 3 * b + e : 3 * b + e + 1] for e in range(3)] for b in range(3)]
        for b in range(3):
            total = -taps[b][0] * up_diag * rs[2, 8 + b : 8 + b + WT]
            for e in range(3):
                si = b - e + 2
                total = total + taps[b][e] * left_terms[:, si * CH : (si + 1) * CH]
            xs[b, 8 : 8 + WT] += total
            zs[b, 8 : 8 + WT] += taps[b][0] * up_diag * ls[2, 7 + b : 7 + b + WT]
        for si in range(5):
            total = None
            for b in range(3):
                e = b - (si - 2)
                if 0 <= e <= 2:
                    term = taps[b][e] * right_terms[:, b * CH : (b + 1) * CH]
                    total = term if total is None else total + term
            ys[si] += total

    grad_left = xs[0, 9 : 9 + WT] + xs[1, 8 : 8 + WT] + xs[2, 7 : 7 + WT]
    grad_right = ys[0, 4 : 4 + WT]
    for si in range(1, 5):
        grad_right = grad_right + ys[si, 4 - si : 4 - si + WT]
    for b in range(3):
        grad_right = grad_right - zs[b, 8 - b : 8 - b + WT]
    for dst in range(WA):
        out_ref[dst, 0] = grad_left[TILE * dst : TILE * (dst + 1)].astype(BF16)
        out_ref[dst, 1] = grad_right[TILE * dst : TILE * (dst + 1)].astype(BF16)


def payload_kernel(grads_ref, sums_ref, out_ref):
    total = sums_ref[0]
    for i in range(1, sums_ref.shape[0]):
        total = total + sums_ref[i]
    parts = [part.astype(F32) for part in split3(total)]
    packed = jnp.concatenate(parts, axis=0).astype(BF16)
    for dst in range(WA):
        out_ref[dst, 0] = grads_ref[dst, 0]
        out_ref[dst, 1] = grads_ref[dst, 1]
        out_ref[dst, 2] = packed


def finish_kernel(recv_ref, left_ref, right_ref, weight_ref, loss_ref):
    total = recv_ref[0, 2].astype(F32)
    for src in range(1, WA):
        total = total + recv_ref[src, 2].astype(F32)
    total = total[0:8] + total[8:16] + total[16:24]
    norm = 1.0 / jnp.maximum(total[0:1, COUNT_LANE : COUNT_LANE + 1], 1.0)
    for src in range(WA):
        left_ref[src] = recv_ref[src, 0].astype(F32) * norm
        right_ref[src] = recv_ref[src, 1].astype(F32) * norm
    loss_ref[...] = total[0:1, LOSS_LANE : LOSS_LANE + 1] * norm
    by_tap = jnp.concatenate([total * norm, jnp.zeros((CH - 8, CH), F32)], axis=0).T
    for a in range(3):
        for b in range(3):
            at = 16 * a + 3 * b
            weight_ref[a, b] = by_tap[at : at + 3, 0:8]


def call(kernel, out_shape, *args, scratch=(), flops=0, params=VMEM):
    cost = pl.CostEstimate(flops=flops, bytes_accessed=1 << 20, transcendentals=0)
    return pl.pallas_call(
        kernel, out_shape=out_shape, scratch_shapes=list(scratch), compiler_params=params, cost_estimate=cost
    )(*args)


def shards(left_feat, right_feat, conv_weight, disparity_gt, valid_mask):
    left, right = left_feat[0], right_feat[0]
    gt, valid = disparity_gt[0], valid_mask[0]
    ha_count = lax.axis_size("ha")
    halo = jax.ShapeDtypeStruct((5, TILE, CH), BF16)
    up, down = call(halo_kernel, (halo, halo), left, right, gt, valid, params=FIRST)
    before = lax.ppermute(up, "ha", [(i, i + 1) for i in range(ha_count - 1)])
    after = lax.ppermute(down, "ha", [(i + 1, i) for i in range(ha_count - 1)])
    taps = jnp.repeat(conv_weight.reshape(8, 27).T, 16, axis=1) * (1.0 / 16.0)
    taps = jnp.pad(taps.reshape(3, 9, CH), ((0, 0), (0, 7), (0, 0)))
    block = jax.ShapeDtypeStruct((13, TILE, CH), BF16)
    blocks = call(
        pack_kernel,
        (block,) * CHIPS,
        left,
        right,
        gt,
        valid,
        before,
        after,
        scratch=(pltpu.VMEM((24, TILE, CH), BF16),),
    )
    same_core = [blocks[0]]
    for hop in range(1, CHIPS):
        same_core.append(lax.ppermute(blocks[hop], "wa", [(i, (i + 2 * hop) % WA) for i in range(WA)]))
    other_core = [lax.ppermute(value, "wa", [(i, i ^ 1) for i in range(WA)]) for value in same_core]
    tiles = same_core + other_core
    shared = (
        pltpu.VMEM((5, WT + 16, CH), F32),
        pltpu.VMEM((5, WT + 80, CH), F32),
        pltpu.VMEM((5, JP, 5 * CH), BF16),
        pltpu.VMEM((3 * WT, 15 * CH), BF16),
        pltpu.VMEM((WT, CH), F32),
        pltpu.VMEM((2 * WT, JP), BF16),
    )
    others = lax.axis_size("dp") * ha_count
    sums = call(
        sums_kernel,
        jax.ShapeDtypeStruct((others, 8, CH), F32),
        *tiles,
        taps,
        scratch=shared + (pltpu.VMEM((CH, CH), F32),),
        flops=1 << 30,
    )
    sums = lax.all_to_all(sums, ("dp", "ha"), 0, 0, tiled=True)
    grads = call(
        grads_kernel,
        jax.ShapeDtypeStruct((WA, 2, TILE, CH), BF16),
        *tiles,
        taps,
        scratch=shared
        + (
            pltpu.VMEM((2 * JP, JP), BF16),
            pltpu.VMEM((JP, 3 * CH), BF16),
            pltpu.VMEM((3, WT + 16, CH), F32),
            pltpu.VMEM((5, JP, CH), F32),
            pltpu.VMEM((3, WT + 16, CH), F32),
        ),
        flops=5 << 30,
    )
    payload = call(payload_kernel, jax.ShapeDtypeStruct((WA, 3, TILE, CH), BF16), grads, sums)
    back = lax.all_to_all(payload, "wa", 0, 0, tiled=True)
    tile = jax.ShapeDtypeStruct((ROWS, TILE, CH), F32)
    grad_left, grad_right, weight, loss = call(
        finish_kernel,
        (tile, tile, jax.ShapeDtypeStruct((3, 3, 3, 8), F32), jax.ShapeDtypeStruct((1, 1), F32)),
        back,
    )
    return (loss[0, 0], grad_left[None], grad_right[None], jnp.transpose(weight, (3, 0, 1, 2)))


def solution(mesh):
    placed = (
        P("dp", "ha", "wa", None),
        P("dp", "ha", "wa", None),
        P(),
        P("dp", "ha", "wa"),
        P("dp", "ha", "wa"),
    )
    return jax.shard_map(
        shards,
        mesh=mesh,
        in_specs=placed,
        out_specs=(P(), P("dp", "ha", "wa", None), P("dp", "ha", "wa", None), P()),
        check_vma=False,
    )
```

time: 62.4 us -> 53.3 us (0.85)
  the two profiles are of different devices: /device:TPU:0 before, /device:TPU:1 now
where the time goes in v2:
time: 53.3 us; the launch traced here: 52.9 us
  starting transfers between devices  23.6 us (44%)
  Pallas kernels  13.3 us (25%)
  blocking collectives  10.7 us (20%)
  waiting for transfers between devices  4.39 us (8%)
  between operations  0.8 us (2%)
    pallas_call x6, Pallas kernels, call(): pl.pallas_call(kernel, out_shape=out_shape, scratch_shapes=list(scratch),...  13.3 us
    all_to_all x1, blocking collectives, shards(): back = lax.all_to_all(payload, 'wa', 0, 0, tiled=True)  10.7 us
    all_to_all x1, starting transfers between devices, shards(): sums = lax.all_to_all(sums, ('dp', 'ha'), 0, 0, tiled=True)  7.32 us
    ppermute x4, starting transfers between devices, shards(): lax.ppermute(value, 'wa', [(i, i ^ 1) for i in range(WA)])  5.73 us
    ppermute x3, starting transfers between devices, shards(): lax.ppermute(blocks[hop], 'wa', [(i, (i + 2 * hop) % WA) for i in range(W...  4.88 us
    ppermute x1, starting transfers between devices, shards(): before = lax.ppermute(up, 'ha', [(i, i + 1) for i in range(ha_count - 1)])  4.36 us
    ppermute x1, waiting for transfers between devices, shards(): after = lax.ppermute(down, 'ha', [(i + 1, i) for i in range(ha_count - 1)])  3.72 us
    ppermute x1, starting transfers between devices, shards(): after = lax.ppermute(down, 'ha', [(i + 1, i) for i in range(ha_count - 1)])  1.29 us
  transfers between devices with their start and end apart: 10, of which 2 were waited for; matrix products, arithmetic and copies ran while one was open for 0% of the time, Pallas kernels for 13%

profile of v2, /device:TPU:1, one launch (start us, length us, event | category | flops | bytes accessed | tf_op | source)
XLA Modules:
  0.0 52.9 jit_solution(4877527483254806594)
XLA Ops:
  0.7 1.7 %shard_map.84 = (bf16[5,24,128]{2,1,0:T(8,128)(2,1)}, bf16[5,24,128]{2,1,0:T(8,128)(2,1)}) custom-call(bf16[8,24,128]{2,1,0:T(8,128)(2,1)} %bitcast.11, bf16[8,24,128]{2,1,0:T(8,128)(2,1)} %bitcast.13, s32[8,24]{1,0:T(8,128)} %bitcast.15, s32[8,24]{1,0:T(8,128)} %bitcast.17), custom_call_target="tpu_custom_call" | custom-call | bytes 1048576 | tf_op jit(solution)/shard_map/pallas_call | solution.py:279
  2.4 4.4 %collective-permute-start = (bf16[5,24,128]{2,1,0:T(8,128)(2,1)}, bf16[5,24,128]{2,1,0:T(8,128)(2,1)S(1)}, u32[]{:S(2)}, u32[]{:S(2)}) collective-permute-start(bf16[5,24,128]{2,1,0:T(8,128)(2,1)} %get-tuple-element.14), channel_id=1, source_target_pairs={{0,8},{8,16},{16,24},{1,9},{9,17},{17,25},{2,10},{10,18},{18,26},{... | collective-permute-start | bytes 92168 | tf_op jit(solution)/shard_map/ppermute | solution.py:290
  6.7 1.3 %collective-permute-start.1 = (bf16[5,24,128]{2,1,0:T(8,128)(2,1)}, bf16[5,24,128]{2,1,0:T(8,128)(2,1)S(1)}, u32[]{:S(2)}, u32[]{:S(2)}) collective-permute-start(bf16[5,24,128]{2,1,0:T(8,128)(2,1)} %get-tuple-element.15), channel_id=1, source_target_pairs={{8,0},{16,8},{24,16},{9,1},{17,9},{25,17},{10,2},{18,10},{26,18},{... | collective-permute-start | bytes 92168 | tf_op jit(solution)/shard_map/ppermute | solution.py:291
  8.0 0.0 collective-permute-done.prev_ref
  8.0 3.7 %collective-permute-done.1.next_ref = bf16[5,24,128]{2,1,0:T(8,128)(2,1)S(1)} collective-permute-done((bf16[5,24,128]{2,1,0:T(8,128)(2,1)}, bf16[5,24,128]{2,1,0:T(8,128)(2,1)S(1)}, u32[]{:S(2)}, u32[]{:S(2)}) %collective-permute-start.1) | collective-permute-done | bytes 30752 | tf_op jit(solution)/shard_map/ppermute | solution.py:291
  11.8 0.0 copy-start.4
  11.8 0.2 shard_map.85
  12.0 1.3 %collective-permute-start.2 = (bf16[13,24,128]{2,1,0:T(8,128)(2,1)S(1)}, bf16[13,24,128]{2,1,0:T(8,128)(2,1)S(1)}, u32[]{:S(2)}, u32[]{:S(2)}) collective-permute-start(bf16[13,24,128]{2,1,0:T(8,128)(2,1)S(1)} %get-tuple-element.17), channel_id=1, source_target_pairs={{0,2},{1,3},{2,4},{3,5},{4,6},{5,7},{6,0},{7,1},{8,10},{9,11},{10,... | collective-permute-start | bytes 239624 | tf_op jit(solution)/shard_map/ppermute | solution.py:308
  13.3 2.5 %collective-permute-start.3 = (bf16[13,24,128]{2,1,0:T(8,128)(2,1)S(1)}, bf16[13,24,128]{2,1,0:T(8,128)(2,1)S(1)}, u32[]{:S(2)}, u32[]{:S(2)}) collective-permute-start(bf16[13,24,128]{2,1,0:T(8,128)(2,1)S(1)} %get-tuple-element.18), channel_id=1, source_target_pairs={{0,4},{1,5},{2,6},{3,7},{4,0},{5,1},{6,2},{7,3},{8,12},{9,13},{10,... | collective-permute-start | bytes 239624 | tf_op jit(solution)/shard_map/ppermute | solution.py:308
  15.7 1.2 %collective-permute-start.4 = (bf16[13,24,128]{2,1,0:T(8,128)(2,1)S(1)}, bf16[13,24,128]{2,1,0:T(8,128)(2,1)S(1)}, u32[]{:S(2)}, u32[]{:S(2)}) collective-permute-start(bf16[13,24,128]{2,1,0:T(8,128)(2,1)S(1)} %get-tuple-element.19), channel_id=1, source_target_pairs={{0,6},{1,7},{2,0},{3,1},{4,2},{5,3},{6,4},{7,5},{8,14},{9,15},{10,... | collective-permute-start | bytes 239624 | tf_op jit(solution)/shard_map/ppermute | solution.py:308
  16.9 2.8 %collective-permute-start.5 = (bf16[13,24,128]{2,1,0:T(8,128)(2,1)S(1)}, bf16[13,24,128]{2,1,0:T(8,128)(2,1)S(1)}, u32[]{:S(2)}, u32[]{:S(2)}) collective-permute-start(bf16[13,24,128]{2,1,0:T(8,128)(2,1)S(1)} %get-tuple-element.16.refs_0_), channel_id=1, source_target_pairs={{0,1},{1,0},{2,3},{3,2},{4,5},{5,4},{6,7},{7,6},{8,9},{9,8},{10,11... | collective-permute-start | bytes 239624 | tf_op jit(solution)/shard_map/ppermute | solution.py:309
  19.6 0.0 collective-permute-done.2.refs_1_
  19.6 0.3 collective-permute-start.6
  19.9 0.0 collective-permute-done.3.refs_2_
  19.9 1.5 %collective-permute-start.7 = (bf16[13,24,128]{2,1,0:T(8,128)(2,1)S(1)}, bf16[13,24,128]{2,1,0:T(8,128)(2,1)S(1)}, u32[]{:S(2)}, u32[]{:S(2)}) collective-permute-start(bf16[13,24,128]{2,1,0:T(8,128)(2,1)S(1)} %collective-permute-done.3.refs_2_), channel_id=1, source_target_pairs={{0,1},{1,0},{2,3},{3,2},{4,5},{5,4},{6,7},{7,6},{8,9},{9,8},{10,11... | collective-permute-start | bytes 239624 | tf_op jit(solution)/shard_map/ppermute | solution.py:309
  21.4 1.2 %collective-permute-start.8 = (bf16[13,24,128]{2,1,0:T(8,128)(2,1)S(1)}, bf16[13,24,128]{2,1,0:T(8,128)(2,1)S(1)}, u32[]{:S(2)}, u32[]{:S(2)}) collective-permute-start(bf16[13,24,128]{2,1,0:T(8,128)(2,1)S(1)} %collective-permute-done.4.refs_3_), channel_id=1, source_target_pairs={{0,1},{1,0},{2,3},{3,2},{4,5},{5,4},{6,7},{7,6},{8,9},{9,8},{10,11... | collective-permute-start | bytes 239624 | tf_op jit(solution)/shard_map/ppermute | solution.py:309
  22.6 0.1 broadcast_in_dim.9
  22.7 0.1 mul.21
  22.9 0.6 %collective-permute-done.8.refs_7_ = bf16[13,24,128]{2,1,0:T(8,128)(2,1)S(1)} collective-permute-done((bf16[13,24,128]{2,1,0:T(8,128)(2,1)S(1)}, bf16[13,24,128]{2,1,0:T(8,128)(2,1)S(1)}, u32[]{:S(2)}, u32[]{:S(2)}) %collective-permute-start.8) | collective-permute-done | bytes 79904 | tf_op jit(solution)/shard_map/ppermute | solution.py:309
  23.5 3.8 %shard_map.87 = f32[16,8,128]{2,1,0:T(8,128)} custom-call(bf16[13,24,128]{2,1,0:T(8,128)(2,1)S(1)} %get-tuple-element.16.refs_0_, bf16[13,24,128]{2,1,0:T(8,128)(2,1)S(1)} %collective-permute-done.2.refs_1_, bf16[13,24,128]{2,1,0:T(8,128)(2,1)S(1)} %collective-permute-done.3.refs_2_, bf16[13,24,128]{2,1,0:T(8,128)(2,1)S(1)} %collective-permute-done.4.refs_3_, ...), custom_call_target="tpu_custom_call" | custom-call | flops 1073741824 | bytes 1048576 | tf_op jit(solution)/shard_map/pallas_call | solution.py:279
  27.3 7.3 %all-to-all-start = ((f32[16,8,128]{2,1,0:T(8,128)}), f32[16,8,128]{2,1,0:T(8,128)S(1)}, u32[]{:S(2)}, u32[]{:S(2)}) async-start(f32[16,8,128]{2,1,0:T(8,128)} %shard_map.87), calls=%async_computation | async-start | bytes 131072 | tf_op jit(solution)/shard_map/all_to_all | solution.py:328
  34.7 6.7 %shard_map.86.grads_ref = bf16[8,2,24,128]{3,2,1,0:T(8,128)(2,1)S(1)} custom-call(bf16[13,24,128]{2,1,0:T(8,128)(2,1)S(1)} %get-tuple-element.16.refs_0_, bf16[13,24,128]{2,1,0:T(8,128)(2,1)S(1)} %collective-permute-done.2.refs_1_, bf16[13,24,128]{2,1,0:T(8,128)(2,1)S(1)} %collective-permute-done.3.refs_2_, ...), custom_call_target="tpu_custom_call" | custom-call | flops 5368709120 | bytes 1048576 | tf_op jit(solution)/shard_map/pallas_call | solution.py:279
  41.4 10.7 %all_to_all.10.recv_ref = bf16[8,3,24,128]{3,2,1,0:T(8,128)(2,1)S(1)} all-to-all(bf16[8,3,24,128]{3,2,1,0:T(8,128)(2,1)S(1)} %shard_map.88), channel_id=1, replica_groups=mesh['dp'=4,'ha'=4,'wa'=8] {'wa'}, dimensions={0} | all-to-all | bytes 294912 | tf_op jit(solution)/shard_map/all_to_all | solution.py:345
  52.1 0.8 %shard_map.89 = (f32[8,24,128]{2,1,0:T(8,128)}, f32[8,24,128]{2,1,0:T(8,128)}, f32[3,3,3,8]{3,2,1,0:T(4,128)}, f32[1,1]{1,0:T(1,128)}) custom-call(bf16[8,3,24,128]{3,2,1,0:T(8,128)(2,1)S(1)} %all_to_all.10.recv_ref), custom_call_target="tpu_custom_call" | custom-call | bytes 1048576 | tf_op jit(solution)/shard_map/pallas_call | solution.py:279
  (18 shorter events, 0.1 us)
Async XLA Ops:
  0.6 11.1 %copy-start = (bf16[1,8,24,128]{3,2,1,0:T(8,128)(2,1)S(1)}, bf16[1,8,24,128]{3,2,1,0:T(8,128)(2,1)}, u32[]{:S(2)}) copy-start(bf16[1,8,24,128]{3,2,1,0:T(8,128)(2,1)} %param.5) | copy-start | bytes 147460
  0.6 11.1 %copy-start.1 = (bf16[1,8,24,128]{3,2,1,0:T(8,128)(2,1)S(1)}, bf16[1,8,24,128]{3,2,1,0:T(8,128)(2,1)}, u32[]{:S(2)}) copy-start(bf16[1,8,24,128]{3,2,1,0:T(8,128)(2,1)} %param.6) | copy-start | bytes 147460
  0.7 11.1 %copy-start.2 = (s32[1,8,24]{2,1,0:T(8,128)S(1)}, s32[1,8,24]{2,1,0:T(8,128)}, u32[]{:S(2)}) copy-start(s32[1,8,24]{2,1,0:T(8,128)} %param.8) | copy-start | bytes 2308
  0.7 11.1 %copy-start.3 = (s32[1,8,24]{2,1,0:T(8,128)S(1)}, s32[1,8,24]{2,1,0:T(8,128)}, u32[]{:S(2)}) copy-start(s32[1,8,24]{2,1,0:T(8,128)} %param.9) | copy-start | bytes 2308
  2.4 5.7 %collective-permute-start = (bf16[5,24,128]{2,1,0:T(8,128)(2,1)}, bf16[5,24,128]{2,1,0:T(8,128)(2,1)S(1)}, u32[]{:S(2)}, u32[]{:S(2)}) collective-permute-start(bf16[5,24,128]{2,1,0:T(8,128)(2,1)} %get-tuple-element.14), channel_id=1, source_target_pairs={{0,8},{8,16},{16,24},{1,9},{9,17},{17,25},{2,10},{10,18},{18,26},{... | collective-permute-start | bytes 92168 | tf_op jit(solution)/shard_map/ppermute | solution.py:290
  6.7 5.0 %collective-permute-start.1 = (bf16[5,24,128]{2,1,0:T(8,128)(2,1)}, bf16[5,24,128]{2,1,0:T(8,128)(2,1)S(1)}, u32[]{:S(2)}, u32[]{:S(2)}) collective-permute-start(bf16[5,24,128]{2,1,0:T(8,128)(2,1)} %get-tuple-element.15), channel_id=1, source_target_pairs={{8,0},{16,8},{24,16},{9,1},{17,9},{25,17},{10,2},{18,10},{26,18},{... | collective-permute-start | bytes 92168 | tf_op jit(solution)/shard_map/ppermute | solution.py:291
  11.8 10.8 %copy-start.4 = (f32[8,3,3,3]{0,3,2,1:T(4,128)S(1)}, f32[8,3,3,3]{0,3,2,1:T(4,128)}, u32[]{:S(2)}) copy-start(f32[8,3,3,3]{0,3,2,1:T(4,128)} %param.7) | copy-start | bytes 2596
  12.0 7.6 %collective-permute-start.2 = (bf16[13,24,128]{2,1,0:T(8,128)(2,1)S(1)}, bf16[13,24,128]{2,1,0:T(8,128)(2,1)S(1)}, u32[]{:S(2)}, u32[]{:S(2)}) collective-permute-start(bf16[13,24,128]{2,1,0:T(8,128)(2,1)S(1)} %get-tuple-element.17), channel_id=1, source_target_pairs={{0,2},{1,3},{2,4},{3,5},{4,6},{5,7},{6,0},{7,1},{8,10},{9,11},{10,... | collective-permute-start | bytes 239624 | tf_op jit(solution)/shard_map/ppermute | solution.py:308
  13.3 6.7 %collective-permute-start.3 = (bf16[13,24,128]{2,1,0:T(8,128)(2,1)S(1)}, bf16[13,24,128]{2,1,0:T(8,128)(2,1)S(1)}, u32[]{:S(2)}, u32[]{:S(2)}) collective-permute-start(bf16[13,24,128]{2,1,0:T(8,128)(2,1)S(1)} %get-tuple-element.18), channel_id=1, source_target_pairs={{0,4},{1,5},{2,6},{3,7},{4,0},{5,1},{6,2},{7,3},{8,12},{9,13},{10,... | collective-permute-start | bytes 239624 | tf_op jit(solution)/shard_map/ppermute | solution.py:308
  15.7 5.7 %collective-permute-start.4 = (bf16[13,24,128]{2,1,0:T(8,128)(2,1)S(1)}, bf16[13,24,128]{2,1,0:T(8,128)(2,1)S(1)}, u32[]{:S(2)}, u32[]{:S(2)}) collective-permute-start(bf16[13,24,128]{2,1,0:T(8,128)(2,1)S(1)} %get-tuple-element.19), channel_id=1, source_target_pairs={{0,6},{1,7},{2,0},{3,1},{4,2},{5,3},{6,4},{7,5},{8,14},{9,15},{10,... | collective-permute-start | bytes 239624 | tf_op jit(solution)/shard_map/ppermute | solution.py:308
  16.9 6.0 %collective-permute-start.5 = (bf16[13,24,128]{2,1,0:T(8,128)(2,1)S(1)}, bf16[13,24,128]{2,1,0:T(8,128)(2,1)S(1)}, u32[]{:S(2)}, u32[]{:S(2)}) collective-permute-start(bf16[13,24,128]{2,1,0:T(8,128)(2,1)S(1)} %get-tuple-element.16.refs_0_), channel_id=1, source_target_pairs={{0,1},{1,0},{2,3},{3,2},{4,5},{5,4},{6,7},{7,6},{8,9},{9,8},{10,11... | collective-permute-start | bytes 239624 | tf_op jit(solution)/shard_map/ppermute | solution.py:309
  19.6 3.2 %collective-permute-start.6 = (bf16[13,24,128]{2,1,0:T(8,128)(2,1)S(1)}, bf16[13,24,128]{2,1,0:T(8,128)(2,1)S(1)}, u32[]{:S(2)}, u32[]{:S(2)}) collective-permute-start(bf16[13,24,128]{2,1,0:T(8,128)(2,1)S(1)} %collective-permute-done.2.refs_1_), channel_id=1, source_target_pairs={{0,1},{1,0},{2,3},{3,2},{4,5},{5,4},{6,7},{7,6},{8,9},{9,8},{10,11... | collective-permute-start | bytes 239624 | tf_op jit(solution)/shard_map/ppermute | solution.py:309
  19.9 3.0 %collective-permute-start.7 = (bf16[13,24,128]{2,1,0:T(8,128)(2,1)S(1)}, bf16[13,24,128]{2,1,0:T(8,128)(2,1)S(1)}, u32[]{:S(2)}, u32[]{:S(2)}) collective-permute-start(bf16[13,24,128]{2,1,0:T(8,128)(2,1)S(1)} %collective-permute-done.3.refs_2_), channel_id=1, source_target_pairs={{0,1},{1,0},{2,3},{3,2},{4,5},{5,4},{6,7},{7,6},{8,9},{9,8},{10,11... | collective-permute-start | bytes 239624 | tf_op jit(solution)/shard_map/ppermute | solution.py:309
  21.4 2.1 %collective-permute-start.8 = (bf16[13,24,128]{2,1,0:T(8,128)(2,1)S(1)}, bf16[13,24,128]{2,1,0:T(8,128)(2,1)S(1)}, u32[]{:S(2)}, u32[]{:S(2)}) collective-permute-start(bf16[13,24,128]{2,1,0:T(8,128)(2,1)S(1)} %collective-permute-done.4.refs_3_), channel_id=1, source_target_pairs={{0,1},{1,0},{2,3},{3,2},{4,5},{5,4},{6,7},{7,6},{8,9},{9,8},{10,11... | collective-permute-start | bytes 239624 | tf_op jit(solution)/shard_map/ppermute | solution.py:309
  27.3 14.1 %all-to-all-start = ((f32[16,8,128]{2,1,0:T(8,128)}), f32[16,8,128]{2,1,0:T(8,128)S(1)}, u32[]{:S(2)}, u32[]{:S(2)}) async-start(f32[16,8,128]{2,1,0:T(8,128)} %shard_map.87), calls=%async_computation | async-start | bytes 131072 | tf_op jit(solution)/shard_map/all_to_all | solution.py:328

commit v3 on v2

--- a/solution.py
+++ b/solution.py
@@ -54,14 +54,24 @@
 def pack_kernel(left_ref, right_ref, gt_ref, valid_ref, prev_ref, next_ref, *refs):
     outs, ext = refs[:CHIPS], refs[CHIPS]
     chip, _ = position()
+    band = lax.axis_index("ha")
+    has_prev = band > 0
+    has_next = band < lax.axis_size("ha") - 1
+
+    def of_prev(i):
+        return jnp.where(has_prev, prev_ref[i], jnp.zeros((TILE, CH), BF16))
+
+    def of_next(i):
+        return jnp.where(has_next, next_ref[i], jnp.zeros((TILE, CH), BF16))
+
     gt = gt_ref[...].astype(F32)
     valid = valid_ref[...].astype(F32)
     meta = meta_block(gt, valid, 0, ROWS, 2)
-    meta = (meta + prev_ref[4].astype(F32) + next_ref[4].astype(F32)).astype(BF16)
+    meta = (meta + of_prev(4).astype(F32) + of_next(4).astype(F32)).astype(BF16)
     for side, ref in ((0, left_ref), (1, right_ref)):
         for i in range(2):
-            ext[12 * side + i] = prev_ref[2 * side + i]
-            ext[12 * side + ROWS + 2 + i] = next_ref[2 * side + i]
+            ext[12 * side + i] = of_prev(2 * side + i)
+            ext[12 * side + ROWS + 2 + i] = of_next(2 * side + i)
         for i in range(ROWS):
             ext[12 * side + 2 + i] = ref[i]
     for hop in range(CHIPS):
@@ -98,7 +108,7 @@
             ls[rho, pl.ds(at, TILE)] = ref[core + rho].astype(F32)
             rs[rho, pl.ds(at, TILE)] = ref[6 + core + rho].astype(F32)
         for si in range(5):
-            rb[rho, :, si * CH : (si + 1) * CH] = rs[rho, 4 + si : 4 + si + JP].astype(BF16)
+            rb[:, pl.ds(pl.multiple_of((5 * rho + si) * CH, CH), CH)] = rs[rho, 4 + si : 4 + si + JP].astype(BF16)
 
     return tiles
 
@@ -108,36 +118,25 @@
         ms[pl.ds(at - 8, TILE)] = ref[12].astype(F32)
 
 
-def row_gradient(q, wc_ref, ls, rs, rb, ab, ms):
-    lane = lax.broadcasted_iota(jnp.int32, (WT, CH), 1)
-    ww = lax.broadcasted_iota(jnp.int32, (WT, JP), 0)
-    jj = lax.broadcasted_iota(jnp.int32, (WT, JP), 1)
-    level = (ww - jj + 2).astype(F32)
-    inside = (jj <= ww + 2) & (jj >= ww - (WT - 3))
-    on_diag = jj == ww + 2
-    wcol = lax.broadcasted_iota(jnp.int32, (WT, 1), 0).astype(F32)
-    zeros_count = jnp.maximum(float(WT - 3) - wcol, 0.0)
-    zeros_mean = (wcol + float(WT + 2)) * 0.5
-    acc = None
-    diag = jnp.zeros((WT, CH), F32)
-    for a in range(3):
-        rho = q + a
-        shifted = [ls[rho, 7 + b : 7 + b + WT] for b in range(3)]
-        for si in range(5):
-            value = None
-            for b in range(3):
-                e = b - (si - 2)
-                if 0 <= e <= 2:
-                    term = wc_ref[a, 3 * b + e : 3 * b + e + 1] * shifted[b]
-                    value = term if value is None else value + term
-            for i, part in enumerate(split3(value)):
-                ab[i * WT : (i + 1) * WT, (a * 5 + si) * CH : (a * 5 + si + 1) * CH] = part
+def split2(value):
+    high = value.astype(BF16)
+    return high, (value - high.astype(F32)).astype(BF16)
+
+
+def weighted(a, left, wc_ref, ab):
+    for si in range(5):
+        value = None
         for b in range(3):
-            diag = diag + wc_ref[a, 3 * b : 3 * b + 1] * shifted[b] * rs[rho, 8 + b : 8 + b + WT]
-        part = dot(ab[:, a * 5 * CH : (a + 1) * 5 * CH], rb[rho], NT)
-        acc = part if acc is None else acc + part
-    diag_col = jnp.sum(diag, axis=1, keepdims=True)
-    logits = acc[0:WT] + acc[WT : 2 * WT] + acc[2 * WT : 3 * WT]
+            e = b - (si - 2)
+            if 0 <= e <= 2:
+                term = wc_ref[a, 3 * b + e : 3 * b + e + 1] * left[b]
+                value = term if value is None else value + term
+        for i, part in enumerate(split3(value)):
+            ab[i * WT : (i + 1) * WT, (5 * a + si) * CH : (5 * a + si + 1) * CH] = part
+
+
+def row_gradient(q, logits, diag_col, ms, masks):
+    lane, level, inside, on_diag, wcol, zeros_count, zeros_mean = masks
     logits = logits - jnp.where(on_diag, diag_col, 0.0)
     top = jnp.max(jnp.where(inside, logits, -3e38), axis=1, keepdims=True)
     top = jnp.where(zeros_count > 0.0, jnp.maximum(top, 0.0), top)
@@ -154,28 +153,55 @@
     usable = jnp.where(target <= wcol, valid, 0.0)
     resid = estimate - target
     factor = jnp.clip(resid, -1.0, 1.0) * usable * inv
-    up = expd * (level - estimate) * factor
-    up_diag = jnp.sum(jnp.where(on_diag, up, 0.0), axis=1, keepdims=True)
-    return up, up_diag, resid, usable
-
-
-def split2(value):
-    high = value.astype(BF16)
-    return high, (value - high.astype(F32)).astype(BF16)
-
-
-def sums_kernel(*refs):
-    recv, (wc_ref, out_ref, ls, rs, rb, ab, ms, ub, ks) = refs[:8], refs[8:]
+    return expd * (level - estimate) * factor, resid, usable
+
+
+def diagonal(up, on_diag):
+    return jnp.sum(jnp.where(on_diag, up, 0.0), axis=1, keepdims=True)
+
+
+def row_masks():
+    lane = lax.broadcasted_iota(jnp.int32, (WT, CH), 1)
+    ww = lax.broadcasted_iota(jnp.int32, (WT, JP), 0)
+    jj = lax.broadcasted_iota(jnp.int32, (WT, JP), 1)
+    level = (ww - jj + 2).astype(F32)
+    inside = (jj <= ww + 2) & (jj >= ww - (WT - 3))
+    on_diag = jj == ww + 2
+    wcol = lax.broadcasted_iota(jnp.int32, (WT, 1), 0).astype(F32)
+    zeros_count = jnp.maximum(float(WT - 3) - wcol, 0.0)
+    zeros_mean = (wcol + float(WT + 2)) * 0.5
+    return lane, level, inside, on_diag, wcol, zeros_count, zeros_mean
+
+
+def forward(q, ls, rs, rb, wc_ref, ab, ms):
+    masks = row_masks()
+    diag = None
+    for a in range(3):
+        left = [ls[q + a, 7 + b : 7 + b + WT] for b in range(3)]
+        weighted(a, left, wc_ref, ab)
+        for b in range(3):
+            term = wc_ref[a, 3 * b : 3 * b + 1] * left[b] * rs[q + a, 8 + b : 8 + b + WT]
+            diag = term if diag is None else diag + term
+    parts = dot(ab[...], rb[:, 5 * q * CH : (5 * q + 15) * CH], NT)
+    logits = parts[0:WT] + parts[WT : 2 * WT] + parts[2 * WT : 3 * WT]
+    up, resid, usable = row_gradient(q, logits, jnp.sum(diag, axis=1, keepdims=True), ms, masks)
+    return up, diagonal(up, masks[3]), resid, usable
+
+
+def own_kernel(*refs):
+    recv, wc_ref = refs[:8], refs[8]
+    sums_ref, ub, diag_ref, ls, rs, rb, ms, ab, ks = refs[9:]
     fill_meta(fill(recv, 1, 3, ls, rs, rb), ms)
     ks[...] = jnp.zeros(ks.shape, F32)
-    up, up_diag, resid, usable = row_gradient(1, wc_ref, ls, rs, rb, ab, ms)
+    up, up_diag, resid, usable = forward(1, ls, rs, rb, wc_ref, ab, ms)
+    ub[0:WT], ub[WT : 2 * WT] = split2(up)
+    diag_ref[...] = jnp.broadcast_to(up_diag, (WT, CH))
     size = jnp.abs(resid)
     smooth = jnp.where(size < 1.0, 0.5 * resid * resid, size - 0.5)
     loss_sum = jnp.sum(usable * smooth, axis=0, keepdims=True)
     count_sum = jnp.sum(usable, axis=0, keepdims=True)
-    ub[0:WT], ub[WT : 2 * WT] = split2(up)
     for a in range(3):
-        terms = dot(ub[...], rb[1 + a])
+        terms = dot(ub[...], rb[:, 5 * (1 + a) * CH : 5 * (2 + a) * CH])
         terms = terms[0:WT] + terms[WT : 2 * WT]
         for b in range(3):
             left = ls[1 + a, 7 + b : 7 + b + WT]
@@ -186,60 +212,66 @@
                     value = value - up_diag * rs[1 + a, 8 + b : 8 + b + WT]
                 at = 16 * a + 3 * b + e
                 ks[at : at + 1] = jnp.sum(left * value, axis=0, keepdims=True)
+    channel = lax.broadcasted_iota(jnp.int32, (8, CH), 1)
     group = lax.broadcasted_iota(jnp.int32, (8, CH), 0)
-    channel = lax.broadcasted_iota(jnp.int32, (8, CH), 1)
-    member = (channel // 16 == group).astype(F32)
+    member = (lax.shift_right_logical(channel, 4) == group).astype(F32)
     sums = dot(member, ks[...], NT, precision=lax.Precision.HIGHEST) * (1.0 / 16.0)
     sums = jnp.where(channel == LOSS_LANE, loss_sum, sums)
     sums = jnp.where(channel == COUNT_LANE, count_sum, sums)
-    for i in range(out_ref.shape[0]):
-        out_ref[i] = sums
-
-
-def grads_kernel(*refs):
-    recv, (wc_ref, out_ref, ls, rs, rb, ab, ms, ub, utb, lb, xs, ys, zs) = refs[:8], refs[8:]
+    for i in range(sums_ref.shape[0]):
+        sums_ref[i] = sums
+
+
+def rest_kernel(*refs):
+    recv, (wc_ref, own_ub, own_diag, out_ref) = refs[:8], refs[8:12]
+    ls, rs, rb, ms, ab, ub, diags, lb, xs, ys = refs[12:]
     fill_meta(fill(recv, 0, 5, ls, rs, rb), ms)
     xs[...] = jnp.zeros(xs.shape, F32)
-    ys[...] = jnp.zeros(ys.shape, F32)
-    zs[...] = jnp.zeros(zs.shape, F32)
-    lb[WT:] = jnp.zeros((JP - WT, 3 * CH), BF16)
+    for q in (0, 2):
+        up, up_diag, _, _ = forward(q, ls, rs, rb, wc_ref, ab, ms)
+        ub[2 * WT * q : 2 * WT * q + WT], ub[2 * WT * q + WT : 2 * WT * (q + 1)] = split2(up)
+        diags[q] = jnp.broadcast_to(up_diag, (WT, CH))
+    ub[2 * WT : 4 * WT] = own_ub[...]
+    diags[1] = own_diag[...]
     for b in range(3):
-        lb[0:WT, b * CH : (b + 1) * CH] = ls[2, 7 + b : 7 + b + WT].astype(BF16)
-
-    @pl.loop(0, 3)
-    def step(q):
-        up, up_diag, _, _ = row_gradient(q, wc_ref, ls, rs, rb, ab, ms)
-        ub[0:WT], ub[WT : 2 * WT] = split2(up)
-        flipped = jnp.concatenate([up, jnp.zeros((JP - WT, JP), F32)], axis=0).T
-        utb[0:JP], utb[JP : 2 * JP] = split2(flipped)
-        left_terms = dot(ub[...], rb[2])
-        left_terms = left_terms[0:WT] + left_terms[WT : 2 * WT]
-        right_terms = dot(utb[...], lb[...])
-        right_terms = right_terms[0:JP] + right_terms[JP : 2 * JP]
-        a = 2 - q
-        taps = [[wc_ref[a, 3 * b + e : 3 * b + e + 1] for e in range(3)] for b in range(3)]
-        for b in range(3):
-            total = -taps[b][0] * up_diag * rs[2, 8 + b : 8 + b + WT]
+        shifted = ls[2, 7 + b : 7 + b + WT].astype(BF16)
+        lb[0:WT, b * CH : (b + 1) * CH] = shifted
+        lb[WT:, b * CH : (b + 1) * CH] = shifted
+
+    def tap(q, b, e):
+        return wc_ref[2 - q, 3 * b + e : 3 * b + e + 1]
+
+    terms = dot(ub[...], rb[:, 10 * CH : 15 * CH])
+    for b in range(3):
+        total = None
+        spread = None
+        for q in range(3):
+            term = tap(q, b, 0) * diags[q]
+            spread = term if spread is None else spread + term
             for e in range(3):
-                si = b - e + 2
-                total = total + taps[b][e] * left_terms[:, si * CH : (si + 1) * CH]
-            xs[b, 8 : 8 + WT] += total
-            zs[b, 8 : 8 + WT] += taps[b][0] * up_diag * ls[2, 7 + b : 7 + b + WT]
+                at, si = 2 * WT * q, b - e + 2
+                value = terms[at : at + WT, si * CH : (si + 1) * CH]
+                value = value + terms[at + WT : at + 2 * WT, si * CH : (si + 1) * CH]
+                term = tap(q, b, e) * value
+                total = term if total is None else total + term
+        xs[b, 8 : 8 + WT] = total - spread * rs[2, 8 + b : 8 + b + WT]
+        xs[3 + b, 8 : 8 + WT] = spread * ls[2, 7 + b : 7 + b + WT]
+    for q in range(3):
+        terms = dot(ub[2 * WT * q : 2 * WT * (q + 1)], lb[...], TN)
         for si in range(5):
             total = None
             for b in range(3):
                 e = b - (si - 2)
                 if 0 <= e <= 2:
-                    term = taps[b][e] * right_terms[:, b * CH : (b + 1) * CH]
+                    term = tap(q, b, e) * terms[:, b * CH : (b + 1) * CH]
                     total = term if total is None else total + term
-            ys[si] += total
-
+            ys[si] = total if q == 0 else ys[si] + total
     grad_left = xs[0, 9 : 9 + WT] + xs[1, 8 : 8 + WT] + xs[2, 7 : 7 + WT]
     grad_right = ys[0, 4 : 4 + WT]
     for si in range(1, 5):
         grad_right = grad_right + ys[si, 4 - si : 4 - si + WT]
     for b in range(3):
-        grad_right = grad_right - zs[b, 8 - b : 8 - b + WT]
+        grad_right = grad_right - xs[3 + b, 8 - b : 8 - b + WT]
     for dst in range(WA):
         out_ref[dst, 0] = grad_left[TILE * dst : TILE * (dst + 1)].astype(BF16)
         out_ref[dst, 1] = grad_right[TILE * dst : TILE * (dst + 1)].astype(BF16)
@@ -249,12 +281,11 @@
     total = sums_ref[0]
     for i in range(1, sums_ref.shape[0]):
         total = total + sums_ref[i]
-    parts = [part.astype(F32) for part in split3(total)]
-    packed = jnp.concatenate(parts, axis=0).astype(BF16)
+    parts = jnp.concatenate([part.astype(F32) for part in split3(total)], axis=0).astype(BF16)
     for dst in range(WA):
         out_ref[dst, 0] = grads_ref[dst, 0]
         out_ref[dst, 1] = grads_ref[dst, 1]
-        out_ref[dst, 2] = packed
+        out_ref[dst, 2] = parts
 
 
 def finish_kernel(recv_ref, left_ref, right_ref, weight_ref, loss_ref):
@@ -287,8 +318,8 @@
     ha_count = lax.axis_size("ha")
     halo = jax.ShapeDtypeStruct((5, TILE, CH), BF16)
     up, down = call(halo_kernel, (halo, halo), left, right, gt, valid, params=FIRST)
-    before = lax.ppermute(up, "ha", [(i, i + 1) for i in range(ha_count - 1)])
-    after = lax.ppermute(down, "ha", [(i + 1, i) for i in range(ha_count - 1)])
+    before = lax.ppermute(up, "ha", [(i, (i + 1) % ha_count) for i in range(ha_count)])
+    after = lax.ppermute(down, "ha", [((i + 1) % ha_count, i) for i in range(ha_count)])
     taps = jnp.repeat(conv_weight.reshape(8, 27).T, 16, axis=1) * (1.0 / 16.0)
     taps = jnp.pad(taps.reshape(3, 9, CH), ((0, 0), (0, 7), (0, 0)))
     block = jax.ShapeDtypeStruct((13, TILE, CH), BF16)
@@ -308,38 +339,43 @@
         same_core.append(lax.ppermute(blocks[hop], "wa", [(i, (i + 2 * hop) % WA) for i in range(WA)]))
     other_core = [lax.ppermute(value, "wa", [(i, i ^ 1) for i in range(WA)]) for value in same_core]
     tiles = same_core + other_core
-    shared = (
+    others = lax.axis_size("dp") * ha_count
+    rows = (
         pltpu.VMEM((5, WT + 16, CH), F32),
         pltpu.VMEM((5, WT + 80, CH), F32),
-        pltpu.VMEM((5, JP, 5 * CH), BF16),
+        pltpu.VMEM((JP, 25 * CH), BF16),
+        pltpu.VMEM((WT, CH), F32),
         pltpu.VMEM((3 * WT, 15 * CH), BF16),
-        pltpu.VMEM((WT, CH), F32),
-        pltpu.VMEM((2 * WT, JP), BF16),
-    )
-    others = lax.axis_size("dp") * ha_count
-    sums = call(
-        sums_kernel,
-        jax.ShapeDtypeStruct((others, 8, CH), F32),
+    )
+    sums, own_ub, own_diag = call(
+        own_kernel,
+        (
+            jax.ShapeDtypeStruct((others, 8, CH), F32),
+            jax.ShapeDtypeStruct((2 * WT, JP), BF16),
+            jax.ShapeDtypeStruct((WT, CH), F32),
+        ),
         *tiles,
         taps,
-        scratch=shared + (pltpu.VMEM((CH, CH), F32),),
-        flops=1 << 30,
+        scratch=rows + (pltpu.VMEM((CH, CH), F32),),
+        flops=2 << 30,
     )
     sums = lax.all_to_all(sums, ("dp", "ha"), 0, 0, tiled=True)
     grads = call(
-        grads_kernel,
+        rest_kernel,
         jax.ShapeDtypeStruct((WA, 2, TILE, CH), BF16),
         *tiles,
         taps,
-        scratch=shared
+        own_ub,
+        own_diag,
+        scratch=rows
         + (
-            pltpu.VMEM((2 * JP, JP), BF16),
-            pltpu.VMEM((JP, 3 * CH), BF16),
-            pltpu.VMEM((3, WT + 16, CH), F32),
+            pltpu.VMEM((6 * WT, JP), BF16),
+            pltpu.VMEM((3, WT, CH), F32),
+            pltpu.VMEM((2 * WT, 3 * CH), BF16),
+            pltpu.VMEM((6, WT + 16, CH), F32),
             pltpu.VMEM((5, JP, CH), F32),
-            pltpu.VMEM((3, WT + 16, CH), F32),
         ),
-        flops=5 << 30,
+        flops=3 << 30,
     )
     payload = call(payload_kernel, jax.ShapeDtypeStruct((WA, 3, TILE, CH), BF16), grads, sums)
     back = lax.all_to_all(payload, "wa", 0, 0, tiled=True)

time: 53.3 us -> 49.4 us (0.927)
  Pallas kernels: 13.3 us -> 10.3 us
  starting transfers between devices: 23.6 us -> 22 us
    pallas_call x6, Pallas kernels: 13.3 us -> 10.3 us  [call(): pl.pallas_call(kernel, out_shape=out_shape, scratch_shapes=list(scratch),...]
    all_to_all x1, waiting for transfers between devices: 0.01 us -> 2.69 us  [shards(): sums = lax.all_to_all(sums, ('dp', 'ha'), 0, 0, tiled=True)]
    ppermute x2, waiting for transfers between devices: 3.73 us -> 1.49 us  [the longest x1 1.49 us: shards(): lax.ppermute(up, 'ha', [(i, (i + 1) % ha_count) for i in range(ha_count)])]
    ppermute x2, starting transfers between devices: 5.65 us -> 4.59 us  [the longest x1 2.47 us: shards(): lax.ppermute(up, 'ha', [(i, (i + 1) % ha_count) for i in range(ha_count)])]
  transfers between devices with their start and end apart: 10 -> 10, of which waited for: 2 -> 3; matrix products, arithmetic and copies ran while one was open for 0% -> 0% of each run, Pallas kernels for 13% -> 8%
where the time goes in v3:
time: 49.4 us; the launch traced here: 49.1 us
  starting transfers between devices  22 us (45%)
  blocking collectives  10.9 us (22%)
  Pallas kernels  10.3 us (21%)
  waiting for transfers between devices  4.84 us (10%)
  between operations  0.78 us (2%)
    all_to_all x1, blocking collectives, shards(): back = lax.all_to_all(payload, 'wa', 0, 0, tiled=True)  10.9 us
    pallas_call x6, Pallas kernels, call(): pl.pallas_call(kernel, out_shape=out_shape, scratch_shapes=list(scratch),...  10.3 us
    all_to_all x1, starting transfers between devices, shards(): sums = lax.all_to_all(sums, ('dp', 'ha'), 0, 0, tiled=True)  7.21 us
    ppermute x4, starting transfers between devices, shards(): lax.ppermute(value, 'wa', [(i, i ^ 1) for i in range(WA)])  5.36 us
    ppermute x3, starting transfers between devices, shards(): lax.ppermute(blocks[hop], 'wa', [(i, (i + 2 * hop) % WA) for i in range(W...  4.88 us
    all_to_all x1, waiting for transfers between devices, shards(): sums = lax.all_to_all(sums, ('dp', 'ha'), 0, 0, tiled=True)  2.69 us
    ppermute x1, starting transfers between devices, shards(): lax.ppermute(up, 'ha', [(i, (i + 1) % ha_count) for i in range(ha_count)])  2.47 us
    ppermute x1, starting transfers between devices, shards(): lax.ppermute(down, 'ha', [((i + 1) % ha_count, i) for i in range(ha_count)])  2.12 us
  transfers between devices with their start and end apart: 10, of which 3 were waited for; matrix products, arithmetic and copies ran while one was open for 0% of the time, Pallas kernels for 8%

profile of v3, /device:TPU:1, one launch (start us, length us, event | category | flops | bytes accessed | tf_op | source)
XLA Modules:
  0.0 49.1 jit_solution(18230705001395863946)
XLA Ops:
  0.7 1.7 %shard_map.84 = (bf16[5,24,128]{2,1,0:T(8,128)(2,1)}, bf16[5,24,128]{2,1,0:T(8,128)(2,1)}) custom-call(bf16[8,24,128]{2,1,0:T(8,128)(2,1)} %bitcast.11, bf16[8,24,128]{2,1,0:T(8,128)(2,1)} %bitcast.13, s32[8,24]{1,0:T(8,128)} %bitcast.15, s32[8,24]{1,0:T(8,128)} %bitcast.17), custom_call_target="tpu_custom_call" | custom-call | bytes 1048576 | tf_op jit(solution)/shard_map/pallas_call | solution.py:310
  2.4 2.5 %collective-permute-start = (bf16[5,24,128]{2,1,0:T(8,128)(2,1)}, bf16[5,24,128]{2,1,0:T(8,128)(2,1)S(1)}, u32[]{:S(2)}, u32[]{:S(2)}) collective-permute-start(bf16[5,24,128]{2,1,0:T(8,128)(2,1)} %get-tuple-element.17), channel_id=1, source_target_pairs={{0,8},{8,16},{16,24},{24,0},{1,9},{9,17},{17,25},{25,1},{2,10},{10... | collective-permute-start | bytes 92168 | tf_op jit(solution)/shard_map/ppermute | solution.py:321
  4.8 2.1 %collective-permute-start.1 = (bf16[5,24,128]{2,1,0:T(8,128)(2,1)}, bf16[5,24,128]{2,1,0:T(8,128)(2,1)S(1)}, u32[]{:S(2)}, u32[]{:S(2)}) collective-permute-start(bf16[5,24,128]{2,1,0:T(8,128)(2,1)} %get-tuple-element.18), channel_id=1, source_target_pairs={{8,0},{16,8},{24,16},{0,24},{9,1},{17,9},{25,17},{1,25},{10,2},{18... | collective-permute-start | bytes 92168 | tf_op jit(solution)/shard_map/ppermute | solution.py:322
  6.9 1.5 %collective-permute-done.prev_ref = bf16[5,24,128]{2,1,0:T(8,128)(2,1)S(1)} collective-permute-done((bf16[5,24,128]{2,1,0:T(8,128)(2,1)}, bf16[5,24,128]{2,1,0:T(8,128)(2,1)S(1)}, u32[]{:S(2)}, u32[]{:S(2)}) %collective-permute-start) | collective-permute-done | bytes 30752 | tf_op jit(solution)/shard_map/ppermute | solution.py:321
  8.4 0.0 collective-permute-done.1.next_ref
  8.5 0.0 copy-start.4
  8.5 0.2 shard_map.85
  8.7 1.3 %collective-permute-start.2 = (bf16[13,24,128]{2,1,0:T(8,128)(2,1)S(1)}, bf16[13,24,128]{2,1,0:T(8,128)(2,1)S(1)}, u32[]{:S(2)}, u32[]{:S(2)}) collective-permute-start(bf16[13,24,128]{2,1,0:T(8,128)(2,1)S(1)} %get-tuple-element.20), channel_id=1, source_target_pairs={{0,2},{1,3},{2,4},{3,5},{4,6},{5,7},{6,0},{7,1},{8,10},{9,11},{10,... | collective-permute-start | bytes 239624 | tf_op jit(solution)/shard_map/ppermute | solution.py:339
  10.0 2.5 %collective-permute-start.3 = (bf16[13,24,128]{2,1,0:T(8,128)(2,1)S(1)}, bf16[13,24,128]{2,1,0:T(8,128)(2,1)S(1)}, u32[]{:S(2)}, u32[]{:S(2)}) collective-permute-start(bf16[13,24,128]{2,1,0:T(8,128)(2,1)S(1)} %get-tuple-element.21), channel_id=1, source_target_pairs={{0,4},{1,5},{2,6},{3,7},{4,0},{5,1},{6,2},{7,3},{8,12},{9,13},{10,... | collective-permute-start | bytes 239624 | tf_op jit(solution)/shard_map/ppermute | solution.py:339
  12.4 1.2 %collective-permute-start.4 = (bf16[13,24,128]{2,1,0:T(8,128)(2,1)S(1)}, bf16[13,24,128]{2,1,0:T(8,128)(2,1)S(1)}, u32[]{:S(2)}, u32[]{:S(2)}) collective-permute-start(bf16[13,24,128]{2,1,0:T(8,128)(2,1)S(1)} %get-tuple-element.22), channel_id=1, source_target_pairs={{0,6},{1,7},{2,0},{3,1},{4,2},{5,3},{6,4},{7,5},{8,14},{9,15},{10,... | collective-permute-start | bytes 239624 | tf_op jit(solution)/shard_map/ppermute | solution.py:339
  13.6 2.4 %collective-permute-start.5 = (bf16[13,24,128]{2,1,0:T(8,128)(2,1)S(1)}, bf16[13,24,128]{2,1,0:T(8,128)(2,1)S(1)}, u32[]{:S(2)}, u32[]{:S(2)}) collective-permute-start(bf16[13,24,128]{2,1,0:T(8,128)(2,1)S(1)} %get-tuple-element.19.refs_0_), channel_id=1, source_target_pairs={{0,1},{1,0},{2,3},{3,2},{4,5},{5,4},{6,7},{7,6},{8,9},{9,8},{10,11... | collective-permute-start | bytes 239624 | tf_op jit(solution)/shard_map/ppermute | solution.py:340
  15.9 0.0 collective-permute-done.2.refs_1_
  15.9 0.7 %collective-permute-start.6 = (bf16[13,24,128]{2,1,0:T(8,128)(2,1)S(1)}, bf16[13,24,128]{2,1,0:T(8,128)(2,1)S(1)}, u32[]{:S(2)}, u32[]{:S(2)}) collective-permute-start(bf16[13,24,128]{2,1,0:T(8,128)(2,1)S(1)} %collective-permute-done.2.refs_1_), channel_id=1, source_target_pairs={{0,1},{1,0},{2,3},{3,2},{4,5},{5,4},{6,7},{7,6},{8,9},{9,8},{10,11... | collective-permute-start | bytes 239624 | tf_op jit(solution)/shard_map/ppermute | solution.py:340
  16.6 1.1 %collective-permute-start.7 = (bf16[13,24,128]{2,1,0:T(8,128)(2,1)S(1)}, bf16[13,24,128]{2,1,0:T(8,128)(2,1)S(1)}, u32[]{:S(2)}, u32[]{:S(2)}) collective-permute-start(bf16[13,24,128]{2,1,0:T(8,128)(2,1)S(1)} %collective-permute-done.3.refs_2_), channel_id=1, source_target_pairs={{0,1},{1,0},{2,3},{3,2},{4,5},{5,4},{6,7},{7,6},{8,9},{9,8},{10,11... | collective-permute-start | bytes 239624 | tf_op jit(solution)/shard_map/ppermute | solution.py:340
  17.8 1.2 %collective-permute-start.8 = (bf16[13,24,128]{2,1,0:T(8,128)(2,1)S(1)}, bf16[13,24,128]{2,1,0:T(8,128)(2,1)S(1)}, u32[]{:S(2)}, u32[]{:S(2)}) collective-permute-start(bf16[13,24,128]{2,1,0:T(8,128)(2,1)S(1)} %collective-permute-done.4.refs_3_), channel_id=1, source_target_pairs={{0,1},{1,0},{2,3},{3,2},{4,5},{5,4},{6,7},{7,6},{8,9},{9,8},{10,11... | collective-permute-start | bytes 239624 | tf_op jit(solution)/shard_map/ppermute | solution.py:340
  19.0 0.1 broadcast_in_dim.9
  19.0 0.1 mul.21
  19.2 0.6 %collective-permute-done.8.refs_7_ = bf16[13,24,128]{2,1,0:T(8,128)(2,1)S(1)} collective-permute-done((bf16[13,24,128]{2,1,0:T(8,128)(2,1)S(1)}, bf16[13,24,128]{2,1,0:T(8,128)(2,1)S(1)}, u32[]{:S(2)}, u32[]{:S(2)}) %collective-permute-start.8) | collective-permute-done | bytes 79904 | tf_op jit(solution)/shard_map/ppermute | solution.py:340
  19.8 3.8 %shard_map.86 = (f32[16,8,128]{2,1,0:T(8,128)}, bf16[384,256]{1,0:T(8,128)(2,1)S(1)}, f32[192,128]{1,0:T(8,128)S(1)}) custom-call(bf16[13,24,128]{2,1,0:T(8,128)(2,1)S(1)} %get-tuple-element.19.refs_0_, bf16[13,24,128]{2,1,0:T(8,128)(2,1)S(1)} %collective-permute-done.2.refs_1_, bf16[13,24,128]{2,1,0:T(8,128)(2,1)S(1)} %collective-permute-done.3.refs_2_, ...), custom_call_target="tpu_custom_call" | custom-call | flops 2147483648 | bytes 1048576 | tf_op jit(solution)/shard_map/pallas_call | solution.py:310
  23.6 7.2 %all-to-all-start = ((f32[16,8,128]{2,1,0:T(8,128)}), f32[16,8,128]{2,1,0:T(8,128)S(1)}, u32[]{:S(2)}, u32[]{:S(2)}) async-start(f32[16,8,128]{2,1,0:T(8,128)} %get-tuple-element.25), calls=%async_computation | async-start | bytes 131072 | tf_op jit(solution)/shard_map/all_to_all | solution.py:362
  30.8 3.8 %shard_map.87.grads_ref = bf16[8,2,24,128]{3,2,1,0:T(8,128)(2,1)S(1)} custom-call(bf16[13,24,128]{2,1,0:T(8,128)(2,1)S(1)} %get-tuple-element.19.refs_0_, bf16[13,24,128]{2,1,0:T(8,128)(2,1)S(1)} %collective-permute-done.2.refs_1_, bf16[13,24,128]{2,1,0:T(8,128)(2,1)S(1)} %collective-permute-done.3.refs_2_, ...), custom_call_target="tpu_custom_call" | custom-call | flops 3221225472 | bytes 1048576 | tf_op jit(solution)/shard_map/pallas_call | solution.py:310
  34.7 2.7 %all-to-all-done.sums_ref = f32[16,8,128]{2,1,0:T(8,128)S(1)} async-done(((f32[16,8,128]{2,1,0:T(8,128)}), f32[16,8,128]{2,1,0:T(8,128)S(1)}, u32[]{:S(2)}, u32[]{:S(2)}) %all-to-all-start) | async-done | bytes 65568 | tf_op jit(solution)/shard_map/all_to_all | solution.py:362
  37.4 10.9 %all_to_all.10.recv_ref = bf16[8,3,24,128]{3,2,1,0:T(8,128)(2,1)S(1)} all-to-all(bf16[8,3,24,128]{3,2,1,0:T(8,128)(2,1)S(1)} %shard_map.88), channel_id=1, replica_groups=mesh['dp'=4,'ha'=4,'wa'=8] {'wa'}, dimensions={0} | all-to-all | bytes 294912 | tf_op jit(solution)/shard_map/all_to_all | solution.py:381
  48.3 0.8 %shard_map.89 = (f32[8,24,128]{2,1,0:T(8,128)}, f32[8,24,128]{2,1,0:T(8,128)}, f32[3,3,3,8]{3,2,1,0:T(4,128)}, f32[1,1]{1,0:T(1,128)}) custom-call(bf16[8,3,24,128]{3,2,1,0:T(8,128)(2,1)S(1)} %all_to_all.10.recv_ref), custom_call_target="tpu_custom_call" | custom-call | bytes 1048576 | tf_op jit(solution)/shard_map/pallas_call | solution.py:310
  (18 shorter events, 0.1 us)
Async XLA Ops:
  0.6 7.8 %copy-start = (bf16[1,8,24,128]{3,2,1,0:T(8,128)(2,1)S(1)}, bf16[1,8,24,128]{3,2,1,0:T(8,128)(2,1)}, u32[]{:S(2)}) copy-start(bf16[1,8,24,128]{3,2,1,0:T(8,128)(2,1)} %param.5) | copy-start | bytes 147460
  0.6 7.8 %copy-start.1 = (bf16[1,8,24,128]{3,2,1,0:T(8,128)(2,1)S(1)}, bf16[1,8,24,128]{3,2,1,0:T(8,128)(2,1)}, u32[]{:S(2)}) copy-start(bf16[1,8,24,128]{3,2,1,0:T(8,128)(2,1)} %param.6) | copy-start | bytes 147460
  0.7 7.8 %copy-start.2 = (s32[1,8,24]{2,1,0:T(8,128)S(1)}, s32[1,8,24]{2,1,0:T(8,128)}, u32[]{:S(2)}) copy-start(s32[1,8,24]{2,1,0:T(8,128)} %param.8) | copy-start | bytes 2308
  0.7 7.8 %copy-start.3 = (s32[1,8,24]{2,1,0:T(8,128)S(1)}, s32[1,8,24]{2,1,0:T(8,128)}, u32[]{:S(2)}) copy-start(s32[1,8,24]{2,1,0:T(8,128)} %param.9) | copy-start | bytes 2308
  2.4 6.1 %collective-permute-start = (bf16[5,24,128]{2,1,0:T(8,128)(2,1)}, bf16[5,24,128]{2,1,0:T(8,128)(2,1)S(1)}, u32[]{:S(2)}, u32[]{:S(2)}) collective-permute-start(bf16[5,24,128]{2,1,0:T(8,128)(2,1)} %get-tuple-element.17), channel_id=1, source_target_pairs={{0,8},{8,16},{16,24},{24,0},{1,9},{9,17},{17,25},{25,1},{2,10},{10... | collective-permute-start | bytes 92168 | tf_op jit(solution)/shard_map/ppermute | solution.py:321
  4.8 3.6 %collective-permute-start.1 = (bf16[5,24,128]{2,1,0:T(8,128)(2,1)}, bf16[5,24,128]{2,1,0:T(8,128)(2,1)S(1)}, u32[]{:S(2)}, u32[]{:S(2)}) collective-permute-start(bf16[5,24,128]{2,1,0:T(8,128)(2,1)} %get-tuple-element.18), channel_id=1, source_target_pairs={{8,0},{16,8},{24,16},{0,24},{9,1},{17,9},{25,17},{1,25},{10,2},{18... | collective-permute-start | bytes 92168 | tf_op jit(solution)/shard_map/ppermute | solution.py:322
  8.5 10.5 %copy-start.4 = (f32[8,3,3,3]{0,3,2,1:T(4,128)S(1)}, f32[8,3,3,3]{0,3,2,1:T(4,128)}, u32[]{:S(2)}) copy-start(f32[8,3,3,3]{0,3,2,1:T(4,128)} %param.7) | copy-start | bytes 2596
  8.7 7.3 %collective-permute-start.2 = (bf16[13,24,128]{2,1,0:T(8,128)(2,1)S(1)}, bf16[13,24,128]{2,1,0:T(8,128)(2,1)S(1)}, u32[]{:S(2)}, u32[]{:S(2)}) collective-permute-start(bf16[13,24,128]{2,1,0:T(8,128)(2,1)S(1)} %get-tuple-element.20), channel_id=1, source_target_pairs={{0,2},{1,3},{2,4},{3,5},{4,6},{5,7},{6,0},{7,1},{8,10},{9,11},{10,... | collective-permute-start | bytes 239624 | tf_op jit(solution)/shard_map/ppermute | solution.py:339
  10.0 6.7 %collective-permute-start.3 = (bf16[13,24,128]{2,1,0:T(8,128)(2,1)S(1)}, bf16[13,24,128]{2,1,0:T(8,128)(2,1)S(1)}, u32[]{:S(2)}, u32[]{:S(2)}) collective-permute-start(bf16[13,24,128]{2,1,0:T(8,128)(2,1)S(1)} %get-tuple-element.21), channel_id=1, source_target_pairs={{0,4},{1,5},{2,6},{3,7},{4,0},{5,1},{6,2},{7,3},{8,12},{9,13},{10,... | collective-permute-start | bytes 239624 | tf_op jit(solution)/shard_map/ppermute | solution.py:339
  12.4 5.4 %collective-permute-start.4 = (bf16[13,24,128]{2,1,0:T(8,128)(2,1)S(1)}, bf16[13,24,128]{2,1,0:T(8,128)(2,1)S(1)}, u32[]{:S(2)}, u32[]{:S(2)}) collective-permute-start(bf16[13,24,128]{2,1,0:T(8,128)(2,1)S(1)} %get-tuple-element.22), channel_id=1, source_target_pairs={{0,6},{1,7},{2,0},{3,1},{4,2},{5,3},{6,4},{7,5},{8,14},{9,15},{10,... | collective-permute-start | bytes 239624 | tf_op jit(solution)/shard_map/ppermute | solution.py:339
  13.6 5.6 %collective-permute-start.5 = (bf16[13,24,128]{2,1,0:T(8,128)(2,1)S(1)}, bf16[13,24,128]{2,1,0:T(8,128)(2,1)S(1)}, u32[]{:S(2)}, u32[]{:S(2)}) collective-permute-start(bf16[13,24,128]{2,1,0:T(8,128)(2,1)S(1)} %get-tuple-element.19.refs_0_), channel_id=1, source_target_pairs={{0,1},{1,0},{2,3},{3,2},{4,5},{5,4},{6,7},{7,6},{8,9},{9,8},{10,11... | collective-permute-start | bytes 239624 | tf_op jit(solution)/shard_map/ppermute | solution.py:340
  15.9 3.2 %collective-permute-start.6 = (bf16[13,24,128]{2,1,0:T(8,128)(2,1)S(1)}, bf16[13,24,128]{2,1,0:T(8,128)(2,1)S(1)}, u32[]{:S(2)}, u32[]{:S(2)}) collective-permute-start(bf16[13,24,128]{2,1,0:T(8,128)(2,1)S(1)} %collective-permute-done.2.refs_1_), channel_id=1, source_target_pairs={{0,1},{1,0},{2,3},{3,2},{4,5},{5,4},{6,7},{7,6},{8,9},{9,8},{10,11... | collective-permute-start | bytes 239624 | tf_op jit(solution)/shard_map/ppermute | solution.py:340
  16.6 2.6 %collective-permute-start.7 = (bf16[13,24,128]{2,1,0:T(8,128)(2,1)S(1)}, bf16[13,24,128]{2,1,0:T(8,128)(2,1)S(1)}, u32[]{:S(2)}, u32[]{:S(2)}) collective-permute-start(bf16[13,24,128]{2,1,0:T(8,128)(2,1)S(1)} %collective-permute-done.3.refs_2_), channel_id=1, source_target_pairs={{0,1},{1,0},{2,3},{3,2},{4,5},{5,4},{6,7},{7,6},{8,9},{9,8},{10,11... | collective-permute-start | bytes 239624 | tf_op jit(solution)/shard_map/ppermute | solution.py:340
  17.8 2.1 %collective-permute-start.8 = (bf16[13,24,128]{2,1,0:T(8,128)(2,1)S(1)}, bf16[13,24,128]{2,1,0:T(8,128)(2,1)S(1)}, u32[]{:S(2)}, u32[]{:S(2)}) collective-permute-start(bf16[13,24,128]{2,1,0:T(8,128)(2,1)S(1)} %collective-permute-done.4.refs_3_), channel_id=1, source_target_pairs={{0,1},{1,0},{2,3},{3,2},{4,5},{5,4},{6,7},{7,6},{8,9},{9,8},{10,11... | collective-permute-start | bytes 239624 | tf_op jit(solution)/shard_map/ppermute | solution.py:340
  23.6 13.7 %all-to-all-start = ((f32[16,8,128]{2,1,0:T(8,128)}), f32[16,8,128]{2,1,0:T(8,128)S(1)}, u32[]{:S(2)}, u32[]{:S(2)}) async-start(f32[16,8,128]{2,1,0:T(8,128)} %get-tuple-element.25), calls=%async_computation | async-start | bytes 131072 | tf_op jit(solution)/shard_map/all_to_all | solution.py:362

commit v4 on v3

--- a/solution.py
+++ b/solution.py
@@ -12,9 +12,8 @@
 WT = 192
 JP = 256
 GT_LANE, VALID_LANE = 0, 16
-LOSS_LANE, COUNT_LANE = 9, 10
+LOSS_LANE, COUNT_LANE, THIRD = 27, 28, 32
 VMEM = pltpu.CompilerParams(vmem_limit_bytes=48 * 1024 * 1024)
-FIRST = pltpu.CompilerParams(vmem_limit_bytes=60 * 1024 * 1024)
 NT = (((1,), (1,)), ((), ()))
 NN = (((1,), (0,)), ((), ()))
 TN = (((0,), (0,)), ((), ()))
@@ -34,16 +33,36 @@
     return dot(gt, pick_gt, TN) + dot(valid, pick_valid, TN)
 
 
-def halo_kernel(left_ref, right_ref, gt_ref, valid_ref, up_ref, down_ref):
+def halo_kernel(left_any, right_any, gt_any, valid_any, weight_any, up_ref, down_ref, own_ref, taps_ref, *scratch):
+    refs, sems = scratch[:5], scratch[5]
+    sources = (left_any, right_any, gt_any, valid_any, weight_any)
+    copies = [pltpu.make_async_copy(src, dst, sems.at[i]) for i, (src, dst) in enumerate(zip(sources, refs))]
+    for copy in copies:
+        copy.start()
+    for copy in copies:
+        copy.wait()
+    left_ref, right_ref, gt_ref, valid_ref, weight_ref = refs
     gt = gt_ref[...].astype(F32)
     valid = valid_ref[...].astype(F32)
-    for i in range(2):
-        up_ref[i] = left_ref[ROWS - 2 + i]
-        up_ref[2 + i] = right_ref[ROWS - 2 + i]
-        down_ref[i] = left_ref[i]
-        down_ref[2 + i] = right_ref[i]
+    for side, ref in ((0, left_ref), (1, right_ref)):
+        for i in range(2):
+            up_ref[2 * side + i] = ref[ROWS - 2 + i]
+            down_ref[2 * side + i] = ref[i]
+        for i in range(ROWS):
+            own_ref[ROWS * side + i] = ref[i]
     up_ref[4] = meta_block(gt, valid, ROWS - 2, 2, 0).astype(BF16)
     down_ref[4] = meta_block(gt, valid, 0, 2, ROWS + 2).astype(BF16)
+    own_ref[2 * ROWS] = meta_block(gt, valid, 0, ROWS, 2).astype(BF16)
+    member = group_member() * (1.0 / 16.0)
+    for a in range(3):
+        taps = jnp.concatenate([weight_ref[a, b] for b in range(3)], axis=0)
+        taps_ref[a, 0:9] = dot(taps, member, precision=lax.Precision.HIGHEST)
+
+
+def group_member():
+    group = lax.broadcasted_iota(jnp.int32, (8, CH), 0)
+    channel = lax.broadcasted_iota(jnp.int32, (8, CH), 1)
+    return (lax.shift_right_logical(channel, 4) == group).astype(F32)
 
 
 def position():
@@ -51,7 +70,7 @@
     return lax.shift_right_logical(index, 1), index & 1
 
 
-def pack_kernel(left_ref, right_ref, gt_ref, valid_ref, prev_ref, next_ref, *refs):
+def pack_kernel(own_ref, prev_ref, next_ref, *refs):
     outs, ext = refs[:CHIPS], refs[CHIPS]
     chip, _ = position()
     band = lax.axis_index("ha")
@@ -64,16 +83,14 @@
     def of_next(i):
         return jnp.where(has_next, next_ref[i], jnp.zeros((TILE, CH), BF16))
 
-    gt = gt_ref[...].astype(F32)
-    valid = valid_ref[...].astype(F32)
-    meta = meta_block(gt, valid, 0, ROWS, 2)
+    meta = own_ref[2 * ROWS].astype(F32)
     meta = (meta + of_prev(4).astype(F32) + of_next(4).astype(F32)).astype(BF16)
-    for side, ref in ((0, left_ref), (1, right_ref)):
+    for side in range(2):
         for i in range(2):
             ext[12 * side + i] = of_prev(2 * side + i)
             ext[12 * side + ROWS + 2 + i] = of_next(2 * side + i)
         for i in range(ROWS):
-            ext[12 * side + 2 + i] = ref[i]
+            ext[12 * side + 2 + i] = own_ref[ROWS * side + i]
     for hop in range(CHIPS):
         first = 2 * ((chip + hop) & (CHIPS - 1))
         for i in range(6):
@@ -200,22 +217,21 @@
     smooth = jnp.where(size < 1.0, 0.5 * resid * resid, size - 0.5)
     loss_sum = jnp.sum(usable * smooth, axis=0, keepdims=True)
     count_sum = jnp.sum(usable, axis=0, keepdims=True)
+    terms = dot(ub[...], rb[:, 5 * CH : 20 * CH])
     for a in range(3):
-        terms = dot(ub[...], rb[:, 5 * (1 + a) * CH : 5 * (2 + a) * CH])
-        terms = terms[0:WT] + terms[WT : 2 * WT]
         for b in range(3):
             left = ls[1 + a, 7 + b : 7 + b + WT]
             for e in range(3):
-                si = b - e + 2
-                value = terms[:, si * CH : (si + 1) * CH]
+                si = 5 * a + b - e + 2
+                value = terms[0:WT, si * CH : (si + 1) * CH] + terms[WT:, si * CH : (si + 1) * CH]
                 if e == 0:
                     value = value - up_diag * rs[1 + a, 8 + b : 8 + b + WT]
-                at = 16 * a + 3 * b + e
+                at = 9 * a + 3 * b + e
                 ks[at : at + 1] = jnp.sum(left * value, axis=0, keepdims=True)
     channel = lax.broadcasted_iota(jnp.int32, (8, CH), 1)
-    group = lax.broadcasted_iota(jnp.int32, (8, CH), 0)
-    member = (lax.shift_right_logical(channel, 4) == group).astype(F32)
-    sums = dot(member, ks[...], NT, precision=lax.Precision.HIGHEST) * (1.0 / 16.0)
+    member = group_member().astype(BF16)
+    parts = [dot(member, part, NT) for part in split3(ks[...])]
+    sums = (parts[0] + (parts[1] + parts[2])) * (1.0 / 16.0)
     sums = jnp.where(channel == LOSS_LANE, loss_sum, sums)
     sums = jnp.where(channel == COUNT_LANE, count_sum, sums)
     for i in range(sums_ref.shape[0]):
@@ -281,27 +297,29 @@
     total = sums_ref[0]
     for i in range(1, sums_ref.shape[0]):
         total = total + sums_ref[i]
-    parts = jnp.concatenate([part.astype(F32) for part in split3(total)], axis=0).astype(BF16)
+    lane = lax.broadcasted_iota(jnp.int32, (8, CH), 1)
+    high, middle, low = [jnp.where(lane < THIRD, part.astype(F32), 0.0) for part in split3(total)]
+    sums = high + pltpu.roll(middle, THIRD, 1) + pltpu.roll(low, 2 * THIRD, 1)
     for dst in range(WA):
-        out_ref[dst, 0] = grads_ref[dst, 0]
-        out_ref[dst, 1] = grads_ref[dst, 1]
-        out_ref[dst, 2] = parts
+        left, right = grads_ref[dst, 0].astype(F32), grads_ref[dst, 1].astype(F32)
+        out_ref[dst] = jnp.concatenate([left, right, sums], axis=0).astype(BF16)
 
 
 def finish_kernel(recv_ref, left_ref, right_ref, weight_ref, loss_ref):
-    total = recv_ref[0, 2].astype(F32)
+    total = recv_ref[0].astype(F32)[2 * TILE :]
     for src in range(1, WA):
-        total = total + recv_ref[src, 2].astype(F32)
-    total = total[0:8] + total[8:16] + total[16:24]
+        total = total + recv_ref[src].astype(F32)[2 * TILE :]
+    total = total + pltpu.roll(total, CH - THIRD, 1) + pltpu.roll(total, CH - 2 * THIRD, 1)
     norm = 1.0 / jnp.maximum(total[0:1, COUNT_LANE : COUNT_LANE + 1], 1.0)
     for src in range(WA):
-        left_ref[src] = recv_ref[src, 0].astype(F32) * norm
-        right_ref[src] = recv_ref[src, 1].astype(F32) * norm
+        block = recv_ref[src].astype(F32) * norm
+        left_ref[src] = block[0:TILE]
+        right_ref[src] = block[TILE : 2 * TILE]
     loss_ref[...] = total[0:1, LOSS_LANE : LOSS_LANE + 1] * norm
     by_tap = jnp.concatenate([total * norm, jnp.zeros((CH - 8, CH), F32)], axis=0).T
     for a in range(3):
         for b in range(3):
-            at = 16 * a + 3 * b
+            at = 9 * a + 3 * b
             weight_ref[a, b] = by_tap[at : at + 3, 0:8]
 
 
@@ -317,19 +335,29 @@
     gt, valid = disparity_gt[0], valid_mask[0]
     ha_count = lax.axis_size("ha")
     halo = jax.ShapeDtypeStruct((5, TILE, CH), BF16)
-    up, down = call(halo_kernel, (halo, halo), left, right, gt, valid, params=FIRST)
+    own = jax.ShapeDtypeStruct((2 * ROWS + 1, TILE, CH), BF16)
+    args = (left, right, gt, valid, jnp.transpose(conv_weight, (1, 2, 3, 0)))
+    up, down, own, taps = pl.pallas_call(
+        halo_kernel,
+        out_shape=(halo, halo, own, jax.ShapeDtypeStruct((3, 16, CH), F32)),
+        in_specs=[pl.BlockSpec(memory_space=pltpu.HBM)] * 5,
+        scratch_shapes=[
+            pltpu.VMEM((ROWS, TILE, CH), BF16),
+            pltpu.VMEM((ROWS, TILE, CH), BF16),
+            pltpu.VMEM((ROWS, TILE), jnp.int32),
+            pltpu.VMEM((ROWS, TILE), jnp.int32),
+            pltpu.VMEM((3, 3, 3, 8), F32),
+            pltpu.SemaphoreType.DMA((5,)),
+        ],
+        compiler_params=VMEM,
+    )(*[pltpu.with_memory_space_constraint(arg, pltpu.HBM) for arg in args])
     before = lax.ppermute(up, "ha", [(i, (i + 1) % ha_count) for i in range(ha_count)])
     after = lax.ppermute(down, "ha", [((i + 1) % ha_count, i) for i in range(ha_count)])
-    taps = jnp.repeat(conv_weight.reshape(8, 27).T, 16, axis=1) * (1.0 / 16.0)
-    taps = jnp.pad(taps.reshape(3, 9, CH), ((0, 0), (0, 7), (0, 0)))
     block = jax.ShapeDtypeStruct((13, TILE, CH), BF16)
     blocks = call(
         pack_kernel,
         (block,) * CHIPS,
-        left,
-        right,
-        gt,
-        valid,
+        own,
         before,
         after,
         scratch=(pltpu.VMEM((24, TILE, CH), BF16),),
@@ -377,7 +405,7 @@
         ),
         flops=3 << 30,
     )
-    payload = call(payload_kernel, jax.ShapeDtypeStruct((WA, 3, TILE, CH), BF16), grads, sums)
+    payload = call(payload_kernel, jax.ShapeDtypeStruct((WA, 2 * TILE + 8, CH), BF16), grads, sums)
     back = lax.all_to_all(payload, "wa", 0, 0, tiled=True)
     tile = jax.ShapeDtypeStruct((ROWS, TILE, CH), F32)
     grad_left, grad_right, weight, loss = call(

time: 49.4 us -> 48.1 us (0.974)
  Pallas kernels: 10.3 us -> 9.48 us
    pallas_call x6 -> x5, Pallas kernels: 10.3 us -> 8.34 us  [call(): pl.pallas_call(kernel, out_shape=out_shape, scratch_shapes=list(scratch),...]
    pallas_call x0 -> x1, Pallas kernels: none -> 1.15 us  [shards(): pl.pallas_call(halo_kernel, out_shape=(halo, halo, own, jax.ShapeDtypeStr...]
where the time goes in v4:
time: 48.1 us; the launch traced here: 47.8 us
  starting transfers between devices  22.2 us (46%)
  blocking collectives  10.6 us (22%)
  Pallas kernels  9.48 us (20%)
  waiting for transfers between devices  4.82 us (10%)
  between operations  0.67 us (1%)
    all_to_all x1, blocking collectives, shards(): back = lax.all_to_all(payload, 'wa', 0, 0, tiled=True)  10.6 us
    pallas_call x5, Pallas kernels, call(): pl.pallas_call(kernel, out_shape=out_shape, scratch_shapes=list(scratch),...  8.34 us
    all_to_all x1, starting transfers between devices, shards(): sums = lax.all_to_all(sums, ('dp', 'ha'), 0, 0, tiled=True)  7.21 us
    ppermute x4, starting transfers between devices, shards(): lax.ppermute(value, 'wa', [(i, i ^ 1) for i in range(WA)])  5.36 us
    ppermute x3, starting transfers between devices, shards(): lax.ppermute(blocks[hop], 'wa', [(i, (i + 2 * hop) % WA) for i in range(W...  4.88 us
    all_to_all x1, waiting for transfers between devices, shards(): sums = lax.all_to_all(sums, ('dp', 'ha'), 0, 0, tiled=True)  2.7 us
    ppermute x1, starting transfers between devices, shards(): lax.ppermute(up, 'ha', [(i, (i + 1) % ha_count) for i in range(ha_count)])  2.54 us
    ppermute x1, starting transfers between devices, shards(): lax.ppermute(down, 'ha', [((i + 1) % ha_count, i) for i in range(ha_count)])  2.2 us
  transfers between devices with their start and end apart: 10, of which 3 were waited for; matrix products, arithmetic and copies ran while one was open for 0% of the time, Pallas kernels for 8%

profile of v4, /device:TPU:1, one launch (start us, length us, event | category | flops | bytes accessed | tf_op | source)
XLA Modules:
  0.0 47.8 jit_solution(8400337572575129763)
XLA Ops:
  0.6 1.1 %shard_map.84 = (bf16[5,24,128]{2,1,0:T(8,128)(2,1)S(1)}, bf16[5,24,128]{2,1,0:T(8,128)(2,1)S(1)}, bf16[17,24,128]{2,1,0:T(8,128)(2,1)S(1)}, f32[3,16,128]{2,1,0:T(8,128)S(1)}) custom-call(bf16[8,24,128]{2,1,0:T(8,128)(2,1)} %bitcast.9, bf16[8,24,128]{2,1,0:T(8,128)(2,1)} %bitcast.10, s32[8,24]{1,0:T(8,128)} %bitcast.12, s32[8,24]{1,0:T(8,128)} %bitcast.13, ...), custom_call_target="tpu_custom_call" | custom-call | tf_op jit(solution)/shard_map/pallas_call | solution.py:340
  1.8 2.5 %collective-permute-start = (bf16[5,24,128]{2,1,0:T(8,128)(2,1)S(1)}, bf16[5,24,128]{2,1,0:T(8,128)(2,1)S(1)}, u32[]{:S(2)}, u32[]{:S(2)}) collective-permute-start(bf16[5,24,128]{2,1,0:T(8,128)(2,1)S(1)} %get-tuple-element.20), channel_id=1, source_target_pairs={{0,8},{8,16},{16,24},{24,0},{1,9},{9,17},{17,25},{25,1},{2,10},{10... | collective-permute-start | bytes 92168 | tf_op jit(solution)/shard_map/ppermute | solution.py:354
  4.3 2.2 %collective-permute-start.1 = (bf16[5,24,128]{2,1,0:T(8,128)(2,1)S(1)}, bf16[5,24,128]{2,1,0:T(8,128)(2,1)S(1)}, u32[]{:S(2)}, u32[]{:S(2)}) collective-permute-start(bf16[5,24,128]{2,1,0:T(8,128)(2,1)S(1)} %get-tuple-element.21), channel_id=1, source_target_pairs={{8,0},{16,8},{24,16},{0,24},{9,1},{17,9},{25,17},{1,25},{10,2},{18... | collective-permute-start | bytes 92168 | tf_op jit(solution)/shard_map/ppermute | solution.py:355
  6.5 1.2 %collective-permute-done.prev_ref = bf16[5,24,128]{2,1,0:T(8,128)(2,1)S(1)} collective-permute-done((bf16[5,24,128]{2,1,0:T(8,128)(2,1)S(1)}, bf16[5,24,128]{2,1,0:T(8,128)(2,1)S(1)}, u32[]{:S(2)}, u32[]{:S(2)}) %collective-permute-start) | collective-permute-done | bytes 30752 | tf_op jit(solution)/shard_map/ppermute | solution.py:354
  7.7 0.0 collective-permute-done.1.next_ref
  7.8 1.3 %collective-permute-start.2 = (bf16[13,24,128]{2,1,0:T(8,128)(2,1)S(1)}, bf16[13,24,128]{2,1,0:T(8,128)(2,1)S(1)}, u32[]{:S(2)}, u32[]{:S(2)}) collective-permute-start(bf16[13,24,128]{2,1,0:T(8,128)(2,1)S(1)} %get-tuple-element.23), channel_id=1, source_target_pairs={{0,2},{1,3},{2,4},{3,5},{4,6},{5,7},{6,0},{7,1},{8,10},{9,11},{10,... | collective-permute-start | bytes 239624 | tf_op jit(solution)/shard_map/ppermute | solution.py:367
  9.1 2.5 %collective-permute-start.3 = (bf16[13,24,128]{2,1,0:T(8,128)(2,1)S(1)}, bf16[13,24,128]{2,1,0:T(8,128)(2,1)S(1)}, u32[]{:S(2)}, u32[]{:S(2)}) collective-permute-start(bf16[13,24,128]{2,1,0:T(8,128)(2,1)S(1)} %get-tuple-element.24), channel_id=1, source_target_pairs={{0,4},{1,5},{2,6},{3,7},{4,0},{5,1},{6,2},{7,3},{8,12},{9,13},{10,... | collective-permute-start | bytes 239624 | tf_op jit(solution)/shard_map/ppermute | solution.py:367
  11.5 1.2 %collective-permute-start.4 = (bf16[13,24,128]{2,1,0:T(8,128)(2,1)S(1)}, bf16[13,24,128]{2,1,0:T(8,128)(2,1)S(1)}, u32[]{:S(2)}, u32[]{:S(2)}) collective-permute-start(bf16[13,24,128]{2,1,0:T(8,128)(2,1)S(1)} %get-tuple-element.25), channel_id=1, source_target_pairs={{0,6},{1,7},{2,0},{3,1},{4,2},{5,3},{6,4},{7,5},{8,14},{9,15},{10,... | collective-permute-start | bytes 239624 | tf_op jit(solution)/shard_map/ppermute | solution.py:367
  12.7 2.4 %collective-permute-start.5 = (bf16[13,24,128]{2,1,0:T(8,128)(2,1)S(1)}, bf16[13,24,128]{2,1,0:T(8,128)(2,1)S(1)}, u32[]{:S(2)}, u32[]{:S(2)}) collective-permute-start(bf16[13,24,128]{2,1,0:T(8,128)(2,1)S(1)} %get-tuple-element.22.refs_0_), channel_id=1, source_target_pairs={{0,1},{1,0},{2,3},{3,2},{4,5},{5,4},{6,7},{7,6},{8,9},{9,8},{10,11... | collective-permute-start | bytes 239624 | tf_op jit(solution)/shard_map/ppermute | solution.py:368
  15.1 0.0 collective-permute-done.2.refs_1_
  15.1 0.7 %collective-permute-start.6 = (bf16[13,24,128]{2,1,0:T(8,128)(2,1)S(1)}, bf16[13,24,128]{2,1,0:T(8,128)(2,1)S(1)}, u32[]{:S(2)}, u32[]{:S(2)}) collective-permute-start(bf16[13,24,128]{2,1,0:T(8,128)(2,1)S(1)} %collective-permute-done.2.refs_1_), channel_id=1, source_target_pairs={{0,1},{1,0},{2,3},{3,2},{4,5},{5,4},{6,7},{7,6},{8,9},{9,8},{10,11... | collective-permute-start | bytes 239624 | tf_op jit(solution)/shard_map/ppermute | solution.py:368
  15.7 0.0 collective-permute-done.3.refs_2_
  15.7 1.1 %collective-permute-start.7 = (bf16[13,24,128]{2,1,0:T(8,128)(2,1)S(1)}, bf16[13,24,128]{2,1,0:T(8,128)(2,1)S(1)}, u32[]{:S(2)}, u32[]{:S(2)}) collective-permute-start(bf16[13,24,128]{2,1,0:T(8,128)(2,1)S(1)} %collective-permute-done.3.refs_2_), channel_id=1, source_target_pairs={{0,1},{1,0},{2,3},{3,2},{4,5},{5,4},{6,7},{7,6},{8,9},{9,8},{10,11... | collective-permute-start | bytes 239624 | tf_op jit(solution)/shard_map/ppermute | solution.py:368
  16.9 0.0 collective-permute-done.4.refs_3_
  16.9 1.2 %collective-permute-start.8 = (bf16[13,24,128]{2,1,0:T(8,128)(2,1)S(1)}, bf16[13,24,128]{2,1,0:T(8,128)(2,1)S(1)}, u32[]{:S(2)}, u32[]{:S(2)}) collective-permute-start(bf16[13,24,128]{2,1,0:T(8,128)(2,1)S(1)} %collective-permute-done.4.refs_3_), channel_id=1, source_target_pairs={{0,1},{1,0},{2,3},{3,2},{4,5},{5,4},{6,7},{7,6},{8,9},{9,8},{10,11... | collective-permute-start | bytes 239624 | tf_op jit(solution)/shard_map/ppermute | solution.py:368
  18.0 0.0 collective-permute-done.5.refs_4_
  18.1 0.9 %collective-permute-done.8.refs_7_ = bf16[13,24,128]{2,1,0:T(8,128)(2,1)S(1)} collective-permute-done((bf16[13,24,128]{2,1,0:T(8,128)(2,1)S(1)}, bf16[13,24,128]{2,1,0:T(8,128)(2,1)S(1)}, u32[]{:S(2)}, u32[]{:S(2)}) %collective-permute-start.8) | collective-permute-done | bytes 79904 | tf_op jit(solution)/shard_map/ppermute | solution.py:368
  19.0 3.5 %shard_map.86 = (f32[16,8,128]{2,1,0:T(8,128)}, bf16[384,256]{1,0:T(8,128)(2,1)S(1)}, f32[192,128]{1,0:T(8,128)S(1)}) custom-call(bf16[13,24,128]{2,1,0:T(8,128)(2,1)S(1)} %get-tuple-element.22.refs_0_, bf16[13,24,128]{2,1,0:T(8,128)(2,1)S(1)} %collective-permute-done.2.refs_1_, bf16[13,24,128]{2,1,0:T(8,128)(2,1)S(1)} %collective-permute-done.3.refs_2_, ...), custom_call_target="tpu_custom_call" | custom-call | flops 2147483648 | bytes 1048576 | tf_op jit(solution)/shard_map/pallas_call | solution.py:328
  22.5 7.2 %all-to-all-start = ((f32[16,8,128]{2,1,0:T(8,128)}), f32[16,8,128]{2,1,0:T(8,128)S(1)}, u32[]{:S(2)}, u32[]{:S(2)}) async-start(f32[16,8,128]{2,1,0:T(8,128)} %get-tuple-element.29), calls=%async_computation | async-start | bytes 131072 | tf_op jit(solution)/shard_map/all_to_all | solution.py:390
  29.7 3.8 %shard_map.87.grads_ref = bf16[8,2,24,128]{3,2,1,0:T(8,128)(2,1)S(1)} custom-call(bf16[13,24,128]{2,1,0:T(8,128)(2,1)S(1)} %get-tuple-element.22.refs_0_, bf16[13,24,128]{2,1,0:T(8,128)(2,1)S(1)} %collective-permute-done.2.refs_1_, bf16[13,24,128]{2,1,0:T(8,128)(2,1)S(1)} %collective-permute-done.3.refs_2_, ...), custom_call_target="tpu_custom_call" | custom-call | flops 3221225472 | bytes 1048576 | tf_op jit(solution)/shard_map/pallas_call | solution.py:328
  33.5 2.7 %all-to-all-done.sums_ref = f32[16,8,128]{2,1,0:T(8,128)S(1)} async-done(((f32[16,8,128]{2,1,0:T(8,128)}), f32[16,8,128]{2,1,0:T(8,128)S(1)}, u32[]{:S(2)}, u32[]{:S(2)}) %all-to-all-start) | async-done | bytes 65568 | tf_op jit(solution)/shard_map/all_to_all | solution.py:390
  36.2 0.1 shard_map.88
  36.3 10.6 %all_to_all.10.recv_ref = bf16[8,56,128]{2,1,0:T(8,128)(2,1)S(1)} all-to-all(bf16[8,56,128]{2,1,0:T(8,128)(2,1)S(1)} %shard_map.88), channel_id=1, replica_groups=mesh['dp'=4,'ha'=4,'wa'=8] {'wa'}, dimensions={0} | all-to-all | bytes 229376 | tf_op jit(solution)/shard_map/all_to_all | solution.py:409
  46.9 0.9 %shard_map.89 = (f32[8,24,128]{2,1,0:T(8,128)}, f32[8,24,128]{2,1,0:T(8,128)}, f32[3,3,3,8]{3,2,1,0:T(4,128)}, f32[1,1]{1,0:T(1,128)}) custom-call(bf16[8,56,128]{2,1,0:T(8,128)(2,1)S(1)} %all_to_all.10.recv_ref), custom_call_target="tpu_custom_call" | custom-call | bytes 1048576 | tf_op jit(solution)/shard_map/pallas_call | solution.py:328
  (3 shorter events, 0.1 us)
Async XLA Ops:
  1.8 5.9 %collective-permute-start = (bf16[5,24,128]{2,1,0:T(8,128)(2,1)S(1)}, bf16[5,24,128]{2,1,0:T(8,128)(2,1)S(1)}, u32[]{:S(2)}, u32[]{:S(2)}) collective-permute-start(bf16[5,24,128]{2,1,0:T(8,128)(2,1)S(1)} %get-tuple-element.20), channel_id=1, source_target_pairs={{0,8},{8,16},{16,24},{24,0},{1,9},{9,17},{17,25},{25,1},{2,10},{10... | collective-permute-start | bytes 92168 | tf_op jit(solution)/shard_map/ppermute | solution.py:354
  4.3 3.4 %collective-permute-start.1 = (bf16[5,24,128]{2,1,0:T(8,128)(2,1)S(1)}, bf16[5,24,128]{2,1,0:T(8,128)(2,1)S(1)}, u32[]{:S(2)}, u32[]{:S(2)}) collective-permute-start(bf16[5,24,128]{2,1,0:T(8,128)(2,1)S(1)} %get-tuple-element.21), channel_id=1, source_target_pairs={{8,0},{16,8},{24,16},{0,24},{9,1},{17,9},{25,17},{1,25},{10,2},{18... | collective-permute-start | bytes 92168 | tf_op jit(solution)/shard_map/ppermute | solution.py:355
  7.8 7.3 %collective-permute-start.2 = (bf16[13,24,128]{2,1,0:T(8,128)(2,1)S(1)}, bf16[13,24,128]{2,1,0:T(8,128)(2,1)S(1)}, u32[]{:S(2)}, u32[]{:S(2)}) collective-permute-start(bf16[13,24,128]{2,1,0:T(8,128)(2,1)S(1)} %get-tuple-element.23), channel_id=1, source_target_pairs={{0,2},{1,3},{2,4},{3,5},{4,6},{5,7},{6,0},{7,1},{8,10},{9,11},{10,... | collective-permute-start | bytes 239624 | tf_op jit(solution)/shard_map/ppermute | solution.py:367
  9.1 6.7 %collective-permute-start.3 = (bf16[13,24,128]{2,1,0:T(8,128)(2,1)S(1)}, bf16[13,24,128]{2,1,0:T(8,128)(2,1)S(1)}, u32[]{:S(2)}, u32[]{:S(2)}) collective-permute-start(bf16[13,24,128]{2,1,0:T(8,128)(2,1)S(1)} %get-tuple-element.24), channel_id=1, source_target_pairs={{0,4},{1,5},{2,6},{3,7},{4,0},{5,1},{6,2},{7,3},{8,12},{9,13},{10,... | collective-permute-start | bytes 239624 | tf_op jit(solution)/shard_map/ppermute | solution.py:367
  11.5 5.4 %collective-permute-start.4 = (bf16[13,24,128]{2,1,0:T(8,128)(2,1)S(1)}, bf16[13,24,128]{2,1,0:T(8,128)(2,1)S(1)}, u32[]{:S(2)}, u32[]{:S(2)}) collective-permute-start(bf16[13,24,128]{2,1,0:T(8,128)(2,1)S(1)} %get-tuple-element.25), channel_id=1, source_target_pairs={{0,6},{1,7},{2,0},{3,1},{4,2},{5,3},{6,4},{7,5},{8,14},{9,15},{10,... | collective-permute-start | bytes 239624 | tf_op jit(solution)/shard_map/ppermute | solution.py:367
  12.7 5.4 %collective-permute-start.5 = (bf16[13,24,128]{2,1,0:T(8,128)(2,1)S(1)}, bf16[13,24,128]{2,1,0:T(8,128)(2,1)S(1)}, u32[]{:S(2)}, u32[]{:S(2)}) collective-permute-start(bf16[13,24,128]{2,1,0:T(8,128)(2,1)S(1)} %get-tuple-element.22.refs_0_), channel_id=1, source_target_pairs={{0,1},{1,0},{2,3},{3,2},{4,5},{5,4},{6,7},{7,6},{8,9},{9,8},{10,11... | collective-permute-start | bytes 239624 | tf_op jit(solution)/shard_map/ppermute | solution.py:368
  15.1 3.0 %collective-permute-start.6 = (bf16[13,24,128]{2,1,0:T(8,128)(2,1)S(1)}, bf16[13,24,128]{2,1,0:T(8,128)(2,1)S(1)}, u32[]{:S(2)}, u32[]{:S(2)}) collective-permute-start(bf16[13,24,128]{2,1,0:T(8,128)(2,1)S(1)} %collective-permute-done.2.refs_1_), channel_id=1, source_target_pairs={{0,1},{1,0},{2,3},{3,2},{4,5},{5,4},{6,7},{7,6},{8,9},{9,8},{10,11... | collective-permute-start | bytes 239624 | tf_op jit(solution)/shard_map/ppermute | solution.py:368
  15.7 2.3 %collective-permute-start.7 = (bf16[13,24,128]{2,1,0:T(8,128)(2,1)S(1)}, bf16[13,24,128]{2,1,0:T(8,128)(2,1)S(1)}, u32[]{:S(2)}, u32[]{:S(2)}) collective-permute-start(bf16[13,24,128]{2,1,0:T(8,128)(2,1)S(1)} %collective-permute-done.3.refs_2_), channel_id=1, source_target_pairs={{0,1},{1,0},{2,3},{3,2},{4,5},{5,4},{6,7},{7,6},{8,9},{9,8},{10,11... | collective-permute-start | bytes 239624 | tf_op jit(solution)/shard_map/ppermute | solution.py:368
  16.9 2.1 %collective-permute-start.8 = (bf16[13,24,128]{2,1,0:T(8,128)(2,1)S(1)}, bf16[13,24,128]{2,1,0:T(8,128)(2,1)S(1)}, u32[]{:S(2)}, u32[]{:S(2)}) collective-permute-start(bf16[13,24,128]{2,1,0:T(8,128)(2,1)S(1)} %collective-permute-done.4.refs_3_), channel_id=1, source_target_pairs={{0,1},{1,0},{2,3},{3,2},{4,5},{5,4},{6,7},{7,6},{8,9},{9,8},{10,11... | collective-permute-start | bytes 239624 | tf_op jit(solution)/shard_map/ppermute | solution.py:368
  22.5 13.7 %all-to-all-start = ((f32[16,8,128]{2,1,0:T(8,128)}), f32[16,8,128]{2,1,0:T(8,128)S(1)}, u32[]{:S(2)}, u32[]{:S(2)}) async-start(f32[16,8,128]{2,1,0:T(8,128)} %get-tuple-element.29), calls=%async_computation | async-start | bytes 131072 | tf_op jit(solution)/shard_map/all_to_all | solution.py:390

commit v5 on v4

--- a/solution.py
+++ b/solution.py
@@ -12,7 +12,7 @@
 WT = 192
 JP = 256
 GT_LANE, VALID_LANE = 0, 16
-LOSS_LANE, COUNT_LANE, THIRD = 27, 28, 32
+LOSS_LANE, COUNT_LANE, SHARE = 27, 28, 32
 VMEM = pltpu.CompilerParams(vmem_limit_bytes=48 * 1024 * 1024)
 NT = (((1,), (1,)), ((), ()))
 NN = (((1,), (0,)), ((), ()))
@@ -140,7 +140,7 @@
     return high, (value - high.astype(F32)).astype(BF16)
 
 
-def weighted(a, left, wc_ref, ab):
+def weighted(a, left, wc_ref, ab, at):
     for si in range(5):
         value = None
         for b in range(3):
@@ -149,7 +149,7 @@
                 term = wc_ref[a, 3 * b + e : 3 * b + e + 1] * left[b]
                 value = term if value is None else value + term
         for i, part in enumerate(split3(value)):
-            ab[i * WT : (i + 1) * WT, (5 * a + si) * CH : (5 * a + si + 1) * CH] = part
+            ab[at + i * WT : at + (i + 1) * WT, si * CH : (si + 1) * CH] = part
 
 
 def row_gradient(q, logits, diag_col, ms, masks):
@@ -190,65 +190,42 @@
     return lane, level, inside, on_diag, wcol, zeros_count, zeros_mean
 
 
-def forward(q, ls, rs, rb, wc_ref, ab, ms):
+def logits_of(ls, rb, wc_ref, ab, acc):
+    for rho in range(5):
+        rows = [q for q in range(3) if 0 <= rho - q <= 2]
+        left = [ls[rho, 7 + b : 7 + b + WT] for b in range(3)]
+        for i, q in enumerate(rows):
+            weighted(rho - q, left, wc_ref, ab.at[rho], 3 * WT * i)
+        part = dot(ab[rho, 0 : 3 * WT * len(rows)], rb[:, 5 * rho * CH : 5 * (rho + 1) * CH], NT)
+        for i, q in enumerate(rows):
+            at = 3 * WT * i
+            total = part[at : at + WT] + part[at + WT : at + 2 * WT] + part[at + 2 * WT : at + 3 * WT]
+            acc[q] = total if rho == q else acc[q] + total
+
+
+def main_kernel(*refs):
+    recv, wc_ref = refs[:8], refs[8]
+    sums_ref, kept_ref, given_ref = refs[9:12]
+    ls, rs, rb, ms, ab, acc, ub, diags, ks, lb, xs, ys, out_ref = refs[12:]
+    fill_meta(fill(recv, 0, 5, ls, rs, rb), ms)
+    ks[...] = jnp.zeros(ks.shape, F32)
+    xs[...] = jnp.zeros(xs.shape, F32)
     masks = row_masks()
-    diag = None
-    for a in range(3):
-        left = [ls[q + a, 7 + b : 7 + b + WT] for b in range(3)]
-        weighted(a, left, wc_ref, ab)
-        for b in range(3):
-            term = wc_ref[a, 3 * b : 3 * b + 1] * left[b] * rs[q + a, 8 + b : 8 + b + WT]
-            diag = term if diag is None else diag + term
-    parts = dot(ab[...], rb[:, 5 * q * CH : (5 * q + 15) * CH], NT)
-    logits = parts[0:WT] + parts[WT : 2 * WT] + parts[2 * WT : 3 * WT]
-    up, resid, usable = row_gradient(q, logits, jnp.sum(diag, axis=1, keepdims=True), ms, masks)
-    return up, diagonal(up, masks[3]), resid, usable
-
-
-def own_kernel(*refs):
-    recv, wc_ref = refs[:8], refs[8]
-    sums_ref, ub, diag_ref, ls, rs, rb, ms, ab, ks = refs[9:]
-    fill_meta(fill(recv, 1, 3, ls, rs, rb), ms)
-    ks[...] = jnp.zeros(ks.shape, F32)
-    up, up_diag, resid, usable = forward(1, ls, rs, rb, wc_ref, ab, ms)
-    ub[0:WT], ub[WT : 2 * WT] = split2(up)
-    diag_ref[...] = jnp.broadcast_to(up_diag, (WT, CH))
-    size = jnp.abs(resid)
-    smooth = jnp.where(size < 1.0, 0.5 * resid * resid, size - 0.5)
-    loss_sum = jnp.sum(usable * smooth, axis=0, keepdims=True)
-    count_sum = jnp.sum(usable, axis=0, keepdims=True)
-    terms = dot(ub[...], rb[:, 5 * CH : 20 * CH])
-    for a in range(3):
-        for b in range(3):
-            left = ls[1 + a, 7 + b : 7 + b + WT]
-            for e in range(3):
-                si = 5 * a + b - e + 2
-                value = terms[0:WT, si * CH : (si + 1) * CH] + terms[WT:, si * CH : (si + 1) * CH]
-                if e == 0:
-                    value = value - up_diag * rs[1 + a, 8 + b : 8 + b + WT]
-                at = 9 * a + 3 * b + e
-                ks[at : at + 1] = jnp.sum(left * value, axis=0, keepdims=True)
-    channel = lax.broadcasted_iota(jnp.int32, (8, CH), 1)
-    member = group_member().astype(BF16)
-    parts = [dot(member, part, NT) for part in split3(ks[...])]
-    sums = (parts[0] + (parts[1] + parts[2])) * (1.0 / 16.0)
-    sums = jnp.where(channel == LOSS_LANE, loss_sum, sums)
-    sums = jnp.where(channel == COUNT_LANE, count_sum, sums)
-    for i in range(sums_ref.shape[0]):
-        sums_ref[i] = sums
-
-
-def rest_kernel(*refs):
-    recv, (wc_ref, own_ub, own_diag, out_ref) = refs[:8], refs[8:12]
-    ls, rs, rb, ms, ab, ub, diags, lb, xs, ys = refs[12:]
-    fill_meta(fill(recv, 0, 5, ls, rs, rb), ms)
-    xs[...] = jnp.zeros(xs.shape, F32)
-    for q in (0, 2):
-        up, up_diag, _, _ = forward(q, ls, rs, rb, wc_ref, ab, ms)
+    logits_of(ls, rb, wc_ref, ab, acc)
+    for q in range(3):
+        diag = None
+        for a in range(3):
+            for b in range(3):
+                term = wc_ref[a, 3 * b : 3 * b + 1] * ls[q + a, 7 + b : 7 + b + WT] * rs[q + a, 8 + b : 8 + b + WT]
+                diag = term if diag is None else diag + term
+        up, resid, usable = row_gradient(q, acc[q], jnp.sum(diag, axis=1, keepdims=True), ms, masks)
         ub[2 * WT * q : 2 * WT * q + WT], ub[2 * WT * q + WT : 2 * WT * (q + 1)] = split2(up)
-        diags[q] = jnp.broadcast_to(up_diag, (WT, CH))
-    ub[2 * WT : 4 * WT] = own_ub[...]
-    diags[1] = own_diag[...]
+        diags[q] = jnp.broadcast_to(diagonal(up, masks[3]), (WT, CH))
+        if q == 1:
+            size = jnp.abs(resid)
+            smooth = jnp.where(size < 1.0, 0.5 * resid * resid, size - 0.5)
+            loss_sum = jnp.sum(usable * smooth, axis=0, keepdims=True)
+            count_sum = jnp.sum(usable, axis=0, keepdims=True)
     for b in range(3):
         shifted = ls[2, 7 + b : 7 + b + WT].astype(BF16)
         lb[0:WT, b * CH : (b + 1) * CH] = shifted
@@ -259,6 +236,7 @@
 
     terms = dot(ub[...], rb[:, 10 * CH : 15 * CH])
     for b in range(3):
+        own_left, own_right = ls[2, 7 + b : 7 + b + WT], rs[2, 8 + b : 8 + b + WT]
         total = None
         spread = None
         for q in range(3):
@@ -268,10 +246,14 @@
                 at, si = 2 * WT * q, b - e + 2
                 value = terms[at : at + WT, si * CH : (si + 1) * CH]
                 value = value + terms[at + WT : at + 2 * WT, si * CH : (si + 1) * CH]
+                if e == 0:
+                    value = value - diags[q] * own_right
+                at = 9 * (2 - q) + 3 * b + e
+                ks[at : at + 1] = jnp.sum(own_left * value, axis=0, keepdims=True)
                 term = tap(q, b, e) * value
                 total = term if total is None else total + term
-        xs[b, 8 : 8 + WT] = total - spread * rs[2, 8 + b : 8 + b + WT]
-        xs[3 + b, 8 : 8 + WT] = spread * ls[2, 7 + b : 7 + b + WT]
+        xs[b, 8 : 8 + WT] = total
+        xs[3 + b, 8 : 8 + WT] = spread * own_left
     for q in range(3):
         terms = dot(ub[2 * WT * q : 2 * WT * (q + 1)], lb[...], TN)
         for si in range(5):
@@ -282,6 +264,20 @@
                     term = tap(q, b, e) * terms[:, b * CH : (b + 1) * CH]
                     total = term if total is None else total + term
             ys[si] = total if q == 0 else ys[si] + total
+    channel = lax.broadcasted_iota(jnp.int32, (8, CH), 1)
+    member = group_member().astype(BF16)
+    parts = [dot(member, part, NT) for part in split3(ks[...])]
+    sums = (parts[0] + (parts[1] + parts[2])) * (1.0 / 16.0)
+    sums = jnp.where(channel == LOSS_LANE, loss_sum, sums)
+    sums = jnp.where(channel == COUNT_LANE, count_sum, sums)
+    sums = jnp.where(channel < SHARE, sums, 0.0)
+    quarter = lax.broadcasted_iota(jnp.int32, (8, CH), 0) & 3
+    placed = jnp.where(quarter == 0, sums, 0.0)
+    for i in range(1, 4):
+        placed = placed + jnp.where(quarter == i, pltpu.roll(sums, SHARE * i, 1), 0.0)
+    packed = jnp.concatenate([jnp.sum(placed[4 * i : 4 * i + 4], axis=0, keepdims=True) for i in range(2)], axis=0)
+    for i in range(sums_ref.shape[0]):
+        sums_ref[i] = packed
     grad_left = xs[0, 9 : 9 + WT] + xs[1, 8 : 8 + WT] + xs[2, 7 : 7 + WT]
     grad_right = ys[0, 4 : 4 + WT]
     for si in range(1, 5):
@@ -291,30 +287,59 @@
     for dst in range(WA):
         out_ref[dst, 0] = grad_left[TILE * dst : TILE * (dst + 1)].astype(BF16)
         out_ref[dst, 1] = grad_right[TILE * dst : TILE * (dst + 1)].astype(BF16)
-
-
-def payload_kernel(grads_ref, sums_ref, out_ref):
-    total = sums_ref[0]
-    for i in range(1, sums_ref.shape[0]):
-        total = total + sums_ref[i]
-    lane = lax.broadcasted_iota(jnp.int32, (8, CH), 1)
-    high, middle, low = [jnp.where(lane < THIRD, part.astype(F32), 0.0) for part in split3(total)]
-    sums = high + pltpu.roll(middle, THIRD, 1) + pltpu.roll(low, 2 * THIRD, 1)
-    for dst in range(WA):
-        left, right = grads_ref[dst, 0].astype(F32), grads_ref[dst, 1].astype(F32)
-        out_ref[dst] = jnp.concatenate([left, right, sums], axis=0).astype(BF16)
-
-
-def finish_kernel(recv_ref, left_ref, right_ref, weight_ref, loss_ref):
-    total = recv_ref[0].astype(F32)[2 * TILE :]
-    for src in range(1, WA):
-        total = total + recv_ref[src].astype(F32)[2 * TILE :]
-    total = total + pltpu.roll(total, CH - THIRD, 1) + pltpu.roll(total, CH - 2 * THIRD, 1)
+    chip, core = position()
+    for ref, holder in ((kept_ref, core), (given_ref, 1 - core)):
+        beside = chip_at(chip, ahead(holder))
+        opposite = chip_at(chip, 2)
+        places = (2 * beside + holder, 2 * beside + 1 - holder, 2 * opposite + holder, 2 * chip + holder)
+        for i, tile in enumerate(places):
+            for side in range(2):
+                ref[2 * i + side] = out_ref[tile, side]
+
+
+def ahead(core):
+    return 1 - 2 * core
+
+
+def chip_at(chip, step):
+    return (chip + step + CHIPS) & (CHIPS - 1)
+
+
+def pack_back_kernel(kept_ref, got_ref, *outs):
+    for place, out_ref in zip((2, 0, 1), outs):
+        for row, ref in enumerate((kept_ref, got_ref)):
+            for side in range(2):
+                out_ref[2 * row + side] = ref[2 * place + side]
+
+
+def finish_kernel(kept, got, near, far, across, sums_ref, left_ref, right_ref, weight_ref, loss_ref):
+    chip, core = position()
+    other = 1 - core
+    before, after, opposite = chip_at(chip, -ahead(core)), chip_at(chip, ahead(core)), chip_at(chip, 2)
+    partial = [sums_ref[i] for i in range(8)]
+    for i in range(8, sums_ref.shape[0]):
+        partial[i % 8] = partial[i % 8] + sums_ref[i]
+    while len(partial) > 1:
+        partial = [x + y for x, y in zip(partial[0::2], partial[1::2])]
+    placed = partial[0]
+    total = jnp.concatenate(
+        [pltpu.roll(jnp.broadcast_to(placed[g // 4 : g // 4 + 1], (8, CH)), (CH - SHARE * (g % 4)) % CH, 1)[0:1] for g in range(8)],
+        axis=0,
+    )
     norm = 1.0 / jnp.maximum(total[0:1, COUNT_LANE : COUNT_LANE + 1], 1.0)
-    for src in range(WA):
-        block = recv_ref[src].astype(F32) * norm
-        left_ref[src] = block[0:TILE]
-        right_ref[src] = block[TILE : 2 * TILE]
+    blocks = (
+        (kept, 6, 2 * chip + core),
+        (got, 6, 2 * chip + other),
+        (near, 0, 2 * before + core),
+        (near, 2, 2 * before + other),
+        (far, 0, 2 * after + other),
+        (far, 2, 2 * after + core),
+        (across, 0, 2 * opposite + core),
+        (across, 2, 2 * opposite + other),
+    )
+    for ref, at, row in blocks:
+        left_ref[row] = ref[at].astype(F32) * norm
+        right_ref[row] = ref[at + 1].astype(F32) * norm
     loss_ref[...] = total[0:1, LOSS_LANE : LOSS_LANE + 1] * norm
     by_tap = jnp.concatenate([total * norm, jnp.zeros((CH - 8, CH), F32)], axis=0).T
     for a in range(3):
@@ -328,6 +353,10 @@
     return pl.pallas_call(
         kernel, out_shape=out_shape, scratch_shapes=list(scratch), compiler_params=params, cost_estimate=cost
     )(*args)
+
+
+def swapped(value):
+    return lax.ppermute(value, "wa", [(i, i ^ 1) for i in range(WA)])
 
 
 def shards(left_feat, right_feat, conv_weight, disparity_gt, valid_mask):
@@ -367,51 +396,47 @@
         same_core.append(lax.ppermute(blocks[hop], "wa", [(i, (i + 2 * hop) % WA) for i in range(WA)]))
     other_core = [lax.ppermute(value, "wa", [(i, i ^ 1) for i in range(WA)]) for value in same_core]
     tiles = same_core + other_core
-    others = lax.axis_size("dp") * ha_count
-    rows = (
-        pltpu.VMEM((5, WT + 16, CH), F32),
-        pltpu.VMEM((5, WT + 80, CH), F32),
-        pltpu.VMEM((JP, 25 * CH), BF16),
-        pltpu.VMEM((WT, CH), F32),
-        pltpu.VMEM((3 * WT, 15 * CH), BF16),
-    )
-    sums, own_ub, own_diag = call(
-        own_kernel,
-        (
-            jax.ShapeDtypeStruct((others, 8, CH), F32),
-            jax.ShapeDtypeStruct((2 * WT, JP), BF16),
-            jax.ShapeDtypeStruct((WT, CH), F32),
-        ),
+    others = lax.axis_size("dp") * ha_count * WA
+    half = jax.ShapeDtypeStruct((8, TILE, CH), BF16)
+    sums, kept, given = call(
+        main_kernel,
+        (jax.ShapeDtypeStruct((others, 2, CH), F32), half, half),
         *tiles,
         taps,
-        scratch=rows + (pltpu.VMEM((CH, CH), F32),),
-        flops=2 << 30,
-    )
-    sums = lax.all_to_all(sums, ("dp", "ha"), 0, 0, tiled=True)
-    grads = call(
-        rest_kernel,
-        jax.ShapeDtypeStruct((WA, 2, TILE, CH), BF16),
-        *tiles,
-        taps,
-        own_ub,
-        own_diag,
-        scratch=rows
-        + (
+        scratch=(
+            pltpu.VMEM((5, WT + 16, CH), F32),
+            pltpu.VMEM((5, WT + 80, CH), F32),
+            pltpu.VMEM((JP, 25 * CH), BF16),
+            pltpu.VMEM((WT, CH), F32),
+            pltpu.VMEM((5, 9 * WT, 5 * CH), BF16),
+            pltpu.VMEM((3, WT, JP), F32),
             pltpu.VMEM((6 * WT, JP), BF16),
             pltpu.VMEM((3, WT, CH), F32),
+            pltpu.VMEM((CH, CH), F32),
             pltpu.VMEM((2 * WT, 3 * CH), BF16),
             pltpu.VMEM((6, WT + 16, CH), F32),
             pltpu.VMEM((5, JP, CH), F32),
+            pltpu.VMEM((WA, 2, TILE, CH), BF16),
         ),
-        flops=3 << 30,
-    )
-    payload = call(payload_kernel, jax.ShapeDtypeStruct((WA, 2 * TILE + 8, CH), BF16), grads, sums)
-    back = lax.all_to_all(payload, "wa", 0, 0, tiled=True)
+        flops=5 << 30,
+    )
+    sums = lax.all_to_all(sums, ("dp", "ha", "wa"), 0, 0, tiled=True)
+    got = swapped(given)
+    block = jax.ShapeDtypeStruct((4, TILE, CH), BF16)
+    opposite, beside, beside_other = call(pack_back_kernel, (block,) * 3, kept, got)
+    across = lax.ppermute(opposite, "wa", [(i, (i + 4) % WA) for i in range(WA)])
+    near = lax.ppermute(beside, "wa", [(i, (i + 2 - 4 * (i % 2)) % WA) for i in range(WA)])
+    far = lax.ppermute(beside_other, "wa", [(i, (i + 3 - 6 * (i % 2)) % WA) for i in range(WA)])
     tile = jax.ShapeDtypeStruct((ROWS, TILE, CH), F32)
     grad_left, grad_right, weight, loss = call(
         finish_kernel,
         (tile, tile, jax.ShapeDtypeStruct((3, 3, 3, 8), F32), jax.ShapeDtypeStruct((1, 1), F32)),
-        back,
+        kept,
+        got,
+        near,
+        far,
+        across,
+        sums,
     )
     return (loss[0, 0], grad_left[None], grad_right[None], jnp.transpose(weight, (3, 0, 1, 2)))
 

time: 48.1 us -> 45.9 us (0.954)
  blocking collectives: 10.6 us -> 0 us
  starting transfers between devices: 22.2 us -> 29.7 us
  waiting for transfers between devices: 4.82 us -> 6.77 us
  Pallas kernels: 9.48 us -> 8.59 us
    all_to_all x1 -> x0, blocking collectives: 10.6 us -> none  [shards(): back = lax.all_to_all(payload, 'wa', 0, 0, tiled=True)]
    ppermute x0 -> x4, starting transfers between devices: none -> 5.31 us  [the longest x1 1.89 us: shards(): lax.ppermute(beside, 'wa', [(i, (i + 2 - 4 * (i % 2)) % WA) for i in rang...]
    ppermute x0 -> x4, waiting for transfers between devices: none -> 4.38 us  [the longest x1 2.74 us: shards(): lax.ppermute(beside_other, 'wa', [(i, (i + 3 - 6 * (i % 2)) % WA) for i i...]
    all_to_all x1, waiting for transfers between devices: 2.7 us -> 0.26 us  [shards(): sums = lax.all_to_all(sums, ('dp', 'ha', 'wa'), 0, 0, tiled=True)]
    all_to_all x1, starting transfers between devices: 7.21 us -> 9.41 us  [shards(): sums = lax.all_to_all(sums, ('dp', 'ha', 'wa'), 0, 0, tiled=True)]
    pallas_call x5 -> x4, Pallas kernels: 8.34 us -> 7.45 us  [call(): pl.pallas_call(kernel, out_shape=out_shape, scratch_shapes=list(scratch),...]
  transfers between devices with their start and end apart: 10 -> 14, of which waited for: 3 -> 6; matrix products, arithmetic and copies ran while one was open for 0% -> 0% of each run, Pallas kernels for 8% -> 0%
where the time goes in v5:
time: 45.9 us; the launch traced here: 45.7 us
  starting transfers between devices  29.7 us (65%)
  Pallas kernels  8.59 us (19%)
  waiting for transfers between devices  6.77 us (15%)
  between operations  0.67 us (1%)
    all_to_all x1, starting transfers between devices, shards(): sums = lax.all_to_all(sums, ('dp', 'ha', 'wa'), 0, 0, tiled=True)  9.41 us
    pallas_call x4, Pallas kernels, call(): pl.pallas_call(kernel, out_shape=out_shape, scratch_shapes=list(scratch),...  7.45 us
    ppermute x4, starting transfers between devices, shards(): lax.ppermute(value, 'wa', [(i, i ^ 1) for i in range(WA)])  5.36 us
    ppermute x3, starting transfers between devices, shards(): lax.ppermute(blocks[hop], 'wa', [(i, (i + 2 * hop) % WA) for i in range(W...  4.88 us
    ppermute x1, waiting for transfers between devices, shards(): lax.ppermute(beside_other, 'wa', [(i, (i + 3 - 6 * (i % 2)) % WA) for i i...  2.74 us
    ppermute x1, starting transfers between devices, shards(): lax.ppermute(up, 'ha', [(i, (i + 1) % ha_count) for i in range(ha_count)])  2.54 us
    ppermute x1, starting transfers between devices, shards(): lax.ppermute(down, 'ha', [((i + 1) % ha_count, i) for i in range(ha_count)])  2.2 us
    ppermute x1, starting transfers between devices, shards(): lax.ppermute(beside, 'wa', [(i, (i + 2 - 4 * (i % 2)) % WA) for i in rang...  1.89 us
  transfers between devices with their start and end apart: 14, of which 6 were waited for; matrix products, arithmetic and copies ran while one was open for 0% of the time, Pallas kernels for 0%

profile of v5, /device:TPU:1, one launch (start us, length us, event | category | flops | bytes accessed | tf_op | source)
XLA Modules:
  0.0 45.7 jit_solution(7082086253576813226)
XLA Ops:
  0.6 1.1 %shard_map.84 = (bf16[5,24,128]{2,1,0:T(8,128)(2,1)S(1)}, bf16[5,24,128]{2,1,0:T(8,128)(2,1)S(1)}, bf16[17,24,128]{2,1,0:T(8,128)(2,1)S(1)}, f32[3,16,128]{2,1,0:T(8,128)S(1)}) custom-call(bf16[8,24,128]{2,1,0:T(8,128)(2,1)} %bitcast.9, bf16[8,24,128]{2,1,0:T(8,128)(2,1)} %bitcast.10, s32[8,24]{1,0:T(8,128)} %bitcast.12, s32[8,24]{1,0:T(8,128)} %bitcast.13, ...), custom_call_target="tpu_custom_call" | custom-call | tf_op jit(solution)/shard_map/pallas_call | solution.py:369
  1.8 2.5 %collective-permute-start = (bf16[5,24,128]{2,1,0:T(8,128)(2,1)S(1)}, bf16[5,24,128]{2,1,0:T(8,128)(2,1)S(1)}, u32[]{:S(2)}, u32[]{:S(2)}) collective-permute-start(bf16[5,24,128]{2,1,0:T(8,128)(2,1)S(1)} %get-tuple-element.23), channel_id=1, source_target_pairs={{0,8},{8,16},{16,24},{24,0},{1,9},{9,17},{17,25},{25,1},{2,10},{10... | collective-permute-start | bytes 92168 | tf_op jit(solution)/shard_map/ppermute | solution.py:383
  4.3 2.2 %collective-permute-start.1 = (bf16[5,24,128]{2,1,0:T(8,128)(2,1)S(1)}, bf16[5,24,128]{2,1,0:T(8,128)(2,1)S(1)}, u32[]{:S(2)}, u32[]{:S(2)}) collective-permute-start(bf16[5,24,128]{2,1,0:T(8,128)(2,1)S(1)} %get-tuple-element.24), channel_id=1, source_target_pairs={{8,0},{16,8},{24,16},{0,24},{9,1},{17,9},{25,17},{1,25},{10,2},{18... | collective-permute-start | bytes 92168 | tf_op jit(solution)/shard_map/ppermute | solution.py:384
  6.5 1.2 %collective-permute-done.prev_ref = bf16[5,24,128]{2,1,0:T(8,128)(2,1)S(1)} collective-permute-done((bf16[5,24,128]{2,1,0:T(8,128)(2,1)S(1)}, bf16[5,24,128]{2,1,0:T(8,128)(2,1)S(1)}, u32[]{:S(2)}, u32[]{:S(2)}) %collective-permute-start) | collective-permute-done | bytes 30752 | tf_op jit(solution)/shard_map/ppermute | solution.py:383
  7.8 1.3 %collective-permute-start.2 = (bf16[13,24,128]{2,1,0:T(8,128)(2,1)S(1)}, bf16[13,24,128]{2,1,0:T(8,128)(2,1)S(1)}, u32[]{:S(2)}, u32[]{:S(2)}) collective-permute-start(bf16[13,24,128]{2,1,0:T(8,128)(2,1)S(1)} %get-tuple-element.26), channel_id=1, source_target_pairs={{0,2},{1,3},{2,4},{3,5},{4,6},{5,7},{6,0},{7,1},{8,10},{9,11},{10,... | collective-permute-start | bytes 239624 | tf_op jit(solution)/shard_map/ppermute | solution.py:396
  9.1 2.5 %collective-permute-start.3 = (bf16[13,24,128]{2,1,0:T(8,128)(2,1)S(1)}, bf16[13,24,128]{2,1,0:T(8,128)(2,1)S(1)}, u32[]{:S(2)}, u32[]{:S(2)}) collective-permute-start(bf16[13,24,128]{2,1,0:T(8,128)(2,1)S(1)} %get-tuple-element.27), channel_id=1, source_target_pairs={{0,4},{1,5},{2,6},{3,7},{4,0},{5,1},{6,2},{7,3},{8,12},{9,13},{10,... | collective-permute-start | bytes 239624 | tf_op jit(solution)/shard_map/ppermute | solution.py:396
  11.5 1.2 %collective-permute-start.4 = (bf16[13,24,128]{2,1,0:T(8,128)(2,1)S(1)}, bf16[13,24,128]{2,1,0:T(8,128)(2,1)S(1)}, u32[]{:S(2)}, u32[]{:S(2)}) collective-permute-start(bf16[13,24,128]{2,1,0:T(8,128)(2,1)S(1)} %get-tuple-element.28), channel_id=1, source_target_pairs={{0,6},{1,7},{2,0},{3,1},{4,2},{5,3},{6,4},{7,5},{8,14},{9,15},{10,... | collective-permute-start | bytes 239624 | tf_op jit(solution)/shard_map/ppermute | solution.py:396
  12.7 2.4 %collective-permute-start.5 = (bf16[13,24,128]{2,1,0:T(8,128)(2,1)S(1)}, bf16[13,24,128]{2,1,0:T(8,128)(2,1)S(1)}, u32[]{:S(2)}, u32[]{:S(2)}) collective-permute-start(bf16[13,24,128]{2,1,0:T(8,128)(2,1)S(1)} %get-tuple-element.25.refs_0_), channel_id=1, source_target_pairs={{0,1},{1,0},{2,3},{3,2},{4,5},{5,4},{6,7},{7,6},{8,9},{9,8},{10,11... | collective-permute-start | bytes 239624 | tf_op jit(solution)/shard_map/ppermute | solution.py:397
  15.1 0.7 %collective-permute-start.6 = (bf16[13,24,128]{2,1,0:T(8,128)(2,1)S(1)}, bf16[13,24,128]{2,1,0:T(8,128)(2,1)S(1)}, u32[]{:S(2)}, u32[]{:S(2)}) collective-permute-start(bf16[13,24,128]{2,1,0:T(8,128)(2,1)S(1)} %collective-permute-done.2.refs_1_), channel_id=1, source_target_pairs={{0,1},{1,0},{2,3},{3,2},{4,5},{5,4},{6,7},{7,6},{8,9},{9,8},{10,11... | collective-permute-start | bytes 239624 | tf_op jit(solution)/shard_map/ppermute | solution.py:397
  15.7 0.0 collective-permute-done.3.refs_2_
  15.7 1.1 %collective-permute-start.7 = (bf16[13,24,128]{2,1,0:T(8,128)(2,1)S(1)}, bf16[13,24,128]{2,1,0:T(8,128)(2,1)S(1)}, u32[]{:S(2)}, u32[]{:S(2)}) collective-permute-start(bf16[13,24,128]{2,1,0:T(8,128)(2,1)S(1)} %collective-permute-done.3.refs_2_), channel_id=1, source_target_pairs={{0,1},{1,0},{2,3},{3,2},{4,5},{5,4},{6,7},{7,6},{8,9},{9,8},{10,11... | collective-permute-start | bytes 239624 | tf_op jit(solution)/shard_map/ppermute | solution.py:397
  16.9 1.2 %collective-permute-start.8 = (bf16[13,24,128]{2,1,0:T(8,128)(2,1)S(1)}, bf16[13,24,128]{2,1,0:T(8,128)(2,1)S(1)}, u32[]{:S(2)}, u32[]{:S(2)}) collective-permute-start(bf16[13,24,128]{2,1,0:T(8,128)(2,1)S(1)} %collective-permute-done.4.refs_3_), channel_id=1, source_target_pairs={{0,1},{1,0},{2,3},{3,2},{4,5},{5,4},{6,7},{7,6},{8,9},{9,8},{10,11... | collective-permute-start | bytes 239624 | tf_op jit(solution)/shard_map/ppermute | solution.py:397
  18.1 0.9 %collective-permute-done.8.refs_7_ = bf16[13,24,128]{2,1,0:T(8,128)(2,1)S(1)} collective-permute-done((bf16[13,24,128]{2,1,0:T(8,128)(2,1)S(1)}, bf16[13,24,128]{2,1,0:T(8,128)(2,1)S(1)}, u32[]{:S(2)}, u32[]{:S(2)}) %collective-permute-start.8) | collective-permute-done | bytes 79904 | tf_op jit(solution)/shard_map/ppermute | solution.py:397
  19.0 6.5 %shard_map.86 = (f32[128,2,128]{2,1,0:T(2,128)}, bf16[8,24,128]{2,1,0:T(8,128)(2,1)S(1)}, bf16[8,24,128]{2,1,0:T(8,128)(2,1)S(1)}) custom-call(bf16[13,24,128]{2,1,0:T(8,128)(2,1)S(1)} %get-tuple-element.25.refs_0_, bf16[13,24,128]{2,1,0:T(8,128)(2,1)S(1)} %collective-permute-done.2.refs_1_, bf16[13,24,128]{2,1,0:T(8,128)(2,1)S(1)} %collective-permute-done.3.refs_2_, ...), custom_call_target="tpu_custom_call" | custom-call | flops 5368709120 | bytes 1048576 | tf_op jit(solution)/shard_map/pallas_call | solution.py:353
  25.5 9.4 %all-to-all-start = ((f32[128,2,128]{2,1,0:T(2,128)}), f32[128,2,128]{2,1,0:T(2,128)S(1)}, u32[]{:S(2)}, u32[]{:S(2)}) async-start(f32[128,2,128]{2,1,0:T(2,128)} %get-tuple-element.35), calls=%async_computation | async-start | bytes 262144 | tf_op jit(solution)/shard_map/all_to_all | solution.py:423
  34.9 1.1 %collective-permute-start.9 = (bf16[8,24,128]{2,1,0:T(8,128)(2,1)S(1)}, bf16[8,24,128]{2,1,0:T(8,128)(2,1)S(1)}, u32[]{:S(2)}, u32[]{:S(2)}) collective-permute-start(bf16[8,24,128]{2,1,0:T(8,128)(2,1)S(1)} %get-tuple-element.31), channel_id=1, source_target_pairs={{0,1},{1,0},{2,3},{3,2},{4,5},{5,4},{6,7},{7,6},{8,9},{9,8},{10,11... | collective-permute-start | bytes 147464 | tf_op jit(solution)/shard_map/ppermute | solution.py:359
  36.0 0.9 %collective-permute-done.9.got_ref.got = bf16[8,24,128]{2,1,0:T(8,128)(2,1)S(1)} collective-permute-done((bf16[8,24,128]{2,1,0:T(8,128)(2,1)S(1)}, bf16[8,24,128]{2,1,0:T(8,128)(2,1)S(1)}, u32[]{:S(2)}, u32[]{:S(2)}) %collective-permute-start.9) | collective-permute-done | bytes 49184 | tf_op jit(solution)/shard_map/ppermute | solution.py:359
  36.9 1.9 %collective-permute-start.10 = (bf16[4,24,128]{2,1,0:T(8,128)(2,1)S(1)}, bf16[4,24,128]{2,1,0:T(8,128)(2,1)S(1)}, u32[]{:S(2)}, u32[]{:S(2)}) collective-permute-start(bf16[4,24,128]{2,1,0:T(8,128)(2,1)S(1)} %get-tuple-element.32), channel_id=1, source_target_pairs={{0,2},{1,7},{2,4},{3,1},{4,6},{5,3},{6,0},{7,5},{8,10},{9,15},{10,... | collective-permute-start | bytes 73736 | tf_op jit(solution)/shard_map/ppermute | solution.py:428
  38.8 1.3 %collective-permute-start.11 = (bf16[4,24,128]{2,1,0:T(8,128)(2,1)S(1)}, bf16[4,24,128]{2,1,0:T(8,128)(2,1)S(1)}, u32[]{:S(2)}, u32[]{:S(2)}) collective-permute-start(bf16[4,24,128]{2,1,0:T(8,128)(2,1)S(1)} %get-tuple-element.33), channel_id=1, source_target_pairs={{0,3},{1,6},{2,5},{3,0},{4,7},{5,2},{6,1},{7,4},{8,11},{9,14},{10,... | collective-permute-start | bytes 73736 | tf_op jit(solution)/shard_map/ppermute | solution.py:429
  40.1 1.0 %collective-permute-start.12 = (bf16[4,24,128]{2,1,0:T(8,128)(2,1)S(1)}, bf16[4,24,128]{2,1,0:T(8,128)(2,1)S(1)}, u32[]{:S(2)}, u32[]{:S(2)}) collective-permute-start(bf16[4,24,128]{2,1,0:T(8,128)(2,1)S(1)} %get-tuple-element.34), channel_id=1, source_target_pairs={{0,4},{1,5},{2,6},{3,7},{4,0},{5,1},{6,2},{7,3},{8,12},{9,13},{10,... | collective-permute-start | bytes 73736 | tf_op jit(solution)/shard_map/ppermute | solution.py:427
  41.1 2.7 %collective-permute-done.11.far = bf16[4,24,128]{2,1,0:T(8,128)(2,1)S(1)} collective-permute-done((bf16[4,24,128]{2,1,0:T(8,128)(2,1)S(1)}, bf16[4,24,128]{2,1,0:T(8,128)(2,1)S(1)}, u32[]{:S(2)}, u32[]{:S(2)}) %collective-permute-start.11) | collective-permute-done | bytes 24608 | tf_op jit(solution)/shard_map/ppermute | solution.py:429
  43.8 0.8 %collective-permute-done.12.across = bf16[4,24,128]{2,1,0:T(8,128)(2,1)S(1)} collective-permute-done((bf16[4,24,128]{2,1,0:T(8,128)(2,1)S(1)}, bf16[4,24,128]{2,1,0:T(8,128)(2,1)S(1)}, u32[]{:S(2)}, u32[]{:S(2)}) %collective-permute-start.12) | collective-permute-done | bytes 24608 | tf_op jit(solution)/shard_map/ppermute | solution.py:427
  44.6 0.3 all-to-all-done.sums_ref
  44.8 0.9 %shard_map.88 = (f32[8,24,128]{2,1,0:T(8,128)}, f32[8,24,128]{2,1,0:T(8,128)}, f32[3,3,3,8]{3,2,1,0:T(4,128)}, f32[1,1]{1,0:T(1,128)}) custom-call(bf16[8,24,128]{2,1,0:T(8,128)(2,1)S(1)} %get-tuple-element.30.kept_ref.kept, bf16[8,24,128]{2,1,0:T(8,128)(2,1)S(1)} %collective-permute-done.9.got_ref.got, ...), custom_call_target="tpu_custom_call" | custom-call | bytes 1048576 | tf_op jit(solution)/shard_map/pallas_call | solution.py:353
  (9 shorter events, 0.1 us)
Async XLA Ops:
  1.8 5.9 %collective-permute-start = (bf16[5,24,128]{2,1,0:T(8,128)(2,1)S(1)}, bf16[5,24,128]{2,1,0:T(8,128)(2,1)S(1)}, u32[]{:S(2)}, u32[]{:S(2)}) collective-permute-start(bf16[5,24,128]{2,1,0:T(8,128)(2,1)S(1)} %get-tuple-element.23), channel_id=1, source_target_pairs={{0,8},{8,16},{16,24},{24,0},{1,9},{9,17},{17,25},{25,1},{2,10},{10... | collective-permute-start | bytes 92168 | tf_op jit(solution)/shard_map/ppermute | solution.py:383
  4.3 3.4 %collective-permute-start.1 = (bf16[5,24,128]{2,1,0:T(8,128)(2,1)S(1)}, bf16[5,24,128]{2,1,0:T(8,128)(2,1)S(1)}, u32[]{:S(2)}, u32[]{:S(2)}) collective-permute-start(bf16[5,24,128]{2,1,0:T(8,128)(2,1)S(1)} %get-tuple-element.24), channel_id=1, source_target_pairs={{8,0},{16,8},{24,16},{0,24},{9,1},{17,9},{25,17},{1,25},{10,2},{18... | collective-permute-start | bytes 92168 | tf_op jit(solution)/shard_map/ppermute | solution.py:384
  7.8 7.3 %collective-permute-start.2 = (bf16[13,24,128]{2,1,0:T(8,128)(2,1)S(1)}, bf16[13,24,128]{2,1,0:T(8,128)(2,1)S(1)}, u32[]{:S(2)}, u32[]{:S(2)}) collective-permute-start(bf16[13,24,128]{2,1,0:T(8,128)(2,1)S(1)} %get-tuple-element.26), channel_id=1, source_target_pairs={{0,2},{1,3},{2,4},{3,5},{4,6},{5,7},{6,0},{7,1},{8,10},{9,11},{10,... | collective-permute-start | bytes 239624 | tf_op jit(solution)/shard_map/ppermute | solution.py:396
  9.1 6.7 %collective-permute-start.3 = (bf16[13,24,128]{2,1,0:T(8,128)(2,1)S(1)}, bf16[13,24,128]{2,1,0:T(8,128)(2,1)S(1)}, u32[]{:S(2)}, u32[]{:S(2)}) collective-permute-start(bf16[13,24,128]{2,1,0:T(8,128)(2,1)S(1)} %get-tuple-element.27), channel_id=1, source_target_pairs={{0,4},{1,5},{2,6},{3,7},{4,0},{5,1},{6,2},{7,3},{8,12},{9,13},{10,... | collective-permute-start | bytes 239624 | tf_op jit(solution)/shard_map/ppermute | solution.py:396
  11.5 5.4 %collective-permute-start.4 = (bf16[13,24,128]{2,1,0:T(8,128)(2,1)S(1)}, bf16[13,24,128]{2,1,0:T(8,128)(2,1)S(1)}, u32[]{:S(2)}, u32[]{:S(2)}) collective-permute-start(bf16[13,24,128]{2,1,0:T(8,128)(2,1)S(1)} %get-tuple-element.28), channel_id=1, source_target_pairs={{0,6},{1,7},{2,0},{3,1},{4,2},{5,3},{6,4},{7,5},{8,14},{9,15},{10,... | collective-permute-start | bytes 239624 | tf_op jit(solution)/shard_map/ppermute | solution.py:396
  12.7 5.4 %collective-permute-start.5 = (bf16[13,24,128]{2,1,0:T(8,128)(2,1)S(1)}, bf16[13,24,128]{2,1,0:T(8,128)(2,1)S(1)}, u32[]{:S(2)}, u32[]{:S(2)}) collective-permute-start(bf16[13,24,128]{2,1,0:T(8,128)(2,1)S(1)} %get-tuple-element.25.refs_0_), channel_id=1, source_target_pairs={{0,1},{1,0},{2,3},{3,2},{4,5},{5,4},{6,7},{7,6},{8,9},{9,8},{10,11... | collective-permute-start | bytes 239624 | tf_op jit(solution)/shard_map/ppermute | solution.py:397
  15.1 3.0 %collective-permute-start.6 = (bf16[13,24,128]{2,1,0:T(8,128)(2,1)S(1)}, bf16[13,24,128]{2,1,0:T(8,128)(2,1)S(1)}, u32[]{:S(2)}, u32[]{:S(2)}) collective-permute-start(bf16[13,24,128]{2,1,0:T(8,128)(2,1)S(1)} %collective-permute-done.2.refs_1_), channel_id=1, source_target_pairs={{0,1},{1,0},{2,3},{3,2},{4,5},{5,4},{6,7},{7,6},{8,9},{9,8},{10,11... | collective-permute-start | bytes 239624 | tf_op jit(solution)/shard_map/ppermute | solution.py:397
  15.7 2.3 %collective-permute-start.7 = (bf16[13,24,128]{2,1,0:T(8,128)(2,1)S(1)}, bf16[13,24,128]{2,1,0:T(8,128)(2,1)S(1)}, u32[]{:S(2)}, u32[]{:S(2)}) collective-permute-start(bf16[13,24,128]{2,1,0:T(8,128)(2,1)S(1)} %collective-permute-done.3.refs_2_), channel_id=1, source_target_pairs={{0,1},{1,0},{2,3},{3,2},{4,5},{5,4},{6,7},{7,6},{8,9},{9,8},{10,11... | collective-permute-start | bytes 239624 | tf_op jit(solution)/shard_map/ppermute | solution.py:397
  16.9 2.1 %collective-permute-start.8 = (bf16[13,24,128]{2,1,0:T(8,128)(2,1)S(1)}, bf16[13,24,128]{2,1,0:T(8,128)(2,1)S(1)}, u32[]{:S(2)}, u32[]{:S(2)}) collective-permute-start(bf16[13,24,128]{2,1,0:T(8,128)(2,1)S(1)} %collective-permute-done.4.refs_3_), channel_id=1, source_target_pairs={{0,1},{1,0},{2,3},{3,2},{4,5},{5,4},{6,7},{7,6},{8,9},{9,8},{10,11... | collective-permute-start | bytes 239624 | tf_op jit(solution)/shard_map/ppermute | solution.py:397
  25.5 19.4 %all-to-all-start = ((f32[128,2,128]{2,1,0:T(2,128)}), f32[128,2,128]{2,1,0:T(2,128)S(1)}, u32[]{:S(2)}, u32[]{:S(2)}) async-start(f32[128,2,128]{2,1,0:T(2,128)} %get-tuple-element.35), calls=%async_computation | async-start | bytes 262144 | tf_op jit(solution)/shard_map/all_to_all | solution.py:423
  34.9 2.0 %collective-permute-start.9 = (bf16[8,24,128]{2,1,0:T(8,128)(2,1)S(1)}, bf16[8,24,128]{2,1,0:T(8,128)(2,1)S(1)}, u32[]{:S(2)}, u32[]{:S(2)}) collective-permute-start(bf16[8,24,128]{2,1,0:T(8,128)(2,1)S(1)} %get-tuple-element.31), channel_id=1, source_target_pairs={{0,1},{1,0},{2,3},{3,2},{4,5},{5,4},{6,7},{7,6},{8,9},{9,8},{10,11... | collective-permute-start | bytes 147464 | tf_op jit(solution)/shard_map/ppermute | solution.py:359
  36.9 4.2 %collective-permute-start.10 = (bf16[4,24,128]{2,1,0:T(8,128)(2,1)S(1)}, bf16[4,24,128]{2,1,0:T(8,128)(2,1)S(1)}, u32[]{:S(2)}, u32[]{:S(2)}) collective-permute-start(bf16[4,24,128]{2,1,0:T(8,128)(2,1)S(1)} %get-tuple-element.32), channel_id=1, source_target_pairs={{0,2},{1,7},{2,4},{3,1},{4,6},{5,3},{6,0},{7,5},{8,10},{9,15},{10,... | collective-permute-start | bytes 73736 | tf_op jit(solution)/shard_map/ppermute | solution.py:428
  38.8 5.0 %collective-permute-start.11 = (bf16[4,24,128]{2,1,0:T(8,128)(2,1)S(1)}, bf16[4,24,128]{2,1,0:T(8,128)(2,1)S(1)}, u32[]{:S(2)}, u32[]{:S(2)}) collective-permute-start(bf16[4,24,128]{2,1,0:T(8,128)(2,1)S(1)} %get-tuple-element.33), channel_id=1, source_target_pairs={{0,3},{1,6},{2,5},{3,0},{4,7},{5,2},{6,1},{7,4},{8,11},{9,14},{10,... | collective-permute-start | bytes 73736 | tf_op jit(solution)/shard_map/ppermute | solution.py:429
  40.1 4.5 %collective-permute-start.12 = (bf16[4,24,128]{2,1,0:T(8,128)(2,1)S(1)}, bf16[4,24,128]{2,1,0:T(8,128)(2,1)S(1)}, u32[]{:S(2)}, u32[]{:S(2)}) collective-permute-start(bf16[4,24,128]{2,1,0:T(8,128)(2,1)S(1)} %get-tuple-element.34), channel_id=1, source_target_pairs={{0,4},{1,5},{2,6},{3,7},{4,0},{5,1},{6,2},{7,3},{8,12},{9,13},{10,... | collective-permute-start | bytes 73736 | tf_op jit(solution)/shard_map/ppermute | solution.py:427

commit v6 on v5

--- a/solution.py
+++ b/solution.py
@@ -1,3 +1,5 @@
+import functools
+
 import jax
 import jax.numpy as jnp
 from jax import lax
@@ -206,7 +208,7 @@
 def main_kernel(*refs):
     recv, wc_ref = refs[:8], refs[8]
     sums_ref, kept_ref, given_ref = refs[9:12]
-    ls, rs, rb, ms, ab, acc, ub, diags, ks, lb, xs, ys, out_ref = refs[12:]
+    ls, rs, rb, ms, ab, acc, ub, diags, ks, lb, xs, ys, out_ref, fanned, sem = refs[12:]
     fill_meta(fill(recv, 0, 5, ls, rs, rb), ms)
     ks[...] = jnp.zeros(ks.shape, F32)
     xs[...] = jnp.zeros(xs.shape, F32)
@@ -254,16 +256,6 @@
                 total = term if total is None else total + term
         xs[b, 8 : 8 + WT] = total
         xs[3 + b, 8 : 8 + WT] = spread * own_left
-    for q in range(3):
-        terms = dot(ub[2 * WT * q : 2 * WT * (q + 1)], lb[...], TN)
-        for si in range(5):
-            total = None
-            for b in range(3):
-                e = b - (si - 2)
-                if 0 <= e <= 2:
-                    term = tap(q, b, e) * terms[:, b * CH : (b + 1) * CH]
-                    total = term if total is None else total + term
-            ys[si] = total if q == 0 else ys[si] + total
     channel = lax.broadcasted_iota(jnp.int32, (8, CH), 1)
     member = group_member().astype(BF16)
     parts = [dot(member, part, NT) for part in split3(ks[...])]
@@ -277,7 +269,19 @@
         placed = placed + jnp.where(quarter == i, pltpu.roll(sums, SHARE * i, 1), 0.0)
     packed = jnp.concatenate([jnp.sum(placed[4 * i : 4 * i + 4], axis=0, keepdims=True) for i in range(2)], axis=0)
     for i in range(sums_ref.shape[0]):
-        sums_ref[i] = packed
+        fanned[i] = packed
+    sending = pltpu.make_async_copy(fanned, sums_ref, sem)
+    sending.start()
+    for q in range(3):
+        terms = dot(ub[2 * WT * q : 2 * WT * (q + 1)], lb[...], TN)
+        for si in range(5):
+            total = None
+            for b in range(3):
+                e = b - (si - 2)
+                if 0 <= e <= 2:
+                    term = tap(q, b, e) * terms[:, b * CH : (b + 1) * CH]
+                    total = term if total is None else total + term
+            ys[si] = total if q == 0 else ys[si] + total
     grad_left = xs[0, 9 : 9 + WT] + xs[1, 8 : 8 + WT] + xs[2, 7 : 7 + WT]
     grad_right = ys[0, 4 : 4 + WT]
     for si in range(1, 5):
@@ -295,6 +299,7 @@
         for i, tile in enumerate(places):
             for side in range(2):
                 ref[2 * i + side] = out_ref[tile, side]
+    sending.wait()
 
 
 def ahead(core):
@@ -305,8 +310,8 @@
     return (chip + step + CHIPS) & (CHIPS - 1)
 
 
-def pack_back_kernel(kept_ref, got_ref, *outs):
-    for place, out_ref in zip((2, 0, 1), outs):
+def pack_back_kernel(places, kept_ref, got_ref, *refs):
+    for place, out_ref in zip(places, refs[-len(places) :]):
         for row, ref in enumerate((kept_ref, got_ref)):
             for side in range(2):
                 out_ref[2 * row + side] = ref[2 * place + side]
@@ -398,12 +403,11 @@
     tiles = same_core + other_core
     others = lax.axis_size("dp") * ha_count * WA
     half = jax.ShapeDtypeStruct((8, TILE, CH), BF16)
-    sums, kept, given = call(
+    sums, kept, given = pl.pallas_call(
         main_kernel,
-        (jax.ShapeDtypeStruct((others, 2, CH), F32), half, half),
-        *tiles,
-        taps,
-        scratch=(
+        out_shape=(jax.ShapeDtypeStruct((others, 2, CH), F32), half, half),
+        out_specs=(pl.BlockSpec(memory_space=pltpu.HBM), pl.BlockSpec(memory_space=pltpu.VMEM), pl.BlockSpec(memory_space=pltpu.VMEM)),
+        scratch_shapes=(
             pltpu.VMEM((5, WT + 16, CH), F32),
             pltpu.VMEM((5, WT + 80, CH), F32),
             pltpu.VMEM((JP, 25 * CH), BF16),
@@ -417,14 +421,20 @@
             pltpu.VMEM((6, WT + 16, CH), F32),
             pltpu.VMEM((5, JP, CH), F32),
             pltpu.VMEM((WA, 2, TILE, CH), BF16),
+            pltpu.VMEM((others, 2, CH), F32),
+            pltpu.SemaphoreType.DMA,
         ),
-        flops=5 << 30,
-    )
+        compiler_params=VMEM,
+        cost_estimate=pl.CostEstimate(flops=5 << 30, bytes_accessed=1 << 20, transcendentals=0),
+    )(*tiles, taps)
     sums = lax.all_to_all(sums, ("dp", "ha", "wa"), 0, 0, tiled=True)
     got = swapped(given)
     block = jax.ShapeDtypeStruct((4, TILE, CH), BF16)
-    opposite, beside, beside_other = call(pack_back_kernel, (block,) * 3, kept, got)
+    (opposite,) = call(functools.partial(pack_back_kernel, (2,)), (block,), kept, got)
     across = lax.ppermute(opposite, "wa", [(i, (i + 4) % WA) for i in range(WA)])
+    beside, beside_other = call(
+        functools.partial(pack_back_kernel, (0, 1)), (block,) * 2, kept, got, opposite, flops=1 << 31
+    )
     near = lax.ppermute(beside, "wa", [(i, (i + 2 - 4 * (i % 2)) % WA) for i in range(WA)])
     far = lax.ppermute(beside_other, "wa", [(i, (i + 3 - 6 * (i % 2)) % WA) for i in range(WA)])
     tile = jax.ShapeDtypeStruct((ROWS, TILE, CH), F32)

time: 45.9 us -> 45.7 us (level)
  starting transfers between devices: 29.7 us -> 31.1 us
  waiting for transfers between devices: 6.77 us -> 5.72 us
  Pallas kernels: 8.59 us -> 8.02 us
    pallas_call x4, Pallas kernels: 7.45 us -> 0.96 us  [call(): pl.pallas_call(kernel, out_shape=out_shape, scratch_shapes=list(scratch),...]
    pallas_call x0 -> x1, Pallas kernels: none -> 5.92 us  [shards(): pl.pallas_call(main_kernel, out_shape=(jax.ShapeDtypeStruct((others, 2, C...]
    ppermute x1, starting transfers between devices: 0.97 us -> 2.97 us  [shards(): lax.ppermute(opposite, 'wa', [(i, (i + 4) % WA) for i in range(WA)])]
    ppermute x1, starting transfers between devices: 1.3 us -> 2.6 us  [shards(): lax.ppermute(beside_other, 'wa', [(i, (i + 3 - 6 * (i % 2)) % WA) for i i...]
    all_to_all x1, waiting for transfers between devices: 0.26 us -> 1.43 us  [shards(): sums = lax.all_to_all(sums, ('dp', 'ha', 'wa'), 0, 0, tiled=True)]
    ppermute x1, starting transfers between devices: 1.89 us -> 0.89 us  [shards(): lax.ppermute(beside, 'wa', [(i, (i + 2 - 4 * (i % 2)) % WA) for i in rang...]
    ppermute x1, waiting for transfers between devices: 0.88 us -> 0.01 us  [swapped(): return lax.ppermute(value, 'wa', [(i, i ^ 1) for i in range(WA)])]
    ppermute x1, waiting for transfers between devices: 0.76 us -> 0.01 us  [shards(): lax.ppermute(opposite, 'wa', [(i, (i + 4) % WA) for i in range(WA)])]
  transfers between devices with their start and end apart: 14 -> 14, of which waited for: 6 -> 4; matrix products, arithmetic and copies ran while one was open for 0% -> 0% of each run, Pallas kernels for 0% -> 0%
where the time goes in v6:
time: 45.7 us; the launch traced here: 45.5 us
  starting transfers between devices  31.1 us (68%)
  Pallas kernels  8.02 us (18%)
  waiting for transfers between devices  5.72 us (13%)
  between operations  0.69 us (2%)
    all_to_all x1, starting transfers between devices, shards(): sums = lax.all_to_all(sums, ('dp', 'ha', 'wa'), 0, 0, tiled=True)  9.22 us
    pallas_call x1, Pallas kernels, shards(): pl.pallas_call(main_kernel, out_shape=(jax.ShapeDtypeStruct((others, 2, C...  5.92 us
    ppermute x4, starting transfers between devices, shards(): lax.ppermute(value, 'wa', [(i, i ^ 1) for i in range(WA)])  5.36 us
    ppermute x3, starting transfers between devices, shards(): lax.ppermute(blocks[hop], 'wa', [(i, (i + 2 * hop) % WA) for i in range(W...  4.88 us
    ppermute x1, starting transfers between devices, shards(): lax.ppermute(opposite, 'wa', [(i, (i + 4) % WA) for i in range(WA)])  2.97 us
    ppermute x1, starting transfers between devices, shards(): lax.ppermute(beside_other, 'wa', [(i, (i + 3 - 6 * (i % 2)) % WA) for i i...  2.6 us
    ppermute x1, starting transfers between devices, shards(): lax.ppermute(up, 'ha', [(i, (i + 1) % ha_count) for i in range(ha_count)])  2.54 us
    ppermute x1, starting transfers between devices, shards(): lax.ppermute(down, 'ha', [((i + 1) % ha_count, i) for i in range(ha_count)])  2.2 us
  transfers between devices with their start and end apart: 14, of which 4 were waited for; matrix products, arithmetic and copies ran while one was open for 0% of the time, Pallas kernels for 0%

profile of v6, /device:TPU:1, one launch (start us, length us, event | category | flops | bytes accessed | tf_op | source)
XLA Modules:
  0.0 45.5 jit_solution(14306219603515814274)
XLA Ops:
  0.6 1.1 %shard_map.84 = (bf16[5,24,128]{2,1,0:T(8,128)(2,1)S(1)}, bf16[5,24,128]{2,1,0:T(8,128)(2,1)S(1)}, bf16[17,24,128]{2,1,0:T(8,128)(2,1)S(1)}, f32[3,16,128]{2,1,0:T(8,128)S(1)}) custom-call(bf16[8,24,128]{2,1,0:T(8,128)(2,1)} %bitcast.9, bf16[8,24,128]{2,1,0:T(8,128)(2,1)} %bitcast.10, s32[8,24]{1,0:T(8,128)} %bitcast.12, s32[8,24]{1,0:T(8,128)} %bitcast.13, ...), custom_call_target="tpu_custom_call" | custom-call | tf_op jit(solution)/shard_map/pallas_call | solution.py:374
  1.8 2.5 %collective-permute-start = (bf16[5,24,128]{2,1,0:T(8,128)(2,1)S(1)}, bf16[5,24,128]{2,1,0:T(8,128)(2,1)S(1)}, u32[]{:S(2)}, u32[]{:S(2)}) collective-permute-start(bf16[5,24,128]{2,1,0:T(8,128)(2,1)S(1)} %get-tuple-element.22), channel_id=1, source_target_pairs={{0,8},{8,16},{16,24},{24,0},{1,9},{9,17},{17,25},{25,1},{2,10},{10... | collective-permute-start | bytes 92168 | tf_op jit(solution)/shard_map/ppermute | solution.py:388
  4.3 2.2 %collective-permute-start.1 = (bf16[5,24,128]{2,1,0:T(8,128)(2,1)S(1)}, bf16[5,24,128]{2,1,0:T(8,128)(2,1)S(1)}, u32[]{:S(2)}, u32[]{:S(2)}) collective-permute-start(bf16[5,24,128]{2,1,0:T(8,128)(2,1)S(1)} %get-tuple-element.23), channel_id=1, source_target_pairs={{8,0},{16,8},{24,16},{0,24},{9,1},{17,9},{25,17},{1,25},{10,2},{18... | collective-permute-start | bytes 92168 | tf_op jit(solution)/shard_map/ppermute | solution.py:389
  6.5 1.2 %collective-permute-done.prev_ref = bf16[5,24,128]{2,1,0:T(8,128)(2,1)S(1)} collective-permute-done((bf16[5,24,128]{2,1,0:T(8,128)(2,1)S(1)}, bf16[5,24,128]{2,1,0:T(8,128)(2,1)S(1)}, u32[]{:S(2)}, u32[]{:S(2)}) %collective-permute-start) | collective-permute-done | bytes 30752 | tf_op jit(solution)/shard_map/ppermute | solution.py:388
  7.8 1.3 %collective-permute-start.2 = (bf16[13,24,128]{2,1,0:T(8,128)(2,1)S(1)}, bf16[13,24,128]{2,1,0:T(8,128)(2,1)S(1)}, u32[]{:S(2)}, u32[]{:S(2)}) collective-permute-start(bf16[13,24,128]{2,1,0:T(8,128)(2,1)S(1)} %get-tuple-element.25), channel_id=1, source_target_pairs={{0,2},{1,3},{2,4},{3,5},{4,6},{5,7},{6,0},{7,1},{8,10},{9,11},{10,... | collective-permute-start | bytes 239624 | tf_op jit(solution)/shard_map/ppermute | solution.py:401
  9.1 2.5 %collective-permute-start.3 = (bf16[13,24,128]{2,1,0:T(8,128)(2,1)S(1)}, bf16[13,24,128]{2,1,0:T(8,128)(2,1)S(1)}, u32[]{:S(2)}, u32[]{:S(2)}) collective-permute-start(bf16[13,24,128]{2,1,0:T(8,128)(2,1)S(1)} %get-tuple-element.26), channel_id=1, source_target_pairs={{0,4},{1,5},{2,6},{3,7},{4,0},{5,1},{6,2},{7,3},{8,12},{9,13},{10,... | collective-permute-start | bytes 239624 | tf_op jit(solution)/shard_map/ppermute | solution.py:401
  11.5 1.2 %collective-permute-start.4 = (bf16[13,24,128]{2,1,0:T(8,128)(2,1)S(1)}, bf16[13,24,128]{2,1,0:T(8,128)(2,1)S(1)}, u32[]{:S(2)}, u32[]{:S(2)}) collective-permute-start(bf16[13,24,128]{2,1,0:T(8,128)(2,1)S(1)} %get-tuple-element.27), channel_id=1, source_target_pairs={{0,6},{1,7},{2,0},{3,1},{4,2},{5,3},{6,4},{7,5},{8,14},{9,15},{10,... | collective-permute-start | bytes 239624 | tf_op jit(solution)/shard_map/ppermute | solution.py:401
  12.7 2.4 %collective-permute-start.5 = (bf16[13,24,128]{2,1,0:T(8,128)(2,1)S(1)}, bf16[13,24,128]{2,1,0:T(8,128)(2,1)S(1)}, u32[]{:S(2)}, u32[]{:S(2)}) collective-permute-start(bf16[13,24,128]{2,1,0:T(8,128)(2,1)S(1)} %get-tuple-element.24.refs_0_), channel_id=1, source_target_pairs={{0,1},{1,0},{2,3},{3,2},{4,5},{5,4},{6,7},{7,6},{8,9},{9,8},{10,11... | collective-permute-start | bytes 239624 | tf_op jit(solution)/shard_map/ppermute | solution.py:402
  15.1 0.7 %collective-permute-start.6 = (bf16[13,24,128]{2,1,0:T(8,128)(2,1)S(1)}, bf16[13,24,128]{2,1,0:T(8,128)(2,1)S(1)}, u32[]{:S(2)}, u32[]{:S(2)}) collective-permute-start(bf16[13,24,128]{2,1,0:T(8,128)(2,1)S(1)} %collective-permute-done.2.refs_1_), channel_id=1, source_target_pairs={{0,1},{1,0},{2,3},{3,2},{4,5},{5,4},{6,7},{7,6},{8,9},{9,8},{10,11... | collective-permute-start | bytes 239624 | tf_op jit(solution)/shard_map/ppermute | solution.py:402
  15.7 0.0 collective-permute-done.3.refs_2_
  15.7 1.1 %collective-permute-start.7 = (bf16[13,24,128]{2,1,0:T(8,128)(2,1)S(1)}, bf16[13,24,128]{2,1,0:T(8,128)(2,1)S(1)}, u32[]{:S(2)}, u32[]{:S(2)}) collective-permute-start(bf16[13,24,128]{2,1,0:T(8,128)(2,1)S(1)} %collective-permute-done.3.refs_2_), channel_id=1, source_target_pairs={{0,1},{1,0},{2,3},{3,2},{4,5},{5,4},{6,7},{7,6},{8,9},{9,8},{10,11... | collective-permute-start | bytes 239624 | tf_op jit(solution)/shard_map/ppermute | solution.py:402
  16.9 1.2 %collective-permute-start.8 = (bf16[13,24,128]{2,1,0:T(8,128)(2,1)S(1)}, bf16[13,24,128]{2,1,0:T(8,128)(2,1)S(1)}, u32[]{:S(2)}, u32[]{:S(2)}) collective-permute-start(bf16[13,24,128]{2,1,0:T(8,128)(2,1)S(1)} %collective-permute-done.4.refs_3_), channel_id=1, source_target_pairs={{0,1},{1,0},{2,3},{3,2},{4,5},{5,4},{6,7},{7,6},{8,9},{9,8},{10,11... | collective-permute-start | bytes 239624 | tf_op jit(solution)/shard_map/ppermute | solution.py:402
  18.0 0.0 collective-permute-done.5.refs_4_
  18.0 0.0 collective-permute-done.6.refs_5_
  18.1 0.9 %collective-permute-done.8.refs_7_ = bf16[13,24,128]{2,1,0:T(8,128)(2,1)S(1)} collective-permute-done((bf16[13,24,128]{2,1,0:T(8,128)(2,1)S(1)}, bf16[13,24,128]{2,1,0:T(8,128)(2,1)S(1)}, u32[]{:S(2)}, u32[]{:S(2)}) %collective-permute-start.8) | collective-permute-done | bytes 79904 | tf_op jit(solution)/shard_map/ppermute | solution.py:402
  19.0 5.9 %shard_map.86 = (f32[128,2,128]{2,1,0:T(2,128)}, bf16[8,24,128]{2,1,0:T(8,128)(2,1)S(1)}, bf16[8,24,128]{2,1,0:T(8,128)(2,1)S(1)}) custom-call(bf16[13,24,128]{2,1,0:T(8,128)(2,1)S(1)} %get-tuple-element.24.refs_0_, bf16[13,24,128]{2,1,0:T(8,128)(2,1)S(1)} %collective-permute-done.2.refs_1_, bf16[13,24,128]{2,1,0:T(8,128)(2,1)S(1)} %collective-permute-done.3.refs_2_, ...), custom_call_target="tpu_custom_call" | custom-call | flops 5368709120 | bytes 1048576 | tf_op jit(solution)/shard_map/pallas_call | solution.py:406
  24.9 0.4 collective-permute-start.9
  25.3 9.2 %all-to-all-start = ((f32[128,2,128]{2,1,0:T(2,128)}), f32[128,2,128]{2,1,0:T(2,128)S(1)}, u32[]{:S(2)}, u32[]{:S(2)}) async-start(f32[128,2,128]{2,1,0:T(2,128)} %get-tuple-element.33), calls=%async_computation | async-start | bytes 262144 | tf_op jit(solution)/shard_map/all_to_all | solution.py:430
  34.6 3.0 %collective-permute-start.12 = (bf16[4,24,128]{2,1,0:T(8,128)(2,1)S(1)}, bf16[4,24,128]{2,1,0:T(8,128)(2,1)S(1)}, u32[]{:S(2)}, u32[]{:S(2)}) collective-permute-start(bf16[4,24,128]{2,1,0:T(8,128)(2,1)S(1)} %shard_map.87.refs_0_), channel_id=1, source_target_pairs={{0,4},{1,5},{2,6},{3,7},{4,0},{5,1},{6,2},{7,3},{8,12},{9,13},{10,... | collective-permute-start | bytes 73736 | tf_op jit(solution)/shard_map/ppermute | solution.py:434
  37.5 0.9 %collective-permute-start.10 = (bf16[4,24,128]{2,1,0:T(8,128)(2,1)S(1)}, bf16[4,24,128]{2,1,0:T(8,128)(2,1)S(1)}, u32[]{:S(2)}, u32[]{:S(2)}) collective-permute-start(bf16[4,24,128]{2,1,0:T(8,128)(2,1)S(1)} %get-tuple-element.31), channel_id=1, source_target_pairs={{0,2},{1,7},{2,4},{3,1},{4,6},{5,3},{6,0},{7,5},{8,10},{9,15},{10,... | collective-permute-start | bytes 73736 | tf_op jit(solution)/shard_map/ppermute | solution.py:438
  38.4 2.6 %collective-permute-start.11 = (bf16[4,24,128]{2,1,0:T(8,128)(2,1)S(1)}, bf16[4,24,128]{2,1,0:T(8,128)(2,1)S(1)}, u32[]{:S(2)}, u32[]{:S(2)}) collective-permute-start(bf16[4,24,128]{2,1,0:T(8,128)(2,1)S(1)} %get-tuple-element.32), channel_id=1, source_target_pairs={{0,3},{1,6},{2,5},{3,0},{4,7},{5,2},{6,1},{7,4},{8,11},{9,14},{10,... | collective-permute-start | bytes 73736 | tf_op jit(solution)/shard_map/ppermute | solution.py:439
  41.0 2.2 %collective-permute-done.11.far = bf16[4,24,128]{2,1,0:T(8,128)(2,1)S(1)} collective-permute-done((bf16[4,24,128]{2,1,0:T(8,128)(2,1)S(1)}, bf16[4,24,128]{2,1,0:T(8,128)(2,1)S(1)}, u32[]{:S(2)}, u32[]{:S(2)}) %collective-permute-start.11) | collective-permute-done | bytes 24608 | tf_op jit(solution)/shard_map/ppermute | solution.py:439
  43.2 1.4 %all-to-all-done.sums_ref = f32[128,2,128]{2,1,0:T(2,128)S(1)} async-done(((f32[128,2,128]{2,1,0:T(2,128)}), f32[128,2,128]{2,1,0:T(2,128)S(1)}, u32[]{:S(2)}, u32[]{:S(2)}) %all-to-all-start) | async-done | bytes 131104 | tf_op jit(solution)/shard_map/all_to_all | solution.py:430
  44.6 0.9 %shard_map.89 = (f32[8,24,128]{2,1,0:T(8,128)}, f32[8,24,128]{2,1,0:T(8,128)}, f32[3,3,3,8]{3,2,1,0:T(4,128)}, f32[1,1]{1,0:T(1,128)}) custom-call(bf16[8,24,128]{2,1,0:T(8,128)(2,1)S(1)} %get-tuple-element.29.kept_ref.kept, bf16[8,24,128]{2,1,0:T(8,128)(2,1)S(1)} %collective-permute-done.9.got_ref.got, ...), custom_call_target="tpu_custom_call" | custom-call | bytes 1048576 | tf_op jit(solution)/shard_map/pallas_call | solution.py:358
  (10 shorter events, 0.1 us)
Async XLA Ops:
  1.8 5.9 %collective-permute-start = (bf16[5,24,128]{2,1,0:T(8,128)(2,1)S(1)}, bf16[5,24,128]{2,1,0:T(8,128)(2,1)S(1)}, u32[]{:S(2)}, u32[]{:S(2)}) collective-permute-start(bf16[5,24,128]{2,1,0:T(8,128)(2,1)S(1)} %get-tuple-element.22), channel_id=1, source_target_pairs={{0,8},{8,16},{16,24},{24,0},{1,9},{9,17},{17,25},{25,1},{2,10},{10... | collective-permute-start | bytes 92168 | tf_op jit(solution)/shard_map/ppermute | solution.py:388
  4.3 3.4 %collective-permute-start.1 = (bf16[5,24,128]{2,1,0:T(8,128)(2,1)S(1)}, bf16[5,24,128]{2,1,0:T(8,128)(2,1)S(1)}, u32[]{:S(2)}, u32[]{:S(2)}) collective-permute-start(bf16[5,24,128]{2,1,0:T(8,128)(2,1)S(1)} %get-tuple-element.23), channel_id=1, source_target_pairs={{8,0},{16,8},{24,16},{0,24},{9,1},{17,9},{25,17},{1,25},{10,2},{18... | collective-permute-start | bytes 92168 | tf_op jit(solution)/shard_map/ppermute | solution.py:389
  7.8 7.3 %collective-permute-start.2 = (bf16[13,24,128]{2,1,0:T(8,128)(2,1)S(1)}, bf16[13,24,128]{2,1,0:T(8,128)(2,1)S(1)}, u32[]{:S(2)}, u32[]{:S(2)}) collective-permute-start(bf16[13,24,128]{2,1,0:T(8,128)(2,1)S(1)} %get-tuple-element.25), channel_id=1, source_target_pairs={{0,2},{1,3},{2,4},{3,5},{4,6},{5,7},{6,0},{7,1},{8,10},{9,11},{10,... | collective-permute-start | bytes 239624 | tf_op jit(solution)/shard_map/ppermute | solution.py:401
  9.1 6.7 %collective-permute-start.3 = (bf16[13,24,128]{2,1,0:T(8,128)(2,1)S(1)}, bf16[13,24,128]{2,1,0:T(8,128)(2,1)S(1)}, u32[]{:S(2)}, u32[]{:S(2)}) collective-permute-start(bf16[13,24,128]{2,1,0:T(8,128)(2,1)S(1)} %get-tuple-element.26), channel_id=1, source_target_pairs={{0,4},{1,5},{2,6},{3,7},{4,0},{5,1},{6,2},{7,3},{8,12},{9,13},{10,... | collective-permute-start | bytes 239624 | tf_op jit(solution)/shard_map/ppermute | solution.py:401
  11.5 5.4 %collective-permute-start.4 = (bf16[13,24,128]{2,1,0:T(8,128)(2,1)S(1)}, bf16[13,24,128]{2,1,0:T(8,128)(2,1)S(1)}, u32[]{:S(2)}, u32[]{:S(2)}) collective-permute-start(bf16[13,24,128]{2,1,0:T(8,128)(2,1)S(1)} %get-tuple-element.27), channel_id=1, source_target_pairs={{0,6},{1,7},{2,0},{3,1},{4,2},{5,3},{6,4},{7,5},{8,14},{9,15},{10,... | collective-permute-start | bytes 239624 | tf_op jit(solution)/shard_map/ppermute | solution.py:401
  12.7 5.4 %collective-permute-start.5 = (bf16[13,24,128]{2,1,0:T(8,128)(2,1)S(1)}, bf16[13,24,128]{2,1,0:T(8,128)(2,1)S(1)}, u32[]{:S(2)}, u32[]{:S(2)}) collective-permute-start(bf16[13,24,128]{2,1,0:T(8,128)(2,1)S(1)} %get-tuple-element.24.refs_0_), channel_id=1, source_target_pairs={{0,1},{1,0},{2,3},{3,2},{4,5},{5,4},{6,7},{7,6},{8,9},{9,8},{10,11... | collective-permute-start | bytes 239624 | tf_op jit(solution)/shard_map/ppermute | solution.py:402
  15.1 3.0 %collective-permute-start.6 = (bf16[13,24,128]{2,1,0:T(8,128)(2,1)S(1)}, bf16[13,24,128]{2,1,0:T(8,128)(2,1)S(1)}, u32[]{:S(2)}, u32[]{:S(2)}) collective-permute-start(bf16[13,24,128]{2,1,0:T(8,128)(2,1)S(1)} %collective-permute-done.2.refs_1_), channel_id=1, source_target_pairs={{0,1},{1,0},{2,3},{3,2},{4,5},{5,4},{6,7},{7,6},{8,9},{9,8},{10,11... | collective-permute-start | bytes 239624 | tf_op jit(solution)/shard_map/ppermute | solution.py:402
  15.7 2.3 %collective-permute-start.7 = (bf16[13,24,128]{2,1,0:T(8,128)(2,1)S(1)}, bf16[13,24,128]{2,1,0:T(8,128)(2,1)S(1)}, u32[]{:S(2)}, u32[]{:S(2)}) collective-permute-start(bf16[13,24,128]{2,1,0:T(8,128)(2,1)S(1)} %collective-permute-done.3.refs_2_), channel_id=1, source_target_pairs={{0,1},{1,0},{2,3},{3,2},{4,5},{5,4},{6,7},{7,6},{8,9},{9,8},{10,11... | collective-permute-start | bytes 239624 | tf_op jit(solution)/shard_map/ppermute | solution.py:402
  16.9 2.1 %collective-permute-start.8 = (bf16[13,24,128]{2,1,0:T(8,128)(2,1)S(1)}, bf16[13,24,128]{2,1,0:T(8,128)(2,1)S(1)}, u32[]{:S(2)}, u32[]{:S(2)}) collective-permute-start(bf16[13,24,128]{2,1,0:T(8,128)(2,1)S(1)} %collective-permute-done.4.refs_3_), channel_id=1, source_target_pairs={{0,1},{1,0},{2,3},{3,2},{4,5},{5,4},{6,7},{7,6},{8,9},{9,8},{10,11... | collective-permute-start | bytes 239624 | tf_op jit(solution)/shard_map/ppermute | solution.py:402
  24.9 9.7 %collective-permute-start.9 = (bf16[8,24,128]{2,1,0:T(8,128)(2,1)S(1)}, bf16[8,24,128]{2,1,0:T(8,128)(2,1)S(1)}, u32[]{:S(2)}, u32[]{:S(2)}) collective-permute-start(bf16[8,24,128]{2,1,0:T(8,128)(2,1)S(1)} %get-tuple-element.30), channel_id=1, source_target_pairs={{0,1},{1,0},{2,3},{3,2},{4,5},{5,4},{6,7},{7,6},{8,9},{9,8},{10,11... | collective-permute-start | bytes 147464 | tf_op jit(solution)/shard_map/ppermute | solution.py:364
  25.3 19.3 %all-to-all-start = ((f32[128,2,128]{2,1,0:T(2,128)}), f32[128,2,128]{2,1,0:T(2,128)S(1)}, u32[]{:S(2)}, u32[]{:S(2)}) async-start(f32[128,2,128]{2,1,0:T(2,128)} %get-tuple-element.33), calls=%async_computation | async-start | bytes 262144 | tf_op jit(solution)/shard_map/all_to_all | solution.py:430
  34.6 6.5 %collective-permute-start.12 = (bf16[4,24,128]{2,1,0:T(8,128)(2,1)S(1)}, bf16[4,24,128]{2,1,0:T(8,128)(2,1)S(1)}, u32[]{:S(2)}, u32[]{:S(2)}) collective-permute-start(bf16[4,24,128]{2,1,0:T(8,128)(2,1)S(1)} %shard_map.87.refs_0_), channel_id=1, source_target_pairs={{0,4},{1,5},{2,6},{3,7},{4,0},{5,1},{6,2},{7,3},{8,12},{9,13},{10,... | collective-permute-start | bytes 73736 | tf_op jit(solution)/shard_map/ppermute | solution.py:434
  37.5 3.5 %collective-permute-start.10 = (bf16[4,24,128]{2,1,0:T(8,128)(2,1)S(1)}, bf16[4,24,128]{2,1,0:T(8,128)(2,1)S(1)}, u32[]{:S(2)}, u32[]{:S(2)}) collective-permute-start(bf16[4,24,128]{2,1,0:T(8,128)(2,1)S(1)} %get-tuple-element.31), channel_id=1, source_target_pairs={{0,2},{1,7},{2,4},{3,1},{4,6},{5,3},{6,0},{7,5},{8,10},{9,15},{10,... | collective-permute-start | bytes 73736 | tf_op jit(solution)/shard_map/ppermute | solution.py:438
  38.4 4.8 %collective-permute-start.11 = (bf16[4,24,128]{2,1,0:T(8,128)(2,1)S(1)}, bf16[4,24,128]{2,1,0:T(8,128)(2,1)S(1)}, u32[]{:S(2)}, u32[]{:S(2)}) collective-permute-start(bf16[4,24,128]{2,1,0:T(8,128)(2,1)S(1)} %get-tuple-element.32), channel_id=1, source_target_pairs={{0,3},{1,6},{2,5},{3,0},{4,7},{5,2},{6,1},{7,4},{8,11},{9,14},{10,... | collective-permute-start | bytes 73736 | tf_op jit(solution)/shard_map/ppermute | solution.py:439

commit v7 on v6

--- a/solution.py
+++ b/solution.py
@@ -35,26 +35,36 @@
     return dot(gt, pick_gt, TN) + dot(valid, pick_valid, TN)
 
 
-def halo_kernel(left_any, right_any, gt_any, valid_any, weight_any, up_ref, down_ref, own_ref, taps_ref, *scratch):
-    refs, sems = scratch[:5], scratch[5]
-    sources = (left_any, right_any, gt_any, valid_any, weight_any)
+def copied_in(sources, refs, sems):
     copies = [pltpu.make_async_copy(src, dst, sems.at[i]) for i, (src, dst) in enumerate(zip(sources, refs))]
     for copy in copies:
         copy.start()
     for copy in copies:
         copy.wait()
-    left_ref, right_ref, gt_ref, valid_ref, weight_ref = refs
+
+
+def halo_kernel(left_any, right_any, gt_any, valid_any, up_ref, down_ref, *scratch):
+    refs, sems = scratch[:4], scratch[4]
+    copied_in((left_any, right_any, gt_any, valid_any), refs, sems)
+    left_ref, right_ref, gt_ref, valid_ref = refs
     gt = gt_ref[...].astype(F32)
     valid = valid_ref[...].astype(F32)
     for side, ref in ((0, left_ref), (1, right_ref)):
         for i in range(2):
             up_ref[2 * side + i] = ref[ROWS - 2 + i]
             down_ref[2 * side + i] = ref[i]
+    up_ref[4] = meta_block(gt, valid, ROWS - 2, 2, 0).astype(BF16)
+    down_ref[4] = meta_block(gt, valid, 0, 2, ROWS + 2).astype(BF16)
+
+
+def own_tile_kernel(left_any, right_any, gt_any, valid_any, weight_any, own_ref, taps_ref, *scratch):
+    refs, sems = scratch[:5], scratch[5]
+    copied_in((left_any, right_any, gt_any, valid_any, weight_any), refs, sems)
+    left_ref, right_ref, gt_ref, valid_ref, weight_ref = refs
+    for side, ref in ((0, left_ref), (1, right_ref)):
         for i in range(ROWS):
             own_ref[ROWS * side + i] = ref[i]
-    up_ref[4] = meta_block(gt, valid, ROWS - 2, 2, 0).astype(BF16)
-    down_ref[4] = meta_block(gt, valid, 0, 2, ROWS + 2).astype(BF16)
-    own_ref[2 * ROWS] = meta_block(gt, valid, 0, ROWS, 2).astype(BF16)
+    own_ref[2 * ROWS] = meta_block(gt_ref[...].astype(F32), valid_ref[...].astype(F32), 0, ROWS, 2).astype(BF16)
     member = group_member() * (1.0 / 16.0)
     for a in range(3):
         taps = jnp.concatenate([weight_ref[a, b] for b in range(3)], axis=0)
@@ -371,20 +381,29 @@
     halo = jax.ShapeDtypeStruct((5, TILE, CH), BF16)
     own = jax.ShapeDtypeStruct((2 * ROWS + 1, TILE, CH), BF16)
     args = (left, right, gt, valid, jnp.transpose(conv_weight, (1, 2, 3, 0)))
-    up, down, own, taps = pl.pallas_call(
+    args = [pltpu.with_memory_space_constraint(arg, pltpu.HBM) for arg in args]
+    arg_copies = (
+        pltpu.VMEM((ROWS, TILE, CH), BF16),
+        pltpu.VMEM((ROWS, TILE, CH), BF16),
+        pltpu.VMEM((ROWS, TILE), jnp.int32),
+        pltpu.VMEM((ROWS, TILE), jnp.int32),
+        pltpu.VMEM((3, 3, 3, 8), F32),
+    )
+    up, down = pl.pallas_call(
         halo_kernel,
-        out_shape=(halo, halo, own, jax.ShapeDtypeStruct((3, 16, CH), F32)),
+        out_shape=(halo, halo),
+        in_specs=[pl.BlockSpec(memory_space=pltpu.HBM)] * 4,
+        scratch_shapes=arg_copies[:4] + (pltpu.SemaphoreType.DMA((4,)),),
+        compiler_params=VMEM,
+    )(*args[:4])
+    own, taps = pl.pallas_call(
+        own_tile_kernel,
+        out_shape=(own, jax.ShapeDtypeStruct((3, 16, CH), F32)),
         in_specs=[pl.BlockSpec(memory_space=pltpu.HBM)] * 5,
-        scratch_shapes=[
-            pltpu.VMEM((ROWS, TILE, CH), BF16),
-            pltpu.VMEM((ROWS, TILE, CH), BF16),
-            pltpu.VMEM((ROWS, TILE), jnp.int32),
-            pltpu.VMEM((ROWS, TILE), jnp.int32),
-            pltpu.VMEM((3, 3, 3, 8), F32),
-            pltpu.SemaphoreType.DMA((5,)),
-        ],
+        scratch_shapes=arg_copies + (pltpu.SemaphoreType.DMA((5,)),),
         compiler_params=VMEM,
-    )(*[pltpu.with_memory_space_constraint(arg, pltpu.HBM) for arg in args])
+        cost_estimate=pl.CostEstimate(flops=1 << 30, bytes_accessed=1 << 18, transcendentals=0),
+    )(*args)
     before = lax.ppermute(up, "ha", [(i, (i + 1) % ha_count) for i in range(ha_count)])
     after = lax.ppermute(down, "ha", [((i + 1) % ha_count, i) for i in range(ha_count)])
     block = jax.ShapeDtypeStruct((13, TILE, CH), BF16)

time: 45.7 us -> 45.7 us (level)
  waiting for transfers between devices: 5.72 us -> 4.62 us
  Pallas kernels: 8.02 us -> 9.03 us
    ppermute x1, waiting for transfers between devices: 1.2 us -> 0.1 us  [shards(): lax.ppermute(up, 'ha', [(i, (i + 1) % ha_count) for i in range(ha_count)])]
    pallas_call x1 -> x2, Pallas kernels: 1.15 us -> 2.16 us  [the longest x1 1.09 us: shards(): pl.pallas_call(own_tile_kernel, out_shape=(own, jax.ShapeDtypeStruct((3,...]
  transfers between devices with their start and end apart: 14 -> 14, of which waited for: 4 -> 4; matrix products, arithmetic and copies ran while one was open for 0% -> 0% of each run, Pallas kernels for 0% -> 2%
where the time goes in v7:
time: 45.7 us; the launch traced here: 45.4 us
  starting transfers between devices  31.1 us (68%)
  Pallas kernels  9.03 us (20%)
  waiting for transfers between devices  4.62 us (10%)
  between operations  0.7 us (2%)
    all_to_all x1, starting transfers between devices, shards(): sums = lax.all_to_all(sums, ('dp', 'ha', 'wa'), 0, 0, tiled=True)  9.22 us
    pallas_call x1, Pallas kernels, shards(): pl.pallas_call(main_kernel, out_shape=(jax.ShapeDtypeStruct((others, 2, C...  5.92 us
    ppermute x4, starting transfers between devices, shards(): lax.ppermute(value, 'wa', [(i, i ^ 1) for i in range(WA)])  5.36 us
    ppermute x3, starting transfers between devices, shards(): lax.ppermute(blocks[hop], 'wa', [(i, (i + 2 * hop) % WA) for i in range(W...  4.89 us
    ppermute x1, starting transfers between devices, shards(): lax.ppermute(opposite, 'wa', [(i, (i + 4) % WA) for i in range(WA)])  2.97 us
    ppermute x1, starting transfers between devices, shards(): lax.ppermute(beside_other, 'wa', [(i, (i + 3 - 6 * (i % 2)) % WA) for i i...  2.6 us
    ppermute x1, starting transfers between devices, shards(): lax.ppermute(up, 'ha', [(i, (i + 1) % ha_count) for i in range(ha_count)])  2.54 us
    ppermute x1, starting transfers between devices, shards(): lax.ppermute(down, 'ha', [((i + 1) % ha_count, i) for i in range(ha_count)])  2.2 us
  transfers between devices with their start and end apart: 14, of which 4 were waited for; matrix products, arithmetic and copies ran while one was open for 0% of the time, Pallas kernels for 2%

profile of v7, /device:TPU:1, one launch (start us, length us, event | category | flops | bytes accessed | tf_op | source)
XLA Modules:
  0.0 45.4 jit_solution(10193250530529428601)
XLA Ops:
  0.6 1.1 %shard_map.85 = (bf16[5,24,128]{2,1,0:T(8,128)(2,1)S(1)}, bf16[5,24,128]{2,1,0:T(8,128)(2,1)S(1)}) custom-call(bf16[8,24,128]{2,1,0:T(8,128)(2,1)} %bitcast.9, bf16[8,24,128]{2,1,0:T(8,128)(2,1)} %bitcast.11, s32[8,24]{1,0:T(8,128)} %bitcast.13, s32[8,24]{1,0:T(8,128)} %bitcast.15), custom_call_target="tpu_custom_call" | custom-call | tf_op jit(solution)/shard_map/pallas_call | solution.py:392
  1.7 2.5 %collective-permute-start = (bf16[5,24,128]{2,1,0:T(8,128)(2,1)S(1)}, bf16[5,24,128]{2,1,0:T(8,128)(2,1)S(1)}, u32[]{:S(2)}, u32[]{:S(2)}) collective-permute-start(bf16[5,24,128]{2,1,0:T(8,128)(2,1)S(1)} %get-tuple-element.22), channel_id=1, source_target_pairs={{0,8},{8,16},{16,24},{24,0},{1,9},{9,17},{17,25},{25,1},{2,10},{10... | collective-permute-start | bytes 92168 | tf_op jit(solution)/shard_map/ppermute | solution.py:407
  4.2 2.2 %collective-permute-start.1 = (bf16[5,24,128]{2,1,0:T(8,128)(2,1)S(1)}, bf16[5,24,128]{2,1,0:T(8,128)(2,1)S(1)}, u32[]{:S(2)}, u32[]{:S(2)}) collective-permute-start(bf16[5,24,128]{2,1,0:T(8,128)(2,1)S(1)} %get-tuple-element.23), channel_id=1, source_target_pairs={{8,0},{16,8},{24,16},{0,24},{9,1},{17,9},{25,17},{1,25},{10,2},{18... | collective-permute-start | bytes 92168 | tf_op jit(solution)/shard_map/ppermute | solution.py:408
  6.4 1.1 %shard_map.84 = (bf16[17,24,128]{2,1,0:T(8,128)(2,1)S(1)}, f32[3,16,128]{2,1,0:T(8,128)S(1)}) custom-call(bf16[8,24,128]{2,1,0:T(8,128)(2,1)} %bitcast.10, bf16[8,24,128]{2,1,0:T(8,128)(2,1)} %bitcast.12, s32[8,24]{1,0:T(8,128)} %bitcast.14, s32[8,24]{1,0:T(8,128)} %bitcast.16, f32[3,3,3,8]{3,2,1,0:T(4,128)} %bitcast.19), custom_call_target="tpu_custom_call" | custom-call | flops 1073741824 | bytes 262144 | tf_op jit(solution)/shard_map/pallas_call | solution.py:399
  7.5 0.1 collective-permute-done.prev_ref
  7.6 0.0 collective-permute-done.1.next_ref
  7.7 1.3 %collective-permute-start.2 = (bf16[13,24,128]{2,1,0:T(8,128)(2,1)S(1)}, bf16[13,24,128]{2,1,0:T(8,128)(2,1)S(1)}, u32[]{:S(2)}, u32[]{:S(2)}) collective-permute-start(bf16[13,24,128]{2,1,0:T(8,128)(2,1)S(1)} %get-tuple-element.25), channel_id=1, source_target_pairs={{0,2},{1,3},{2,4},{3,5},{4,6},{5,7},{6,0},{7,1},{8,10},{9,11},{10,... | collective-permute-start | bytes 239624 | tf_op jit(solution)/shard_map/ppermute | solution.py:420
  9.0 2.5 %collective-permute-start.3 = (bf16[13,24,128]{2,1,0:T(8,128)(2,1)S(1)}, bf16[13,24,128]{2,1,0:T(8,128)(2,1)S(1)}, u32[]{:S(2)}, u32[]{:S(2)}) collective-permute-start(bf16[13,24,128]{2,1,0:T(8,128)(2,1)S(1)} %get-tuple-element.26), channel_id=1, source_target_pairs={{0,4},{1,5},{2,6},{3,7},{4,0},{5,1},{6,2},{7,3},{8,12},{9,13},{10,... | collective-permute-start | bytes 239624 | tf_op jit(solution)/shard_map/ppermute | solution.py:420
  11.4 1.2 %collective-permute-start.4 = (bf16[13,24,128]{2,1,0:T(8,128)(2,1)S(1)}, bf16[13,24,128]{2,1,0:T(8,128)(2,1)S(1)}, u32[]{:S(2)}, u32[]{:S(2)}) collective-permute-start(bf16[13,24,128]{2,1,0:T(8,128)(2,1)S(1)} %get-tuple-element.27), channel_id=1, source_target_pairs={{0,6},{1,7},{2,0},{3,1},{4,2},{5,3},{6,4},{7,5},{8,14},{9,15},{10,... | collective-permute-start | bytes 239624 | tf_op jit(solution)/shard_map/ppermute | solution.py:420
  12.6 2.4 %collective-permute-start.5 = (bf16[13,24,128]{2,1,0:T(8,128)(2,1)S(1)}, bf16[13,24,128]{2,1,0:T(8,128)(2,1)S(1)}, u32[]{:S(2)}, u32[]{:S(2)}) collective-permute-start(bf16[13,24,128]{2,1,0:T(8,128)(2,1)S(1)} %get-tuple-element.24.refs_0_), channel_id=1, source_target_pairs={{0,1},{1,0},{2,3},{3,2},{4,5},{5,4},{6,7},{7,6},{8,9},{9,8},{10,11... | collective-permute-start | bytes 239624 | tf_op jit(solution)/shard_map/ppermute | solution.py:421
  15.0 0.7 %collective-permute-start.6 = (bf16[13,24,128]{2,1,0:T(8,128)(2,1)S(1)}, bf16[13,24,128]{2,1,0:T(8,128)(2,1)S(1)}, u32[]{:S(2)}, u32[]{:S(2)}) collective-permute-start(bf16[13,24,128]{2,1,0:T(8,128)(2,1)S(1)} %collective-permute-done.2.refs_1_), channel_id=1, source_target_pairs={{0,1},{1,0},{2,3},{3,2},{4,5},{5,4},{6,7},{7,6},{8,9},{9,8},{10,11... | collective-permute-start | bytes 239624 | tf_op jit(solution)/shard_map/ppermute | solution.py:421
  15.6 0.0 collective-permute-done.3.refs_2_
  15.6 1.1 %collective-permute-start.7 = (bf16[13,24,128]{2,1,0:T(8,128)(2,1)S(1)}, bf16[13,24,128]{2,1,0:T(8,128)(2,1)S(1)}, u32[]{:S(2)}, u32[]{:S(2)}) collective-permute-start(bf16[13,24,128]{2,1,0:T(8,128)(2,1)S(1)} %collective-permute-done.3.refs_2_), channel_id=1, source_target_pairs={{0,1},{1,0},{2,3},{3,2},{4,5},{5,4},{6,7},{7,6},{8,9},{9,8},{10,11... | collective-permute-start | bytes 239624 | tf_op jit(solution)/shard_map/ppermute | solution.py:421
  16.8 1.2 %collective-permute-start.8 = (bf16[13,24,128]{2,1,0:T(8,128)(2,1)S(1)}, bf16[13,24,128]{2,1,0:T(8,128)(2,1)S(1)}, u32[]{:S(2)}, u32[]{:S(2)}) collective-permute-start(bf16[13,24,128]{2,1,0:T(8,128)(2,1)S(1)} %collective-permute-done.4.refs_3_), channel_id=1, source_target_pairs={{0,1},{1,0},{2,3},{3,2},{4,5},{5,4},{6,7},{7,6},{8,9},{9,8},{10,11... | collective-permute-start | bytes 239624 | tf_op jit(solution)/shard_map/ppermute | solution.py:421
  18.0 0.9 %collective-permute-done.8.refs_7_ = bf16[13,24,128]{2,1,0:T(8,128)(2,1)S(1)} collective-permute-done((bf16[13,24,128]{2,1,0:T(8,128)(2,1)S(1)}, bf16[13,24,128]{2,1,0:T(8,128)(2,1)S(1)}, u32[]{:S(2)}, u32[]{:S(2)}) %collective-permute-start.8) | collective-permute-done | bytes 79904 | tf_op jit(solution)/shard_map/ppermute | solution.py:421
  18.9 5.9 %shard_map.87 = (f32[128,2,128]{2,1,0:T(2,128)}, bf16[8,24,128]{2,1,0:T(8,128)(2,1)S(1)}, bf16[8,24,128]{2,1,0:T(8,128)(2,1)S(1)}) custom-call(bf16[13,24,128]{2,1,0:T(8,128)(2,1)S(1)} %get-tuple-element.24.refs_0_, bf16[13,24,128]{2,1,0:T(8,128)(2,1)S(1)} %collective-permute-done.2.refs_1_, bf16[13,24,128]{2,1,0:T(8,128)(2,1)S(1)} %collective-permute-done.3.refs_2_, ...), custom_call_target="tpu_custom_call" | custom-call | flops 5368709120 | bytes 1048576 | tf_op jit(solution)/shard_map/pallas_call | solution.py:425
  24.8 0.4 collective-permute-start.9
  25.2 9.2 %all-to-all-start = ((f32[128,2,128]{2,1,0:T(2,128)}), f32[128,2,128]{2,1,0:T(2,128)S(1)}, u32[]{:S(2)}, u32[]{:S(2)}) async-start(f32[128,2,128]{2,1,0:T(2,128)} %get-tuple-element.33), calls=%async_computation | async-start | bytes 262144 | tf_op jit(solution)/shard_map/all_to_all | solution.py:449
  34.5 3.0 %collective-permute-start.12 = (bf16[4,24,128]{2,1,0:T(8,128)(2,1)S(1)}, bf16[4,24,128]{2,1,0:T(8,128)(2,1)S(1)}, u32[]{:S(2)}, u32[]{:S(2)}) collective-permute-start(bf16[4,24,128]{2,1,0:T(8,128)(2,1)S(1)} %shard_map.88.refs_0_), channel_id=1, source_target_pairs={{0,4},{1,5},{2,6},{3,7},{4,0},{5,1},{6,2},{7,3},{8,12},{9,13},{10,... | collective-permute-start | bytes 73736 | tf_op jit(solution)/shard_map/ppermute | solution.py:453
  37.5 0.9 %collective-permute-start.10 = (bf16[4,24,128]{2,1,0:T(8,128)(2,1)S(1)}, bf16[4,24,128]{2,1,0:T(8,128)(2,1)S(1)}, u32[]{:S(2)}, u32[]{:S(2)}) collective-permute-start(bf16[4,24,128]{2,1,0:T(8,128)(2,1)S(1)} %get-tuple-element.31), channel_id=1, source_target_pairs={{0,2},{1,7},{2,4},{3,1},{4,6},{5,3},{6,0},{7,5},{8,10},{9,15},{10,... | collective-permute-start | bytes 73736 | tf_op jit(solution)/shard_map/ppermute | solution.py:457
  38.3 2.6 %collective-permute-start.11 = (bf16[4,24,128]{2,1,0:T(8,128)(2,1)S(1)}, bf16[4,24,128]{2,1,0:T(8,128)(2,1)S(1)}, u32[]{:S(2)}, u32[]{:S(2)}) collective-permute-start(bf16[4,24,128]{2,1,0:T(8,128)(2,1)S(1)} %get-tuple-element.32), channel_id=1, source_target_pairs={{0,3},{1,6},{2,5},{3,0},{4,7},{5,2},{6,1},{7,4},{8,11},{9,14},{10,... | collective-permute-start | bytes 73736 | tf_op jit(solution)/shard_map/ppermute | solution.py:458
  40.9 2.2 %collective-permute-done.11.far = bf16[4,24,128]{2,1,0:T(8,128)(2,1)S(1)} collective-permute-done((bf16[4,24,128]{2,1,0:T(8,128)(2,1)S(1)}, bf16[4,24,128]{2,1,0:T(8,128)(2,1)S(1)}, u32[]{:S(2)}, u32[]{:S(2)}) %collective-permute-start.11) | collective-permute-done | bytes 24608 | tf_op jit(solution)/shard_map/ppermute | solution.py:458
  43.1 1.4 %all-to-all-done.sums_ref = f32[128,2,128]{2,1,0:T(2,128)S(1)} async-done(((f32[128,2,128]{2,1,0:T(2,128)}), f32[128,2,128]{2,1,0:T(2,128)S(1)}, u32[]{:S(2)}, u32[]{:S(2)}) %all-to-all-start) | async-done | bytes 131104 | tf_op jit(solution)/shard_map/all_to_all | solution.py:449
  44.5 0.9 %shard_map.90 = (f32[8,24,128]{2,1,0:T(8,128)}, f32[8,24,128]{2,1,0:T(8,128)}, f32[3,3,3,8]{3,2,1,0:T(4,128)}, f32[1,1]{1,0:T(1,128)}) custom-call(bf16[8,24,128]{2,1,0:T(8,128)(2,1)S(1)} %get-tuple-element.29.kept_ref.kept, bf16[8,24,128]{2,1,0:T(8,128)(2,1)S(1)} %collective-permute-done.9.got_ref.got, ...), custom_call_target="tpu_custom_call" | custom-call | bytes 1048576 | tf_op jit(solution)/shard_map/pallas_call | solution.py:368
  (11 shorter events, 0.1 us)
Async XLA Ops:
  1.7 5.9 %collective-permute-start = (bf16[5,24,128]{2,1,0:T(8,128)(2,1)S(1)}, bf16[5,24,128]{2,1,0:T(8,128)(2,1)S(1)}, u32[]{:S(2)}, u32[]{:S(2)}) collective-permute-start(bf16[5,24,128]{2,1,0:T(8,128)(2,1)S(1)} %get-tuple-element.22), channel_id=1, source_target_pairs={{0,8},{8,16},{16,24},{24,0},{1,9},{9,17},{17,25},{25,1},{2,10},{10... | collective-permute-start | bytes 92168 | tf_op jit(solution)/shard_map/ppermute | solution.py:407
  4.2 3.4 %collective-permute-start.1 = (bf16[5,24,128]{2,1,0:T(8,128)(2,1)S(1)}, bf16[5,24,128]{2,1,0:T(8,128)(2,1)S(1)}, u32[]{:S(2)}, u32[]{:S(2)}) collective-permute-start(bf16[5,24,128]{2,1,0:T(8,128)(2,1)S(1)} %get-tuple-element.23), channel_id=1, source_target_pairs={{8,0},{16,8},{24,16},{0,24},{9,1},{17,9},{25,17},{1,25},{10,2},{18... | collective-permute-start | bytes 92168 | tf_op jit(solution)/shard_map/ppermute | solution.py:408
  7.7 7.3 %collective-permute-start.2 = (bf16[13,24,128]{2,1,0:T(8,128)(2,1)S(1)}, bf16[13,24,128]{2,1,0:T(8,128)(2,1)S(1)}, u32[]{:S(2)}, u32[]{:S(2)}) collective-permute-start(bf16[13,24,128]{2,1,0:T(8,128)(2,1)S(1)} %get-tuple-element.25), channel_id=1, source_target_pairs={{0,2},{1,3},{2,4},{3,5},{4,6},{5,7},{6,0},{7,1},{8,10},{9,11},{10,... | collective-permute-start | bytes 239624 | tf_op jit(solution)/shard_map/ppermute | solution.py:420
  9.0 6.7 %collective-permute-start.3 = (bf16[13,24,128]{2,1,0:T(8,128)(2,1)S(1)}, bf16[13,24,128]{2,1,0:T(8,128)(2,1)S(1)}, u32[]{:S(2)}, u32[]{:S(2)}) collective-permute-start(bf16[13,24,128]{2,1,0:T(8,128)(2,1)S(1)} %get-tuple-element.26), channel_id=1, source_target_pairs={{0,4},{1,5},{2,6},{3,7},{4,0},{5,1},{6,2},{7,3},{8,12},{9,13},{10,... | collective-permute-start | bytes 239624 | tf_op jit(solution)/shard_map/ppermute | solution.py:420
  11.4 5.4 %collective-permute-start.4 = (bf16[13,24,128]{2,1,0:T(8,128)(2,1)S(1)}, bf16[13,24,128]{2,1,0:T(8,128)(2,1)S(1)}, u32[]{:S(2)}, u32[]{:S(2)}) collective-permute-start(bf16[13,24,128]{2,1,0:T(8,128)(2,1)S(1)} %get-tuple-element.27), channel_id=1, source_target_pairs={{0,6},{1,7},{2,0},{3,1},{4,2},{5,3},{6,4},{7,5},{8,14},{9,15},{10,... | collective-permute-start | bytes 239624 | tf_op jit(solution)/shard_map/ppermute | solution.py:420
  12.6 5.4 %collective-permute-start.5 = (bf16[13,24,128]{2,1,0:T(8,128)(2,1)S(1)}, bf16[13,24,128]{2,1,0:T(8,128)(2,1)S(1)}, u32[]{:S(2)}, u32[]{:S(2)}) collective-permute-start(bf16[13,24,128]{2,1,0:T(8,128)(2,1)S(1)} %get-tuple-element.24.refs_0_), channel_id=1, source_target_pairs={{0,1},{1,0},{2,3},{3,2},{4,5},{5,4},{6,7},{7,6},{8,9},{9,8},{10,11... | collective-permute-start | bytes 239624 | tf_op jit(solution)/shard_map/ppermute | solution.py:421
  15.0 3.0 %collective-permute-start.6 = (bf16[13,24,128]{2,1,0:T(8,128)(2,1)S(1)}, bf16[13,24,128]{2,1,0:T(8,128)(2,1)S(1)}, u32[]{:S(2)}, u32[]{:S(2)}) collective-permute-start(bf16[13,24,128]{2,1,0:T(8,128)(2,1)S(1)} %collective-permute-done.2.refs_1_), channel_id=1, source_target_pairs={{0,1},{1,0},{2,3},{3,2},{4,5},{5,4},{6,7},{7,6},{8,9},{9,8},{10,11... | collective-permute-start | bytes 239624 | tf_op jit(solution)/shard_map/ppermute | solution.py:421
  15.6 2.3 %collective-permute-start.7 = (bf16[13,24,128]{2,1,0:T(8,128)(2,1)S(1)}, bf16[13,24,128]{2,1,0:T(8,128)(2,1)S(1)}, u32[]{:S(2)}, u32[]{:S(2)}) collective-permute-start(bf16[13,24,128]{2,1,0:T(8,128)(2,1)S(1)} %collective-permute-done.3.refs_2_), channel_id=1, source_target_pairs={{0,1},{1,0},{2,3},{3,2},{4,5},{5,4},{6,7},{7,6},{8,9},{9,8},{10,11... | collective-permute-start | bytes 239624 | tf_op jit(solution)/shard_map/ppermute | solution.py:421
  16.8 2.1 %collective-permute-start.8 = (bf16[13,24,128]{2,1,0:T(8,128)(2,1)S(1)}, bf16[13,24,128]{2,1,0:T(8,128)(2,1)S(1)}, u32[]{:S(2)}, u32[]{:S(2)}) collective-permute-start(bf16[13,24,128]{2,1,0:T(8,128)(2,1)S(1)} %collective-permute-done.4.refs_3_), channel_id=1, source_target_pairs={{0,1},{1,0},{2,3},{3,2},{4,5},{5,4},{6,7},{7,6},{8,9},{9,8},{10,11... | collective-permute-start | bytes 239624 | tf_op jit(solution)/shard_map/ppermute | solution.py:421
  24.8 9.7 %collective-permute-start.9 = (bf16[8,24,128]{2,1,0:T(8,128)(2,1)S(1)}, bf16[8,24,128]{2,1,0:T(8,128)(2,1)S(1)}, u32[]{:S(2)}, u32[]{:S(2)}) collective-permute-start(bf16[8,24,128]{2,1,0:T(8,128)(2,1)S(1)} %get-tuple-element.30), channel_id=1, source_target_pairs={{0,1},{1,0},{2,3},{3,2},{4,5},{5,4},{6,7},{7,6},{8,9},{9,8},{10,11... | collective-permute-start | bytes 147464 | tf_op jit(solution)/shard_map/ppermute | solution.py:374
  25.2 19.3 %all-to-all-start = ((f32[128,2,128]{2,1,0:T(2,128)}), f32[128,2,128]{2,1,0:T(2,128)S(1)}, u32[]{:S(2)}, u32[]{:S(2)}) async-start(f32[128,2,128]{2,1,0:T(2,128)} %get-tuple-element.33), calls=%async_computation | async-start | bytes 262144 | tf_op jit(solution)/shard_map/all_to_all | solution.py:449
  34.5 6.5 %collective-permute-start.12 = (bf16[4,24,128]{2,1,0:T(8,128)(2,1)S(1)}, bf16[4,24,128]{2,1,0:T(8,128)(2,1)S(1)}, u32[]{:S(2)}, u32[]{:S(2)}) collective-permute-start(bf16[4,24,128]{2,1,0:T(8,128)(2,1)S(1)} %shard_map.88.refs_0_), channel_id=1, source_target_pairs={{0,4},{1,5},{2,6},{3,7},{4,0},{5,1},{6,2},{7,3},{8,12},{9,13},{10,... | collective-permute-start | bytes 73736 | tf_op jit(solution)/shard_map/ppermute | solution.py:453
  37.5 3.5 %collective-permute-start.10 = (bf16[4,24,128]{2,1,0:T(8,128)(2,1)S(1)}, bf16[4,24,128]{2,1,0:T(8,128)(2,1)S(1)}, u32[]{:S(2)}, u32[]{:S(2)}) collective-permute-start(bf16[4,24,128]{2,1,0:T(8,128)(2,1)S(1)} %get-tuple-element.31), channel_id=1, source_target_pairs={{0,2},{1,7},{2,4},{3,1},{4,6},{5,3},{6,0},{7,5},{8,10},{9,15},{10,... | collective-permute-start | bytes 73736 | tf_op jit(solution)/shard_map/ppermute | solution.py:457
  38.3 4.8 %collective-permute-start.11 = (bf16[4,24,128]{2,1,0:T(8,128)(2,1)S(1)}, bf16[4,24,128]{2,1,0:T(8,128)(2,1)S(1)}, u32[]{:S(2)}, u32[]{:S(2)}) collective-permute-start(bf16[4,24,128]{2,1,0:T(8,128)(2,1)S(1)} %get-tuple-element.32), channel_id=1, source_target_pairs={{0,3},{1,6},{2,5},{3,0},{4,7},{5,2},{6,1},{7,4},{8,11},{9,14},{10,... | collective-permute-start | bytes 73736 | tf_op jit(solution)/shard_map/ppermute | solution.py:458

commit v8 on v6

--- a/solution.py
+++ b/solution.py
@@ -72,8 +72,8 @@
     return lax.shift_right_logical(index, 1), index & 1
 
 
-def pack_kernel(own_ref, prev_ref, next_ref, *refs):
-    outs, ext = refs[:CHIPS], refs[CHIPS]
+def pack_kernel(hops, own_ref, prev_ref, next_ref, *refs):
+    outs, ext = refs[-1 - len(hops) : -1], refs[-1]
     chip, _ = position()
     band = lax.axis_index("ha")
     has_prev = band > 0
@@ -93,12 +93,12 @@
             ext[12 * side + ROWS + 2 + i] = of_next(2 * side + i)
         for i in range(ROWS):
             ext[12 * side + 2 + i] = own_ref[ROWS * side + i]
-    for hop in range(CHIPS):
+    for hop, out_ref in zip(hops, outs):
         first = 2 * ((chip + hop) & (CHIPS - 1))
         for i in range(6):
-            outs[hop][i] = ext[first + i]
-            outs[hop][6 + i] = ext[first + 12 + i]
-        outs[hop][12] = meta
+            out_ref[i] = ext[first + i]
+            out_ref[6 + i] = ext[first + 12 + i]
+        out_ref[12] = meta
 
 
 def split3(value):
@@ -388,19 +388,16 @@
     before = lax.ppermute(up, "ha", [(i, (i + 1) % ha_count) for i in range(ha_count)])
     after = lax.ppermute(down, "ha", [((i + 1) % ha_count, i) for i in range(ha_count)])
     block = jax.ShapeDtypeStruct((13, TILE, CH), BF16)
-    blocks = call(
-        pack_kernel,
-        (block,) * CHIPS,
-        own,
-        before,
-        after,
-        scratch=(pltpu.VMEM((24, TILE, CH), BF16),),
-    )
-    same_core = [blocks[0]]
-    for hop in range(1, CHIPS):
-        same_core.append(lax.ppermute(blocks[hop], "wa", [(i, (i + 2 * hop) % WA) for i in range(WA)]))
-    other_core = [lax.ppermute(value, "wa", [(i, i ^ 1) for i in range(WA)]) for value in same_core]
-    tiles = same_core + other_core
+    scratch = (pltpu.VMEM((24, TILE, CH), BF16),)
+    (opposite,) = call(functools.partial(pack_kernel, (2,)), (block,), own, before, after, scratch=scratch)
+    hop2 = lax.ppermute(opposite, "wa", [(i, (i + 4) % WA) for i in range(WA)])
+    hop0, hop1, hop3 = call(
+        functools.partial(pack_kernel, (0, 1, 3)), (block,) * 3, own, before, after, opposite, scratch=scratch, flops=1 << 31
+    )
+    hop1 = lax.ppermute(hop1, "wa", [(i, (i + 2) % WA) for i in range(WA)])
+    hop3 = lax.ppermute(hop3, "wa", [(i, (i + 6) % WA) for i in range(WA)])
+    same_core = [hop0, hop1, hop2, hop3]
+    tiles = same_core + [swapped(value) for value in same_core]
     others = lax.axis_size("dp") * ha_count * WA
     half = jax.ShapeDtypeStruct((8, TILE, CH), BF16)
     sums, kept, given = pl.pallas_call(

time: 45.7 us -> 45.4 us (level)
  starting transfers between devices: 31.1 us -> 30.4 us
    ppermute x1 -> x5, starting transfers between devices: 0.43 us -> 6.5 us  [swapped(): return lax.ppermute(value, 'wa', [(i, i ^ 1) for i in range(WA)])]
    ppermute x7 -> x3, starting transfers between devices: 10.2 us -> 4.28 us  [the longest x1 1.53 us: shards(): hop2 = lax.ppermute(opposite, 'wa', [(i, (i + 4) % WA) for i in range(WA)])]
    ppermute x1 -> x5, waiting for transfers between devices: 0.01 us -> 0.92 us  [swapped(): return lax.ppermute(value, 'wa', [(i, i ^ 1) for i in range(WA)])]
    all_to_all x1, starting transfers between devices: 9.22 us -> 8.39 us  [shards(): sums = lax.all_to_all(sums, ('dp', 'ha', 'wa'), 0, 0, tiled=True)]
    ppermute x7 -> x3, waiting for transfers between devices: 0.92 us -> 0.42 us  [the longest x1 0.41 us: shards(): hop2 = lax.ppermute(opposite, 'wa', [(i, (i + 4) % WA) for i in range(WA)])]
    pallas_call x4 -> x5, Pallas kernels: 0.96 us -> 0.98 us  [call(): pl.pallas_call(kernel, out_shape=out_shape, scratch_shapes=list(scratch),...]
  transfers between devices with their start and end apart: 14 -> 14, of which waited for: 4 -> 5; matrix products, arithmetic and copies ran while one was open for 0% -> 0% of each run, Pallas kernels for 0% -> 0%
where the time goes in v8:
time: 45.4 us; the launch traced here: 45.2 us
  starting transfers between devices  30.4 us (67%)
  Pallas kernels  8.05 us (18%)
  waiting for transfers between devices  6.13 us (14%)
  between operations  0.7 us (2%)
    all_to_all x1, starting transfers between devices, shards(): sums = lax.all_to_all(sums, ('dp', 'ha', 'wa'), 0, 0, tiled=True)  8.39 us
    ppermute x5, starting transfers between devices, swapped(): return lax.ppermute(value, 'wa', [(i, i ^ 1) for i in range(WA)])  6.5 us
    pallas_call x1, Pallas kernels, shards(): pl.pallas_call(main_kernel, out_shape=(jax.ShapeDtypeStruct((others, 2, C...  5.92 us
    ppermute x1, starting transfers between devices, shards(): lax.ppermute(opposite, 'wa', [(i, (i + 4) % WA) for i in range(WA)])  2.97 us
    ppermute x1, starting transfers between devices, shards(): lax.ppermute(beside_other, 'wa', [(i, (i + 3 - 6 * (i % 2)) % WA) for i i...  2.6 us
    ppermute x1, starting transfers between devices, shards(): lax.ppermute(up, 'ha', [(i, (i + 1) % ha_count) for i in range(ha_count)])  2.54 us
    ppermute x1, starting transfers between devices, shards(): lax.ppermute(down, 'ha', [((i + 1) % ha_count, i) for i in range(ha_count)])  2.2 us
    ppermute x1, waiting for transfers between devices, shards(): lax.ppermute(beside_other, 'wa', [(i, (i + 3 - 6 * (i % 2)) % WA) for i i...  2.16 us
  transfers between devices with their start and end apart: 14, of which 5 were waited for; matrix products, arithmetic and copies ran while one was open for 0% of the time, Pallas kernels for 0%

profile of v8, /device:TPU:1, one launch (start us, length us, event | category | flops | bytes accessed | tf_op | source)
XLA Modules:
  0.0 45.2 jit_solution(5839263029483777992)
XLA Ops:
  0.6 1.1 %shard_map.84 = (bf16[5,24,128]{2,1,0:T(8,128)(2,1)S(1)}, bf16[5,24,128]{2,1,0:T(8,128)(2,1)S(1)}, bf16[17,24,128]{2,1,0:T(8,128)(2,1)S(1)}, f32[3,16,128]{2,1,0:T(8,128)S(1)}) custom-call(bf16[8,24,128]{2,1,0:T(8,128)(2,1)} %bitcast.9, bf16[8,24,128]{2,1,0:T(8,128)(2,1)} %bitcast.10, s32[8,24]{1,0:T(8,128)} %bitcast.12, s32[8,24]{1,0:T(8,128)} %bitcast.13, ...), custom_call_target="tpu_custom_call" | custom-call | tf_op jit(solution)/shard_map/pallas_call | solution.py:374
  1.8 2.5 %collective-permute-start = (bf16[5,24,128]{2,1,0:T(8,128)(2,1)S(1)}, bf16[5,24,128]{2,1,0:T(8,128)(2,1)S(1)}, u32[]{:S(2)}, u32[]{:S(2)}) collective-permute-start(bf16[5,24,128]{2,1,0:T(8,128)(2,1)S(1)} %get-tuple-element.21), channel_id=1, source_target_pairs={{0,8},{8,16},{16,24},{24,0},{1,9},{9,17},{17,25},{25,1},{2,10},{10... | collective-permute-start | bytes 92168 | tf_op jit(solution)/shard_map/ppermute | solution.py:388
  4.3 2.2 %collective-permute-start.1 = (bf16[5,24,128]{2,1,0:T(8,128)(2,1)S(1)}, bf16[5,24,128]{2,1,0:T(8,128)(2,1)S(1)}, u32[]{:S(2)}, u32[]{:S(2)}) collective-permute-start(bf16[5,24,128]{2,1,0:T(8,128)(2,1)S(1)} %get-tuple-element.22), channel_id=1, source_target_pairs={{8,0},{16,8},{24,16},{0,24},{9,1},{17,9},{25,17},{1,25},{10,2},{18... | collective-permute-start | bytes 92168 | tf_op jit(solution)/shard_map/ppermute | solution.py:389
  6.5 1.2 %collective-permute-done.prev_ref = bf16[5,24,128]{2,1,0:T(8,128)(2,1)S(1)} collective-permute-done((bf16[5,24,128]{2,1,0:T(8,128)(2,1)S(1)}, bf16[5,24,128]{2,1,0:T(8,128)(2,1)S(1)}, u32[]{:S(2)}, u32[]{:S(2)}) %collective-permute-start) | collective-permute-done | bytes 30752 | tf_op jit(solution)/shard_map/ppermute | solution.py:388
  7.8 1.3 %collective-permute-start.2 = (bf16[13,24,128]{2,1,0:T(8,128)(2,1)S(1)}, bf16[13,24,128]{2,1,0:T(8,128)(2,1)S(1)}, u32[]{:S(2)}, u32[]{:S(2)}) collective-permute-start(bf16[13,24,128]{2,1,0:T(8,128)(2,1)S(1)} %get-tuple-element.24), channel_id=1, source_target_pairs={{0,2},{1,3},{2,4},{3,5},{4,6},{5,7},{6,0},{7,1},{8,10},{9,11},{10,... | collective-permute-start | bytes 239624 | tf_op jit(solution)/shard_map/ppermute | solution.py:397
  9.1 1.5 %collective-permute-start.4 = (bf16[13,24,128]{2,1,0:T(8,128)(2,1)S(1)}, bf16[13,24,128]{2,1,0:T(8,128)(2,1)S(1)}, u32[]{:S(2)}, u32[]{:S(2)}) collective-permute-start(bf16[13,24,128]{2,1,0:T(8,128)(2,1)S(1)} %get-tuple-element.25), channel_id=1, source_target_pairs={{0,6},{1,7},{2,0},{3,1},{4,2},{5,3},{6,4},{7,5},{8,14},{9,15},{10,... | collective-permute-start | bytes 239624 | tf_op jit(solution)/shard_map/ppermute | solution.py:398
  10.6 1.5 %collective-permute-start.3 = (bf16[13,24,128]{2,1,0:T(8,128)(2,1)S(1)}, bf16[13,24,128]{2,1,0:T(8,128)(2,1)S(1)}, u32[]{:S(2)}, u32[]{:S(2)}) collective-permute-start(bf16[13,24,128]{2,1,0:T(8,128)(2,1)S(1)} %shard_map.85.refs_0_), channel_id=1, source_target_pairs={{0,4},{1,5},{2,6},{3,7},{4,0},{5,1},{6,2},{7,3},{8,12},{9,13},{10,... | collective-permute-start | bytes 239624 | tf_op jit(solution)/shard_map/ppermute | solution.py:393
  12.1 2.4 %collective-permute-start.5 = (bf16[13,24,128]{2,1,0:T(8,128)(2,1)S(1)}, bf16[13,24,128]{2,1,0:T(8,128)(2,1)S(1)}, u32[]{:S(2)}, u32[]{:S(2)}) collective-permute-start(bf16[13,24,128]{2,1,0:T(8,128)(2,1)S(1)} %get-tuple-element.23.refs_0_), channel_id=1, source_target_pairs={{0,1},{1,0},{2,3},{3,2},{4,5},{5,4},{6,7},{7,6},{8,9},{9,8},{10,11... | collective-permute-start | bytes 239624 | tf_op jit(solution)/shard_map/ppermute | solution.py:364
  14.5 0.6 %collective-permute-start.6 = (bf16[13,24,128]{2,1,0:T(8,128)(2,1)S(1)}, bf16[13,24,128]{2,1,0:T(8,128)(2,1)S(1)}, u32[]{:S(2)}, u32[]{:S(2)}) collective-permute-start(bf16[13,24,128]{2,1,0:T(8,128)(2,1)S(1)} %collective-permute-done.2.refs_1_), channel_id=1, source_target_pairs={{0,1},{1,0},{2,3},{3,2},{4,5},{5,4},{6,7},{7,6},{8,9},{9,8},{10,11... | collective-permute-start | bytes 239624 | tf_op jit(solution)/shard_map/ppermute | solution.py:364
  15.1 0.0 collective-permute-done.4.refs_3_
  15.1 0.7 %collective-permute-start.8 = (bf16[13,24,128]{2,1,0:T(8,128)(2,1)S(1)}, bf16[13,24,128]{2,1,0:T(8,128)(2,1)S(1)}, u32[]{:S(2)}, u32[]{:S(2)}) collective-permute-start(bf16[13,24,128]{2,1,0:T(8,128)(2,1)S(1)} %collective-permute-done.4.refs_3_), channel_id=1, source_target_pairs={{0,1},{1,0},{2,3},{3,2},{4,5},{5,4},{6,7},{7,6},{8,9},{9,8},{10,11... | collective-permute-start | bytes 239624 | tf_op jit(solution)/shard_map/ppermute | solution.py:364
  15.8 0.4 collective-permute-done.3.refs_2_
  16.2 2.4 %collective-permute-start.7 = (bf16[13,24,128]{2,1,0:T(8,128)(2,1)S(1)}, bf16[13,24,128]{2,1,0:T(8,128)(2,1)S(1)}, u32[]{:S(2)}, u32[]{:S(2)}) collective-permute-start(bf16[13,24,128]{2,1,0:T(8,128)(2,1)S(1)} %collective-permute-done.3.refs_2_), channel_id=1, source_target_pairs={{0,1},{1,0},{2,3},{3,2},{4,5},{5,4},{6,7},{7,6},{8,9},{9,8},{10,11... | collective-permute-start | bytes 239624 | tf_op jit(solution)/shard_map/ppermute | solution.py:364
  18.6 0.0 collective-permute-done.8.refs_7_
  18.6 0.9 %collective-permute-done.7.refs_6_ = bf16[13,24,128]{2,1,0:T(8,128)(2,1)S(1)} collective-permute-done((bf16[13,24,128]{2,1,0:T(8,128)(2,1)S(1)}, bf16[13,24,128]{2,1,0:T(8,128)(2,1)S(1)}, u32[]{:S(2)}, u32[]{:S(2)}) %collective-permute-start.7) | collective-permute-done | bytes 79904 | tf_op jit(solution)/shard_map/ppermute | solution.py:364
  19.5 5.9 %shard_map.87 = (f32[128,2,128]{2,1,0:T(2,128)}, bf16[8,24,128]{2,1,0:T(8,128)(2,1)S(1)}, bf16[8,24,128]{2,1,0:T(8,128)(2,1)S(1)}) custom-call(bf16[13,24,128]{2,1,0:T(8,128)(2,1)S(1)} %get-tuple-element.23.refs_0_, bf16[13,24,128]{2,1,0:T(8,128)(2,1)S(1)} %collective-permute-done.2.refs_1_, bf16[13,24,128]{2,1,0:T(8,128)(2,1)S(1)} %collective-permute-done.3.refs_2_, ...), custom_call_target="tpu_custom_call" | custom-call | flops 5368709120 | bytes 1048576 | tf_op jit(solution)/shard_map/pallas_call | solution.py:403
  25.4 0.4 collective-permute-start.9
  25.9 8.4 %all-to-all-start = ((f32[128,2,128]{2,1,0:T(2,128)}), f32[128,2,128]{2,1,0:T(2,128)S(1)}, u32[]{:S(2)}, u32[]{:S(2)}) async-start(f32[128,2,128]{2,1,0:T(2,128)} %get-tuple-element.31), calls=%async_computation | async-start | bytes 262144 | tf_op jit(solution)/shard_map/all_to_all | solution.py:427
  34.3 3.0 %collective-permute-start.12 = (bf16[4,24,128]{2,1,0:T(8,128)(2,1)S(1)}, bf16[4,24,128]{2,1,0:T(8,128)(2,1)S(1)}, u32[]{:S(2)}, u32[]{:S(2)}) collective-permute-start(bf16[4,24,128]{2,1,0:T(8,128)(2,1)S(1)} %shard_map.88.refs_0_), channel_id=1, source_target_pairs={{0,4},{1,5},{2,6},{3,7},{4,0},{5,1},{6,2},{7,3},{8,12},{9,13},{10,... | collective-permute-start | bytes 73736 | tf_op jit(solution)/shard_map/ppermute | solution.py:431
  37.3 0.9 %collective-permute-start.10 = (bf16[4,24,128]{2,1,0:T(8,128)(2,1)S(1)}, bf16[4,24,128]{2,1,0:T(8,128)(2,1)S(1)}, u32[]{:S(2)}, u32[]{:S(2)}) collective-permute-start(bf16[4,24,128]{2,1,0:T(8,128)(2,1)S(1)} %get-tuple-element.29), channel_id=1, source_target_pairs={{0,2},{1,7},{2,4},{3,1},{4,6},{5,3},{6,0},{7,5},{8,10},{9,15},{10,... | collective-permute-start | bytes 73736 | tf_op jit(solution)/shard_map/ppermute | solution.py:435
  38.1 2.6 %collective-permute-start.11 = (bf16[4,24,128]{2,1,0:T(8,128)(2,1)S(1)}, bf16[4,24,128]{2,1,0:T(8,128)(2,1)S(1)}, u32[]{:S(2)}, u32[]{:S(2)}) collective-permute-start(bf16[4,24,128]{2,1,0:T(8,128)(2,1)S(1)} %get-tuple-element.30), channel_id=1, source_target_pairs={{0,3},{1,6},{2,5},{3,0},{4,7},{5,2},{6,1},{7,4},{8,11},{9,14},{10,... | collective-permute-start | bytes 73736 | tf_op jit(solution)/shard_map/ppermute | solution.py:436
  40.7 2.2 %collective-permute-done.11.far = bf16[4,24,128]{2,1,0:T(8,128)(2,1)S(1)} collective-permute-done((bf16[4,24,128]{2,1,0:T(8,128)(2,1)S(1)}, bf16[4,24,128]{2,1,0:T(8,128)(2,1)S(1)}, u32[]{:S(2)}, u32[]{:S(2)}) %collective-permute-start.11) | collective-permute-done | bytes 24608 | tf_op jit(solution)/shard_map/ppermute | solution.py:436
  42.9 1.4 %all-to-all-done.sums_ref = f32[128,2,128]{2,1,0:T(2,128)S(1)} async-done(((f32[128,2,128]{2,1,0:T(2,128)}), f32[128,2,128]{2,1,0:T(2,128)S(1)}, u32[]{:S(2)}, u32[]{:S(2)}) %all-to-all-start) | async-done | bytes 131104 | tf_op jit(solution)/shard_map/all_to_all | solution.py:427
  44.3 0.9 %shard_map.90 = (f32[8,24,128]{2,1,0:T(8,128)}, f32[8,24,128]{2,1,0:T(8,128)}, f32[3,3,3,8]{3,2,1,0:T(4,128)}, f32[1,1]{1,0:T(1,128)}) custom-call(bf16[8,24,128]{2,1,0:T(8,128)(2,1)S(1)} %get-tuple-element.27.kept_ref.kept, bf16[8,24,128]{2,1,0:T(8,128)(2,1)S(1)} %collective-permute-done.9.got_ref.got, ...), custom_call_target="tpu_custom_call" | custom-call | bytes 1048576 | tf_op jit(solution)/shard_map/pallas_call | solution.py:358
  (11 shorter events, 0.1 us)
Async XLA Ops:
  1.8 5.9 %collective-permute-start = (bf16[5,24,128]{2,1,0:T(8,128)(2,1)S(1)}, bf16[5,24,128]{2,1,0:T(8,128)(2,1)S(1)}, u32[]{:S(2)}, u32[]{:S(2)}) collective-permute-start(bf16[5,24,128]{2,1,0:T(8,128)(2,1)S(1)} %get-tuple-element.21), channel_id=1, source_target_pairs={{0,8},{8,16},{16,24},{24,0},{1,9},{9,17},{17,25},{25,1},{2,10},{10... | collective-permute-start | bytes 92168 | tf_op jit(solution)/shard_map/ppermute | solution.py:388
  4.3 3.4 %collective-permute-start.1 = (bf16[5,24,128]{2,1,0:T(8,128)(2,1)S(1)}, bf16[5,24,128]{2,1,0:T(8,128)(2,1)S(1)}, u32[]{:S(2)}, u32[]{:S(2)}) collective-permute-start(bf16[5,24,128]{2,1,0:T(8,128)(2,1)S(1)} %get-tuple-element.22), channel_id=1, source_target_pairs={{8,0},{16,8},{24,16},{0,24},{9,1},{17,9},{25,17},{1,25},{10,2},{18... | collective-permute-start | bytes 92168 | tf_op jit(solution)/shard_map/ppermute | solution.py:389
  7.8 6.7 %collective-permute-start.2 = (bf16[13,24,128]{2,1,0:T(8,128)(2,1)S(1)}, bf16[13,24,128]{2,1,0:T(8,128)(2,1)S(1)}, u32[]{:S(2)}, u32[]{:S(2)}) collective-permute-start(bf16[13,24,128]{2,1,0:T(8,128)(2,1)S(1)} %get-tuple-element.24), channel_id=1, source_target_pairs={{0,2},{1,3},{2,4},{3,5},{4,6},{5,7},{6,0},{7,1},{8,10},{9,11},{10,... | collective-permute-start | bytes 239624 | tf_op jit(solution)/shard_map/ppermute | solution.py:397
  9.1 6.0 %collective-permute-start.4 = (bf16[13,24,128]{2,1,0:T(8,128)(2,1)S(1)}, bf16[13,24,128]{2,1,0:T(8,128)(2,1)S(1)}, u32[]{:S(2)}, u32[]{:S(2)}) collective-permute-start(bf16[13,24,128]{2,1,0:T(8,128)(2,1)S(1)} %get-tuple-element.25), channel_id=1, source_target_pairs={{0,6},{1,7},{2,0},{3,1},{4,2},{5,3},{6,4},{7,5},{8,14},{9,15},{10,... | collective-permute-start | bytes 239624 | tf_op jit(solution)/shard_map/ppermute | solution.py:398
  10.6 5.6 %collective-permute-start.3 = (bf16[13,24,128]{2,1,0:T(8,128)(2,1)S(1)}, bf16[13,24,128]{2,1,0:T(8,128)(2,1)S(1)}, u32[]{:S(2)}, u32[]{:S(2)}) collective-permute-start(bf16[13,24,128]{2,1,0:T(8,128)(2,1)S(1)} %shard_map.85.refs_0_), channel_id=1, source_target_pairs={{0,4},{1,5},{2,6},{3,7},{4,0},{5,1},{6,2},{7,3},{8,12},{9,13},{10,... | collective-permute-start | bytes 239624 | tf_op jit(solution)/shard_map/ppermute | solution.py:393
  12.1 6.5 %collective-permute-start.5 = (bf16[13,24,128]{2,1,0:T(8,128)(2,1)S(1)}, bf16[13,24,128]{2,1,0:T(8,128)(2,1)S(1)}, u32[]{:S(2)}, u32[]{:S(2)}) collective-permute-start(bf16[13,24,128]{2,1,0:T(8,128)(2,1)S(1)} %get-tuple-element.23.refs_0_), channel_id=1, source_target_pairs={{0,1},{1,0},{2,3},{3,2},{4,5},{5,4},{6,7},{7,6},{8,9},{9,8},{10,11... | collective-permute-start | bytes 239624 | tf_op jit(solution)/shard_map/ppermute | solution.py:364
  14.5 4.1 %collective-permute-start.6 = (bf16[13,24,128]{2,1,0:T(8,128)(2,1)S(1)}, bf16[13,24,128]{2,1,0:T(8,128)(2,1)S(1)}, u32[]{:S(2)}, u32[]{:S(2)}) collective-permute-start(bf16[13,24,128]{2,1,0:T(8,128)(2,1)S(1)} %collective-permute-done.2.refs_1_), channel_id=1, source_target_pairs={{0,1},{1,0},{2,3},{3,2},{4,5},{5,4},{6,7},{7,6},{8,9},{9,8},{10,11... | collective-permute-start | bytes 239624 | tf_op jit(solution)/shard_map/ppermute | solution.py:364
  15.1 3.5 %collective-permute-start.8 = (bf16[13,24,128]{2,1,0:T(8,128)(2,1)S(1)}, bf16[13,24,128]{2,1,0:T(8,128)(2,1)S(1)}, u32[]{:S(2)}, u32[]{:S(2)}) collective-permute-start(bf16[13,24,128]{2,1,0:T(8,128)(2,1)S(1)} %collective-permute-done.4.refs_3_), channel_id=1, source_target_pairs={{0,1},{1,0},{2,3},{3,2},{4,5},{5,4},{6,7},{7,6},{8,9},{9,8},{10,11... | collective-permute-start | bytes 239624 | tf_op jit(solution)/shard_map/ppermute | solution.py:364
  16.2 3.3 %collective-permute-start.7 = (bf16[13,24,128]{2,1,0:T(8,128)(2,1)S(1)}, bf16[13,24,128]{2,1,0:T(8,128)(2,1)S(1)}, u32[]{:S(2)}, u32[]{:S(2)}) collective-permute-start(bf16[13,24,128]{2,1,0:T(8,128)(2,1)S(1)} %collective-permute-done.3.refs_2_), channel_id=1, source_target_pairs={{0,1},{1,0},{2,3},{3,2},{4,5},{5,4},{6,7},{7,6},{8,9},{9,8},{10,11... | collective-permute-start | bytes 239624 | tf_op jit(solution)/shard_map/ppermute | solution.py:364
  25.4 8.8 %collective-permute-start.9 = (bf16[8,24,128]{2,1,0:T(8,128)(2,1)S(1)}, bf16[8,24,128]{2,1,0:T(8,128)(2,1)S(1)}, u32[]{:S(2)}, u32[]{:S(2)}) collective-permute-start(bf16[8,24,128]{2,1,0:T(8,128)(2,1)S(1)} %get-tuple-element.28), channel_id=1, source_target_pairs={{0,1},{1,0},{2,3},{3,2},{4,5},{5,4},{6,7},{7,6},{8,9},{9,8},{10,11... | collective-permute-start | bytes 147464 | tf_op jit(solution)/shard_map/ppermute | solution.py:364
  25.9 18.5 %all-to-all-start = ((f32[128,2,128]{2,1,0:T(2,128)}), f32[128,2,128]{2,1,0:T(2,128)S(1)}, u32[]{:S(2)}, u32[]{:S(2)}) async-start(f32[128,2,128]{2,1,0:T(2,128)} %get-tuple-element.31), calls=%async_computation | async-start | bytes 262144 | tf_op jit(solution)/shard_map/all_to_all | solution.py:427
  34.3 6.5 %collective-permute-start.12 = (bf16[4,24,128]{2,1,0:T(8,128)(2,1)S(1)}, bf16[4,24,128]{2,1,0:T(8,128)(2,1)S(1)}, u32[]{:S(2)}, u32[]{:S(2)}) collective-permute-start(bf16[4,24,128]{2,1,0:T(8,128)(2,1)S(1)} %shard_map.88.refs_0_), channel_id=1, source_target_pairs={{0,4},{1,5},{2,6},{3,7},{4,0},{5,1},{6,2},{7,3},{8,12},{9,13},{10,... | collective-permute-start | bytes 73736 | tf_op jit(solution)/shard_map/ppermute | solution.py:431
  37.3 3.5 %collective-permute-start.10 = (bf16[4,24,128]{2,1,0:T(8,128)(2,1)S(1)}, bf16[4,24,128]{2,1,0:T(8,128)(2,1)S(1)}, u32[]{:S(2)}, u32[]{:S(2)}) collective-permute-start(bf16[4,24,128]{2,1,0:T(8,128)(2,1)S(1)} %get-tuple-element.29), channel_id=1, source_target_pairs={{0,2},{1,7},{2,4},{3,1},{4,6},{5,3},{6,0},{7,5},{8,10},{9,15},{10,... | collective-permute-start | bytes 73736 | tf_op jit(solution)/shard_map/ppermute | solution.py:435
  38.1 4.8 %collective-permute-start.11 = (bf16[4,24,128]{2,1,0:T(8,128)(2,1)S(1)}, bf16[4,24,128]{2,1,0:T(8,128)(2,1)S(1)}, u32[]{:S(2)}, u32[]{:S(2)}) collective-permute-start(bf16[4,24,128]{2,1,0:T(8,128)(2,1)S(1)} %get-tuple-element.30), channel_id=1, source_target_pairs={{0,3},{1,6},{2,5},{3,0},{4,7},{5,2},{6,1},{7,4},{8,11},{9,14},{10,... | collective-permute-start | bytes 73736 | tf_op jit(solution)/shard_map/ppermute | solution.py:436

commit v9 on v6

--- a/solution.py
+++ b/solution.py
@@ -267,7 +267,7 @@
     placed = jnp.where(quarter == 0, sums, 0.0)
     for i in range(1, 4):
         placed = placed + jnp.where(quarter == i, pltpu.roll(sums, SHARE * i, 1), 0.0)
-    packed = jnp.concatenate([jnp.sum(placed[4 * i : 4 * i + 4], axis=0, keepdims=True) for i in range(2)], axis=0)
+    packed = jnp.concatenate([jnp.sum(placed[4 * i : 4 * i + 4], axis=0, keepdims=True) for i in range(2)], axis=1)
     for i in range(sums_ref.shape[0]):
         fanned[i] = packed
     sending = pltpu.make_async_copy(fanned, sums_ref, sem)
@@ -326,7 +326,7 @@
         partial[i % 8] = partial[i % 8] + sums_ref[i]
     while len(partial) > 1:
         partial = [x + y for x, y in zip(partial[0::2], partial[1::2])]
-    placed = partial[0]
+    placed = jnp.concatenate([partial[0][:, 0:CH], partial[0][:, CH:]], axis=0)
     total = jnp.concatenate(
         [pltpu.roll(jnp.broadcast_to(placed[g // 4 : g // 4 + 1], (8, CH)), (CH - SHARE * (g % 4)) % CH, 1)[0:1] for g in range(8)],
         axis=0,
@@ -405,7 +405,7 @@
     half = jax.ShapeDtypeStruct((8, TILE, CH), BF16)
     sums, kept, given = pl.pallas_call(
         main_kernel,
-        out_shape=(jax.ShapeDtypeStruct((others, 2, CH), F32), half, half),
+        out_shape=(jax.ShapeDtypeStruct((others, 1, 2 * CH), F32), half, half),
         out_specs=(pl.BlockSpec(memory_space=pltpu.HBM), pl.BlockSpec(memory_space=pltpu.VMEM), pl.BlockSpec(memory_space=pltpu.VMEM)),
         scratch_shapes=(
             pltpu.VMEM((5, WT + 16, CH), F32),
@@ -421,7 +421,7 @@
             pltpu.VMEM((6, WT + 16, CH), F32),
             pltpu.VMEM((5, JP, CH), F32),
             pltpu.VMEM((WA, 2, TILE, CH), BF16),
-            pltpu.VMEM((others, 2, CH), F32),
+            pltpu.VMEM((others, 1, 2 * CH), F32),
             pltpu.SemaphoreType.DMA,
         ),
         compiler_params=VMEM,

time: 45.7 us -> 45.7 us (level)
  no operation moved by 1% of the time
where the time goes in v9:
time: 45.7 us; the launch traced here: 45.5 us
  starting transfers between devices  31.1 us (68%)
  Pallas kernels  8.02 us (18%)
  waiting for transfers between devices  5.72 us (13%)
  between operations  0.69 us (2%)
    all_to_all x1, starting transfers between devices, shards(): sums = lax.all_to_all(sums, ('dp', 'ha', 'wa'), 0, 0, tiled=True)  9.22 us
    pallas_call x1, Pallas kernels, shards(): pl.pallas_call(main_kernel, out_shape=(jax.ShapeDtypeStruct((others, 1, 2...  5.92 us
    ppermute x4, starting transfers between devices, shards(): lax.ppermute(value, 'wa', [(i, i ^ 1) for i in range(WA)])  5.36 us
    ppermute x3, starting transfers between devices, shards(): lax.ppermute(blocks[hop], 'wa', [(i, (i + 2 * hop) % WA) for i in range(W...  4.88 us
    ppermute x1, starting transfers between devices, shards(): lax.ppermute(opposite, 'wa', [(i, (i + 4) % WA) for i in range(WA)])  2.97 us
    ppermute x1, starting transfers between devices, shards(): lax.ppermute(beside_other, 'wa', [(i, (i + 3 - 6 * (i % 2)) % WA) for i i...  2.6 us
    ppermute x1, starting transfers between devices, shards(): lax.ppermute(up, 'ha', [(i, (i + 1) % ha_count) for i in range(ha_count)])  2.54 us
    ppermute x1, starting transfers between devices, shards(): lax.ppermute(down, 'ha', [((i + 1) % ha_count, i) for i in range(ha_count)])  2.2 us
  transfers between devices with their start and end apart: 14, of which 4 were waited for; matrix products, arithmetic and copies ran while one was open for 0% of the time, Pallas kernels for 0%

profile of v9, /device:TPU:1, one launch (start us, length us, event | category | flops | bytes accessed | tf_op | source)
XLA Modules:
  0.0 45.5 jit_solution(16826218343600284173)
XLA Ops:
  0.6 1.1 %shard_map.84 = (bf16[5,24,128]{2,1,0:T(8,128)(2,1)S(1)}, bf16[5,24,128]{2,1,0:T(8,128)(2,1)S(1)}, bf16[17,24,128]{2,1,0:T(8,128)(2,1)S(1)}, f32[3,16,128]{2,1,0:T(8,128)S(1)}) custom-call(bf16[8,24,128]{2,1,0:T(8,128)(2,1)} %bitcast.9, bf16[8,24,128]{2,1,0:T(8,128)(2,1)} %bitcast.10, s32[8,24]{1,0:T(8,128)} %bitcast.12, s32[8,24]{1,0:T(8,128)} %bitcast.13, ...), custom_call_target="tpu_custom_call" | custom-call | tf_op jit(solution)/shard_map/pallas_call | solution.py:374
  1.8 2.5 %collective-permute-start = (bf16[5,24,128]{2,1,0:T(8,128)(2,1)S(1)}, bf16[5,24,128]{2,1,0:T(8,128)(2,1)S(1)}, u32[]{:S(2)}, u32[]{:S(2)}) collective-permute-start(bf16[5,24,128]{2,1,0:T(8,128)(2,1)S(1)} %get-tuple-element.22), channel_id=1, source_target_pairs={{0,8},{8,16},{16,24},{24,0},{1,9},{9,17},{17,25},{25,1},{2,10},{10... | collective-permute-start | bytes 92168 | tf_op jit(solution)/shard_map/ppermute | solution.py:388
  4.3 2.2 %collective-permute-start.1 = (bf16[5,24,128]{2,1,0:T(8,128)(2,1)S(1)}, bf16[5,24,128]{2,1,0:T(8,128)(2,1)S(1)}, u32[]{:S(2)}, u32[]{:S(2)}) collective-permute-start(bf16[5,24,128]{2,1,0:T(8,128)(2,1)S(1)} %get-tuple-element.23), channel_id=1, source_target_pairs={{8,0},{16,8},{24,16},{0,24},{9,1},{17,9},{25,17},{1,25},{10,2},{18... | collective-permute-start | bytes 92168 | tf_op jit(solution)/shard_map/ppermute | solution.py:389
  6.5 1.2 %collective-permute-done.prev_ref = bf16[5,24,128]{2,1,0:T(8,128)(2,1)S(1)} collective-permute-done((bf16[5,24,128]{2,1,0:T(8,128)(2,1)S(1)}, bf16[5,24,128]{2,1,0:T(8,128)(2,1)S(1)}, u32[]{:S(2)}, u32[]{:S(2)}) %collective-permute-start) | collective-permute-done | bytes 30752 | tf_op jit(solution)/shard_map/ppermute | solution.py:388
  7.8 1.3 %collective-permute-start.2 = (bf16[13,24,128]{2,1,0:T(8,128)(2,1)S(1)}, bf16[13,24,128]{2,1,0:T(8,128)(2,1)S(1)}, u32[]{:S(2)}, u32[]{:S(2)}) collective-permute-start(bf16[13,24,128]{2,1,0:T(8,128)(2,1)S(1)} %get-tuple-element.25), channel_id=1, source_target_pairs={{0,2},{1,3},{2,4},{3,5},{4,6},{5,7},{6,0},{7,1},{8,10},{9,11},{10,... | collective-permute-start | bytes 239624 | tf_op jit(solution)/shard_map/ppermute | solution.py:401
  9.1 2.5 %collective-permute-start.3 = (bf16[13,24,128]{2,1,0:T(8,128)(2,1)S(1)}, bf16[13,24,128]{2,1,0:T(8,128)(2,1)S(1)}, u32[]{:S(2)}, u32[]{:S(2)}) collective-permute-start(bf16[13,24,128]{2,1,0:T(8,128)(2,1)S(1)} %get-tuple-element.26), channel_id=1, source_target_pairs={{0,4},{1,5},{2,6},{3,7},{4,0},{5,1},{6,2},{7,3},{8,12},{9,13},{10,... | collective-permute-start | bytes 239624 | tf_op jit(solution)/shard_map/ppermute | solution.py:401
  11.5 1.2 %collective-permute-start.4 = (bf16[13,24,128]{2,1,0:T(8,128)(2,1)S(1)}, bf16[13,24,128]{2,1,0:T(8,128)(2,1)S(1)}, u32[]{:S(2)}, u32[]{:S(2)}) collective-permute-start(bf16[13,24,128]{2,1,0:T(8,128)(2,1)S(1)} %get-tuple-element.27), channel_id=1, source_target_pairs={{0,6},{1,7},{2,0},{3,1},{4,2},{5,3},{6,4},{7,5},{8,14},{9,15},{10,... | collective-permute-start | bytes 239624 | tf_op jit(solution)/shard_map/ppermute | solution.py:401
  12.7 2.4 %collective-permute-start.5 = (bf16[13,24,128]{2,1,0:T(8,128)(2,1)S(1)}, bf16[13,24,128]{2,1,0:T(8,128)(2,1)S(1)}, u32[]{:S(2)}, u32[]{:S(2)}) collective-permute-start(bf16[13,24,128]{2,1,0:T(8,128)(2,1)S(1)} %get-tuple-element.24.refs_0_), channel_id=1, source_target_pairs={{0,1},{1,0},{2,3},{3,2},{4,5},{5,4},{6,7},{7,6},{8,9},{9,8},{10,11... | collective-permute-start | bytes 239624 | tf_op jit(solution)/shard_map/ppermute | solution.py:402
  15.1 0.7 %collective-permute-start.6 = (bf16[13,24,128]{2,1,0:T(8,128)(2,1)S(1)}, bf16[13,24,128]{2,1,0:T(8,128)(2,1)S(1)}, u32[]{:S(2)}, u32[]{:S(2)}) collective-permute-start(bf16[13,24,128]{2,1,0:T(8,128)(2,1)S(1)} %collective-permute-done.2.refs_1_), channel_id=1, source_target_pairs={{0,1},{1,0},{2,3},{3,2},{4,5},{5,4},{6,7},{7,6},{8,9},{9,8},{10,11... | collective-permute-start | bytes 239624 | tf_op jit(solution)/shard_map/ppermute | solution.py:402
  15.7 0.0 collective-permute-done.3.refs_2_
  15.7 1.1 %collective-permute-start.7 = (bf16[13,24,128]{2,1,0:T(8,128)(2,1)S(1)}, bf16[13,24,128]{2,1,0:T(8,128)(2,1)S(1)}, u32[]{:S(2)}, u32[]{:S(2)}) collective-permute-start(bf16[13,24,128]{2,1,0:T(8,128)(2,1)S(1)} %collective-permute-done.3.refs_2_), channel_id=1, source_target_pairs={{0,1},{1,0},{2,3},{3,2},{4,5},{5,4},{6,7},{7,6},{8,9},{9,8},{10,11... | collective-permute-start | bytes 239624 | tf_op jit(solution)/shard_map/ppermute | solution.py:402
  16.9 1.2 %collective-permute-start.8 = (bf16[13,24,128]{2,1,0:T(8,128)(2,1)S(1)}, bf16[13,24,128]{2,1,0:T(8,128)(2,1)S(1)}, u32[]{:S(2)}, u32[]{:S(2)}) collective-permute-start(bf16[13,24,128]{2,1,0:T(8,128)(2,1)S(1)} %collective-permute-done.4.refs_3_), channel_id=1, source_target_pairs={{0,1},{1,0},{2,3},{3,2},{4,5},{5,4},{6,7},{7,6},{8,9},{9,8},{10,11... | collective-permute-start | bytes 239624 | tf_op jit(solution)/shard_map/ppermute | solution.py:402
  18.0 0.0 collective-permute-done.5.refs_4_
  18.0 0.0 collective-permute-done.6.refs_5_
  18.1 0.9 %collective-permute-done.8.refs_7_ = bf16[13,24,128]{2,1,0:T(8,128)(2,1)S(1)} collective-permute-done((bf16[13,24,128]{2,1,0:T(8,128)(2,1)S(1)}, bf16[13,24,128]{2,1,0:T(8,128)(2,1)S(1)}, u32[]{:S(2)}, u32[]{:S(2)}) %collective-permute-start.8) | collective-permute-done | bytes 79904 | tf_op jit(solution)/shard_map/ppermute | solution.py:402
  19.0 5.9 %shard_map.86 = (f32[128,1,256]{2,1,0:T(1,128)}, bf16[8,24,128]{2,1,0:T(8,128)(2,1)S(1)}, bf16[8,24,128]{2,1,0:T(8,128)(2,1)S(1)}) custom-call(bf16[13,24,128]{2,1,0:T(8,128)(2,1)S(1)} %get-tuple-element.24.refs_0_, bf16[13,24,128]{2,1,0:T(8,128)(2,1)S(1)} %collective-permute-done.2.refs_1_, bf16[13,24,128]{2,1,0:T(8,128)(2,1)S(1)} %collective-permute-done.3.refs_2_, ...), custom_call_target="tpu_custom_call" | custom-call | flops 5368709120 | bytes 1048576 | tf_op jit(solution)/shard_map/pallas_call | solution.py:406
  24.9 0.4 collective-permute-start.9
  25.3 9.2 %all-to-all-start = ((f32[128,1,256]{2,1,0:T(1,128)}), f32[128,1,256]{2,1,0:T(1,128)S(1)}, u32[]{:S(2)}, u32[]{:S(2)}) async-start(f32[128,1,256]{2,1,0:T(1,128)} %get-tuple-element.33), calls=%async_computation | async-start | bytes 262144 | tf_op jit(solution)/shard_map/all_to_all | solution.py:430
  34.6 3.0 %collective-permute-start.12 = (bf16[4,24,128]{2,1,0:T(8,128)(2,1)S(1)}, bf16[4,24,128]{2,1,0:T(8,128)(2,1)S(1)}, u32[]{:S(2)}, u32[]{:S(2)}) collective-permute-start(bf16[4,24,128]{2,1,0:T(8,128)(2,1)S(1)} %shard_map.87.refs_0_), channel_id=1, source_target_pairs={{0,4},{1,5},{2,6},{3,7},{4,0},{5,1},{6,2},{7,3},{8,12},{9,13},{10,... | collective-permute-start | bytes 73736 | tf_op jit(solution)/shard_map/ppermute | solution.py:434
  37.5 0.9 %collective-permute-start.10 = (bf16[4,24,128]{2,1,0:T(8,128)(2,1)S(1)}, bf16[4,24,128]{2,1,0:T(8,128)(2,1)S(1)}, u32[]{:S(2)}, u32[]{:S(2)}) collective-permute-start(bf16[4,24,128]{2,1,0:T(8,128)(2,1)S(1)} %get-tuple-element.31), channel_id=1, source_target_pairs={{0,2},{1,7},{2,4},{3,1},{4,6},{5,3},{6,0},{7,5},{8,10},{9,15},{10,... | collective-permute-start | bytes 73736 | tf_op jit(solution)/shard_map/ppermute | solution.py:438
  38.4 2.6 %collective-permute-start.11 = (bf16[4,24,128]{2,1,0:T(8,128)(2,1)S(1)}, bf16[4,24,128]{2,1,0:T(8,128)(2,1)S(1)}, u32[]{:S(2)}, u32[]{:S(2)}) collective-permute-start(bf16[4,24,128]{2,1,0:T(8,128)(2,1)S(1)} %get-tuple-element.32), channel_id=1, source_target_pairs={{0,3},{1,6},{2,5},{3,0},{4,7},{5,2},{6,1},{7,4},{8,11},{9,14},{10,... | collective-permute-start | bytes 73736 | tf_op jit(solution)/shard_map/ppermute | solution.py:439
  41.0 2.2 %collective-permute-done.11.far = bf16[4,24,128]{2,1,0:T(8,128)(2,1)S(1)} collective-permute-done((bf16[4,24,128]{2,1,0:T(8,128)(2,1)S(1)}, bf16[4,24,128]{2,1,0:T(8,128)(2,1)S(1)}, u32[]{:S(2)}, u32[]{:S(2)}) %collective-permute-start.11) | collective-permute-done | bytes 24608 | tf_op jit(solution)/shard_map/ppermute | solution.py:439
  43.2 1.4 %all-to-all-done.sums_ref = f32[128,1,256]{2,1,0:T(1,128)S(1)} async-done(((f32[128,1,256]{2,1,0:T(1,128)}), f32[128,1,256]{2,1,0:T(1,128)S(1)}, u32[]{:S(2)}, u32[]{:S(2)}) %all-to-all-start) | async-done | bytes 131104 | tf_op jit(solution)/shard_map/all_to_all | solution.py:430
  44.6 0.9 %shard_map.89 = (f32[8,24,128]{2,1,0:T(8,128)}, f32[8,24,128]{2,1,0:T(8,128)}, f32[3,3,3,8]{3,2,1,0:T(4,128)}, f32[1,1]{1,0:T(1,128)}) custom-call(bf16[8,24,128]{2,1,0:T(8,128)(2,1)S(1)} %get-tuple-element.29.kept_ref.kept, bf16[8,24,128]{2,1,0:T(8,128)(2,1)S(1)} %collective-permute-done.9.got_ref.got, ...), custom_call_target="tpu_custom_call" | custom-call | bytes 1048576 | tf_op jit(solution)/shard_map/pallas_call | solution.py:358
  (10 shorter events, 0.1 us)
Async XLA Ops:
  1.8 5.9 %collective-permute-start = (bf16[5,24,128]{2,1,0:T(8,128)(2,1)S(1)}, bf16[5,24,128]{2,1,0:T(8,128)(2,1)S(1)}, u32[]{:S(2)}, u32[]{:S(2)}) collective-permute-start(bf16[5,24,128]{2,1,0:T(8,128)(2,1)S(1)} %get-tuple-element.22), channel_id=1, source_target_pairs={{0,8},{8,16},{16,24},{24,0},{1,9},{9,17},{17,25},{25,1},{2,10},{10... | collective-permute-start | bytes 92168 | tf_op jit(solution)/shard_map/ppermute | solution.py:388
  4.3 3.4 %collective-permute-start.1 = (bf16[5,24,128]{2,1,0:T(8,128)(2,1)S(1)}, bf16[5,24,128]{2,1,0:T(8,128)(2,1)S(1)}, u32[]{:S(2)}, u32[]{:S(2)}) collective-permute-start(bf16[5,24,128]{2,1,0:T(8,128)(2,1)S(1)} %get-tuple-element.23), channel_id=1, source_target_pairs={{8,0},{16,8},{24,16},{0,24},{9,1},{17,9},{25,17},{1,25},{10,2},{18... | collective-permute-start | bytes 92168 | tf_op jit(solution)/shard_map/ppermute | solution.py:389
  7.8 7.3 %collective-permute-start.2 = (bf16[13,24,128]{2,1,0:T(8,128)(2,1)S(1)}, bf16[13,24,128]{2,1,0:T(8,128)(2,1)S(1)}, u32[]{:S(2)}, u32[]{:S(2)}) collective-permute-start(bf16[13,24,128]{2,1,0:T(8,128)(2,1)S(1)} %get-tuple-element.25), channel_id=1, source_target_pairs={{0,2},{1,3},{2,4},{3,5},{4,6},{5,7},{6,0},{7,1},{8,10},{9,11},{10,... | collective-permute-start | bytes 239624 | tf_op jit(solution)/shard_map/ppermute | solution.py:401
  9.1 6.7 %collective-permute-start.3 = (bf16[13,24,128]{2,1,0:T(8,128)(2,1)S(1)}, bf16[13,24,128]{2,1,0:T(8,128)(2,1)S(1)}, u32[]{:S(2)}, u32[]{:S(2)}) collective-permute-start(bf16[13,24,128]{2,1,0:T(8,128)(2,1)S(1)} %get-tuple-element.26), channel_id=1, source_target_pairs={{0,4},{1,5},{2,6},{3,7},{4,0},{5,1},{6,2},{7,3},{8,12},{9,13},{10,... | collective-permute-start | bytes 239624 | tf_op jit(solution)/shard_map/ppermute | solution.py:401
  11.5 5.4 %collective-permute-start.4 = (bf16[13,24,128]{2,1,0:T(8,128)(2,1)S(1)}, bf16[13,24,128]{2,1,0:T(8,128)(2,1)S(1)}, u32[]{:S(2)}, u32[]{:S(2)}) collective-permute-start(bf16[13,24,128]{2,1,0:T(8,128)(2,1)S(1)} %get-tuple-element.27), channel_id=1, source_target_pairs={{0,6},{1,7},{2,0},{3,1},{4,2},{5,3},{6,4},{7,5},{8,14},{9,15},{10,... | collective-permute-start | bytes 239624 | tf_op jit(solution)/shard_map/ppermute | solution.py:401
  12.7 5.4 %collective-permute-start.5 = (bf16[13,24,128]{2,1,0:T(8,128)(2,1)S(1)}, bf16[13,24,128]{2,1,0:T(8,128)(2,1)S(1)}, u32[]{:S(2)}, u32[]{:S(2)}) collective-permute-start(bf16[13,24,128]{2,1,0:T(8,128)(2,1)S(1)} %get-tuple-element.24.refs_0_), channel_id=1, source_target_pairs={{0,1},{1,0},{2,3},{3,2},{4,5},{5,4},{6,7},{7,6},{8,9},{9,8},{10,11... | collective-permute-start | bytes 239624 | tf_op jit(solution)/shard_map/ppermute | solution.py:402
  15.1 3.0 %collective-permute-start.6 = (bf16[13,24,128]{2,1,0:T(8,128)(2,1)S(1)}, bf16[13,24,128]{2,1,0:T(8,128)(2,1)S(1)}, u32[]{:S(2)}, u32[]{:S(2)}) collective-permute-start(bf16[13,24,128]{2,1,0:T(8,128)(2,1)S(1)} %collective-permute-done.2.refs_1_), channel_id=1, source_target_pairs={{0,1},{1,0},{2,3},{3,2},{4,5},{5,4},{6,7},{7,6},{8,9},{9,8},{10,11... | collective-permute-start | bytes 239624 | tf_op jit(solution)/shard_map/ppermute | solution.py:402
  15.7 2.3 %collective-permute-start.7 = (bf16[13,24,128]{2,1,0:T(8,128)(2,1)S(1)}, bf16[13,24,128]{2,1,0:T(8,128)(2,1)S(1)}, u32[]{:S(2)}, u32[]{:S(2)}) collective-permute-start(bf16[13,24,128]{2,1,0:T(8,128)(2,1)S(1)} %collective-permute-done.3.refs_2_), channel_id=1, source_target_pairs={{0,1},{1,0},{2,3},{3,2},{4,5},{5,4},{6,7},{7,6},{8,9},{9,8},{10,11... | collective-permute-start | bytes 239624 | tf_op jit(solution)/shard_map/ppermute | solution.py:402
  16.9 2.1 %collective-permute-start.8 = (bf16[13,24,128]{2,1,0:T(8,128)(2,1)S(1)}, bf16[13,24,128]{2,1,0:T(8,128)(2,1)S(1)}, u32[]{:S(2)}, u32[]{:S(2)}) collective-permute-start(bf16[13,24,128]{2,1,0:T(8,128)(2,1)S(1)} %collective-permute-done.4.refs_3_), channel_id=1, source_target_pairs={{0,1},{1,0},{2,3},{3,2},{4,5},{5,4},{6,7},{7,6},{8,9},{9,8},{10,11... | collective-permute-start | bytes 239624 | tf_op jit(solution)/shard_map/ppermute | solution.py:402
  24.9 9.7 %collective-permute-start.9 = (bf16[8,24,128]{2,1,0:T(8,128)(2,1)S(1)}, bf16[8,24,128]{2,1,0:T(8,128)(2,1)S(1)}, u32[]{:S(2)}, u32[]{:S(2)}) collective-permute-start(bf16[8,24,128]{2,1,0:T(8,128)(2,1)S(1)} %get-tuple-element.30), channel_id=1, source_target_pairs={{0,1},{1,0},{2,3},{3,2},{4,5},{5,4},{6,7},{7,6},{8,9},{9,8},{10,11... | collective-permute-start | bytes 147464 | tf_op jit(solution)/shard_map/ppermute | solution.py:364
  25.3 19.3 %all-to-all-start = ((f32[128,1,256]{2,1,0:T(1,128)}), f32[128,1,256]{2,1,0:T(1,128)S(1)}, u32[]{:S(2)}, u32[]{:S(2)}) async-start(f32[128,1,256]{2,1,0:T(1,128)} %get-tuple-element.33), calls=%async_computation | async-start | bytes 262144 | tf_op jit(solution)/shard_map/all_to_all | solution.py:430
  34.6 6.5 %collective-permute-start.12 = (bf16[4,24,128]{2,1,0:T(8,128)(2,1)S(1)}, bf16[4,24,128]{2,1,0:T(8,128)(2,1)S(1)}, u32[]{:S(2)}, u32[]{:S(2)}) collective-permute-start(bf16[4,24,128]{2,1,0:T(8,128)(2,1)S(1)} %shard_map.87.refs_0_), channel_id=1, source_target_pairs={{0,4},{1,5},{2,6},{3,7},{4,0},{5,1},{6,2},{7,3},{8,12},{9,13},{10,... | collective-permute-start | bytes 73736 | tf_op jit(solution)/shard_map/ppermute | solution.py:434
  37.5 3.5 %collective-permute-start.10 = (bf16[4,24,128]{2,1,0:T(8,128)(2,1)S(1)}, bf16[4,24,128]{2,1,0:T(8,128)(2,1)S(1)}, u32[]{:S(2)}, u32[]{:S(2)}) collective-permute-start(bf16[4,24,128]{2,1,0:T(8,128)(2,1)S(1)} %get-tuple-element.31), channel_id=1, source_target_pairs={{0,2},{1,7},{2,4},{3,1},{4,6},{5,3},{6,0},{7,5},{8,10},{9,15},{10,... | collective-permute-start | bytes 73736 | tf_op jit(solution)/shard_map/ppermute | solution.py:438
  38.4 4.8 %collective-permute-start.11 = (bf16[4,24,128]{2,1,0:T(8,128)(2,1)S(1)}, bf16[4,24,128]{2,1,0:T(8,128)(2,1)S(1)}, u32[]{:S(2)}, u32[]{:S(2)}) collective-permute-start(bf16[4,24,128]{2,1,0:T(8,128)(2,1)S(1)} %get-tuple-element.32), channel_id=1, source_target_pairs={{0,3},{1,6},{2,5},{3,0},{4,7},{5,2},{6,1},{7,4},{8,11},{9,14},{10,... | collective-permute-start | bytes 73736 | tf_op jit(solution)/shard_map/ppermute | solution.py:439

commit v10 on v7

--- a/solution.py
+++ b/solution.py
@@ -277,7 +277,7 @@
     placed = jnp.where(quarter == 0, sums, 0.0)
     for i in range(1, 4):
         placed = placed + jnp.where(quarter == i, pltpu.roll(sums, SHARE * i, 1), 0.0)
-    packed = jnp.concatenate([jnp.sum(placed[4 * i : 4 * i + 4], axis=0, keepdims=True) for i in range(2)], axis=0)
+    packed = jnp.concatenate([jnp.sum(placed[4 * i : 4 * i + 4], axis=0, keepdims=True) for i in range(2)], axis=1)
     for i in range(sums_ref.shape[0]):
         fanned[i] = packed
     sending = pltpu.make_async_copy(fanned, sums_ref, sem)
@@ -336,7 +336,7 @@
         partial[i % 8] = partial[i % 8] + sums_ref[i]
     while len(partial) > 1:
         partial = [x + y for x, y in zip(partial[0::2], partial[1::2])]
-    placed = partial[0]
+    placed = jnp.concatenate([partial[0][:, 0:CH], partial[0][:, CH:]], axis=0)
     total = jnp.concatenate(
         [pltpu.roll(jnp.broadcast_to(placed[g // 4 : g // 4 + 1], (8, CH)), (CH - SHARE * (g % 4)) % CH, 1)[0:1] for g in range(8)],
         axis=0,
@@ -424,7 +424,7 @@
     half = jax.ShapeDtypeStruct((8, TILE, CH), BF16)
     sums, kept, given = pl.pallas_call(
         main_kernel,
-        out_shape=(jax.ShapeDtypeStruct((others, 2, CH), F32), half, half),
+        out_shape=(jax.ShapeDtypeStruct((others, 1, 2 * CH), F32), half, half),
         out_specs=(pl.BlockSpec(memory_space=pltpu.HBM), pl.BlockSpec(memory_space=pltpu.VMEM), pl.BlockSpec(memory_space=pltpu.VMEM)),
         scratch_shapes=(
             pltpu.VMEM((5, WT + 16, CH), F32),
@@ -440,7 +440,7 @@
             pltpu.VMEM((6, WT + 16, CH), F32),
             pltpu.VMEM((5, JP, CH), F32),
             pltpu.VMEM((WA, 2, TILE, CH), BF16),
-            pltpu.VMEM((others, 2, CH), F32),
+            pltpu.VMEM((others, 1, 2 * CH), F32),
             pltpu.SemaphoreType.DMA,
         ),
         compiler_params=VMEM,

time: 45.7 us -> 45.7 us (level)
  no operation moved by 1% of the time
where the time goes in v10:
time: 45.7 us; the launch traced here: 45.4 us
  starting transfers between devices  31.1 us (68%)
  Pallas kernels  9.03 us (20%)
  waiting for transfers between devices  4.62 us (10%)
  between operations  0.7 us (2%)
    all_to_all x1, starting transfers between devices, shards(): sums = lax.all_to_all(sums, ('dp', 'ha', 'wa'), 0, 0, tiled=True)  9.22 us
    pallas_call x1, Pallas kernels, shards(): pl.pallas_call(main_kernel, out_shape=(jax.ShapeDtypeStruct((others, 1, 2...  5.92 us
    ppermute x4, starting transfers between devices, shards(): lax.ppermute(value, 'wa', [(i, i ^ 1) for i in range(WA)])  5.36 us
    ppermute x3, starting transfers between devices, shards(): lax.ppermute(blocks[hop], 'wa', [(i, (i + 2 * hop) % WA) for i in range(W...  4.89 us
    ppermute x1, starting transfers between devices, shards(): lax.ppermute(opposite, 'wa', [(i, (i + 4) % WA) for i in range(WA)])  2.97 us
    ppermute x1, starting transfers between devices, shards(): lax.ppermute(beside_other, 'wa', [(i, (i + 3 - 6 * (i % 2)) % WA) for i i...  2.6 us
    ppermute x1, starting transfers between devices, shards(): lax.ppermute(up, 'ha', [(i, (i + 1) % ha_count) for i in range(ha_count)])  2.54 us
    ppermute x1, starting transfers between devices, shards(): lax.ppermute(down, 'ha', [((i + 1) % ha_count, i) for i in range(ha_count)])  2.2 us
  transfers between devices with their start and end apart: 14, of which 4 were waited for; matrix products, arithmetic and copies ran while one was open for 0% of the time, Pallas kernels for 2%

profile of v10, /device:TPU:1, one launch (start us, length us, event | category | flops | bytes accessed | tf_op | source)
XLA Modules:
  0.0 45.4 jit_solution(2637781833198301727)
XLA Ops:
  0.6 1.1 %shard_map.85 = (bf16[5,24,128]{2,1,0:T(8,128)(2,1)S(1)}, bf16[5,24,128]{2,1,0:T(8,128)(2,1)S(1)}) custom-call(bf16[8,24,128]{2,1,0:T(8,128)(2,1)} %bitcast.9, bf16[8,24,128]{2,1,0:T(8,128)(2,1)} %bitcast.11, s32[8,24]{1,0:T(8,128)} %bitcast.13, s32[8,24]{1,0:T(8,128)} %bitcast.15), custom_call_target="tpu_custom_call" | custom-call | tf_op jit(solution)/shard_map/pallas_call | solution.py:392
  1.7 2.5 %collective-permute-start = (bf16[5,24,128]{2,1,0:T(8,128)(2,1)S(1)}, bf16[5,24,128]{2,1,0:T(8,128)(2,1)S(1)}, u32[]{:S(2)}, u32[]{:S(2)}) collective-permute-start(bf16[5,24,128]{2,1,0:T(8,128)(2,1)S(1)} %get-tuple-element.22), channel_id=1, source_target_pairs={{0,8},{8,16},{16,24},{24,0},{1,9},{9,17},{17,25},{25,1},{2,10},{10... | collective-permute-start | bytes 92168 | tf_op jit(solution)/shard_map/ppermute | solution.py:407
  4.2 2.2 %collective-permute-start.1 = (bf16[5,24,128]{2,1,0:T(8,128)(2,1)S(1)}, bf16[5,24,128]{2,1,0:T(8,128)(2,1)S(1)}, u32[]{:S(2)}, u32[]{:S(2)}) collective-permute-start(bf16[5,24,128]{2,1,0:T(8,128)(2,1)S(1)} %get-tuple-element.23), channel_id=1, source_target_pairs={{8,0},{16,8},{24,16},{0,24},{9,1},{17,9},{25,17},{1,25},{10,2},{18... | collective-permute-start | bytes 92168 | tf_op jit(solution)/shard_map/ppermute | solution.py:408
  6.4 1.1 %shard_map.84 = (bf16[17,24,128]{2,1,0:T(8,128)(2,1)S(1)}, f32[3,16,128]{2,1,0:T(8,128)S(1)}) custom-call(bf16[8,24,128]{2,1,0:T(8,128)(2,1)} %bitcast.10, bf16[8,24,128]{2,1,0:T(8,128)(2,1)} %bitcast.12, s32[8,24]{1,0:T(8,128)} %bitcast.14, s32[8,24]{1,0:T(8,128)} %bitcast.16, f32[3,3,3,8]{3,2,1,0:T(4,128)} %bitcast.19), custom_call_target="tpu_custom_call" | custom-call | flops 1073741824 | bytes 262144 | tf_op jit(solution)/shard_map/pallas_call | solution.py:399
  7.5 0.1 collective-permute-done.prev_ref
  7.6 0.0 collective-permute-done.1.next_ref
  7.7 1.3 %collective-permute-start.2 = (bf16[13,24,128]{2,1,0:T(8,128)(2,1)S(1)}, bf16[13,24,128]{2,1,0:T(8,128)(2,1)S(1)}, u32[]{:S(2)}, u32[]{:S(2)}) collective-permute-start(bf16[13,24,128]{2,1,0:T(8,128)(2,1)S(1)} %get-tuple-element.25), channel_id=1, source_target_pairs={{0,2},{1,3},{2,4},{3,5},{4,6},{5,7},{6,0},{7,1},{8,10},{9,11},{10,... | collective-permute-start | bytes 239624 | tf_op jit(solution)/shard_map/ppermute | solution.py:420
  9.0 2.5 %collective-permute-start.3 = (bf16[13,24,128]{2,1,0:T(8,128)(2,1)S(1)}, bf16[13,24,128]{2,1,0:T(8,128)(2,1)S(1)}, u32[]{:S(2)}, u32[]{:S(2)}) collective-permute-start(bf16[13,24,128]{2,1,0:T(8,128)(2,1)S(1)} %get-tuple-element.26), channel_id=1, source_target_pairs={{0,4},{1,5},{2,6},{3,7},{4,0},{5,1},{6,2},{7,3},{8,12},{9,13},{10,... | collective-permute-start | bytes 239624 | tf_op jit(solution)/shard_map/ppermute | solution.py:420
  11.4 1.2 %collective-permute-start.4 = (bf16[13,24,128]{2,1,0:T(8,128)(2,1)S(1)}, bf16[13,24,128]{2,1,0:T(8,128)(2,1)S(1)}, u32[]{:S(2)}, u32[]{:S(2)}) collective-permute-start(bf16[13,24,128]{2,1,0:T(8,128)(2,1)S(1)} %get-tuple-element.27), channel_id=1, source_target_pairs={{0,6},{1,7},{2,0},{3,1},{4,2},{5,3},{6,4},{7,5},{8,14},{9,15},{10,... | collective-permute-start | bytes 239624 | tf_op jit(solution)/shard_map/ppermute | solution.py:420
  12.6 2.4 %collective-permute-start.5 = (bf16[13,24,128]{2,1,0:T(8,128)(2,1)S(1)}, bf16[13,24,128]{2,1,0:T(8,128)(2,1)S(1)}, u32[]{:S(2)}, u32[]{:S(2)}) collective-permute-start(bf16[13,24,128]{2,1,0:T(8,128)(2,1)S(1)} %get-tuple-element.24.refs_0_), channel_id=1, source_target_pairs={{0,1},{1,0},{2,3},{3,2},{4,5},{5,4},{6,7},{7,6},{8,9},{9,8},{10,11... | collective-permute-start | bytes 239624 | tf_op jit(solution)/shard_map/ppermute | solution.py:421
  15.0 0.7 %collective-permute-start.6 = (bf16[13,24,128]{2,1,0:T(8,128)(2,1)S(1)}, bf16[13,24,128]{2,1,0:T(8,128)(2,1)S(1)}, u32[]{:S(2)}, u32[]{:S(2)}) collective-permute-start(bf16[13,24,128]{2,1,0:T(8,128)(2,1)S(1)} %collective-permute-done.2.refs_1_), channel_id=1, source_target_pairs={{0,1},{1,0},{2,3},{3,2},{4,5},{5,4},{6,7},{7,6},{8,9},{9,8},{10,11... | collective-permute-start | bytes 239624 | tf_op jit(solution)/shard_map/ppermute | solution.py:421
  15.6 0.0 collective-permute-done.3.refs_2_
  15.6 1.1 %collective-permute-start.7 = (bf16[13,24,128]{2,1,0:T(8,128)(2,1)S(1)}, bf16[13,24,128]{2,1,0:T(8,128)(2,1)S(1)}, u32[]{:S(2)}, u32[]{:S(2)}) collective-permute-start(bf16[13,24,128]{2,1,0:T(8,128)(2,1)S(1)} %collective-permute-done.3.refs_2_), channel_id=1, source_target_pairs={{0,1},{1,0},{2,3},{3,2},{4,5},{5,4},{6,7},{7,6},{8,9},{9,8},{10,11... | collective-permute-start | bytes 239624 | tf_op jit(solution)/shard_map/ppermute | solution.py:421
  16.8 1.2 %collective-permute-start.8 = (bf16[13,24,128]{2,1,0:T(8,128)(2,1)S(1)}, bf16[13,24,128]{2,1,0:T(8,128)(2,1)S(1)}, u32[]{:S(2)}, u32[]{:S(2)}) collective-permute-start(bf16[13,24,128]{2,1,0:T(8,128)(2,1)S(1)} %collective-permute-done.4.refs_3_), channel_id=1, source_target_pairs={{0,1},{1,0},{2,3},{3,2},{4,5},{5,4},{6,7},{7,6},{8,9},{9,8},{10,11... | collective-permute-start | bytes 239624 | tf_op jit(solution)/shard_map/ppermute | solution.py:421
  18.0 0.9 %collective-permute-done.8.refs_7_ = bf16[13,24,128]{2,1,0:T(8,128)(2,1)S(1)} collective-permute-done((bf16[13,24,128]{2,1,0:T(8,128)(2,1)S(1)}, bf16[13,24,128]{2,1,0:T(8,128)(2,1)S(1)}, u32[]{:S(2)}, u32[]{:S(2)}) %collective-permute-start.8) | collective-permute-done | bytes 79904 | tf_op jit(solution)/shard_map/ppermute | solution.py:421
  18.9 5.9 %shard_map.87 = (f32[128,1,256]{2,1,0:T(1,128)}, bf16[8,24,128]{2,1,0:T(8,128)(2,1)S(1)}, bf16[8,24,128]{2,1,0:T(8,128)(2,1)S(1)}) custom-call(bf16[13,24,128]{2,1,0:T(8,128)(2,1)S(1)} %get-tuple-element.24.refs_0_, bf16[13,24,128]{2,1,0:T(8,128)(2,1)S(1)} %collective-permute-done.2.refs_1_, bf16[13,24,128]{2,1,0:T(8,128)(2,1)S(1)} %collective-permute-done.3.refs_2_, ...), custom_call_target="tpu_custom_call" | custom-call | flops 5368709120 | bytes 1048576 | tf_op jit(solution)/shard_map/pallas_call | solution.py:425
  24.8 0.4 collective-permute-start.9
  25.2 9.2 %all-to-all-start = ((f32[128,1,256]{2,1,0:T(1,128)}), f32[128,1,256]{2,1,0:T(1,128)S(1)}, u32[]{:S(2)}, u32[]{:S(2)}) async-start(f32[128,1,256]{2,1,0:T(1,128)} %get-tuple-element.33), calls=%async_computation | async-start | bytes 262144 | tf_op jit(solution)/shard_map/all_to_all | solution.py:449
  34.5 3.0 %collective-permute-start.12 = (bf16[4,24,128]{2,1,0:T(8,128)(2,1)S(1)}, bf16[4,24,128]{2,1,0:T(8,128)(2,1)S(1)}, u32[]{:S(2)}, u32[]{:S(2)}) collective-permute-start(bf16[4,24,128]{2,1,0:T(8,128)(2,1)S(1)} %shard_map.88.refs_0_), channel_id=1, source_target_pairs={{0,4},{1,5},{2,6},{3,7},{4,0},{5,1},{6,2},{7,3},{8,12},{9,13},{10,... | collective-permute-start | bytes 73736 | tf_op jit(solution)/shard_map/ppermute | solution.py:453
  37.5 0.9 %collective-permute-start.10 = (bf16[4,24,128]{2,1,0:T(8,128)(2,1)S(1)}, bf16[4,24,128]{2,1,0:T(8,128)(2,1)S(1)}, u32[]{:S(2)}, u32[]{:S(2)}) collective-permute-start(bf16[4,24,128]{2,1,0:T(8,128)(2,1)S(1)} %get-tuple-element.31), channel_id=1, source_target_pairs={{0,2},{1,7},{2,4},{3,1},{4,6},{5,3},{6,0},{7,5},{8,10},{9,15},{10,... | collective-permute-start | bytes 73736 | tf_op jit(solution)/shard_map/ppermute | solution.py:457
  38.3 2.6 %collective-permute-start.11 = (bf16[4,24,128]{2,1,0:T(8,128)(2,1)S(1)}, bf16[4,24,128]{2,1,0:T(8,128)(2,1)S(1)}, u32[]{:S(2)}, u32[]{:S(2)}) collective-permute-start(bf16[4,24,128]{2,1,0:T(8,128)(2,1)S(1)} %get-tuple-element.32), channel_id=1, source_target_pairs={{0,3},{1,6},{2,5},{3,0},{4,7},{5,2},{6,1},{7,4},{8,11},{9,14},{10,... | collective-permute-start | bytes 73736 | tf_op jit(solution)/shard_map/ppermute | solution.py:458
  40.9 2.2 %collective-permute-done.11.far = bf16[4,24,128]{2,1,0:T(8,128)(2,1)S(1)} collective-permute-done((bf16[4,24,128]{2,1,0:T(8,128)(2,1)S(1)}, bf16[4,24,128]{2,1,0:T(8,128)(2,1)S(1)}, u32[]{:S(2)}, u32[]{:S(2)}) %collective-permute-start.11) | collective-permute-done | bytes 24608 | tf_op jit(solution)/shard_map/ppermute | solution.py:458
  43.1 1.4 %all-to-all-done.sums_ref = f32[128,1,256]{2,1,0:T(1,128)S(1)} async-done(((f32[128,1,256]{2,1,0:T(1,128)}), f32[128,1,256]{2,1,0:T(1,128)S(1)}, u32[]{:S(2)}, u32[]{:S(2)}) %all-to-all-start) | async-done | bytes 131104 | tf_op jit(solution)/shard_map/all_to_all | solution.py:449
  44.5 0.9 %shard_map.90 = (f32[8,24,128]{2,1,0:T(8,128)}, f32[8,24,128]{2,1,0:T(8,128)}, f32[3,3,3,8]{3,2,1,0:T(4,128)}, f32[1,1]{1,0:T(1,128)}) custom-call(bf16[8,24,128]{2,1,0:T(8,128)(2,1)S(1)} %get-tuple-element.29.kept_ref.kept, bf16[8,24,128]{2,1,0:T(8,128)(2,1)S(1)} %collective-permute-done.9.got_ref.got, ...), custom_call_target="tpu_custom_call" | custom-call | bytes 1048576 | tf_op jit(solution)/shard_map/pallas_call | solution.py:368
  (11 shorter events, 0.1 us)
Async XLA Ops:
  1.7 5.9 %collective-permute-start = (bf16[5,24,128]{2,1,0:T(8,128)(2,1)S(1)}, bf16[5,24,128]{2,1,0:T(8,128)(2,1)S(1)}, u32[]{:S(2)}, u32[]{:S(2)}) collective-permute-start(bf16[5,24,128]{2,1,0:T(8,128)(2,1)S(1)} %get-tuple-element.22), channel_id=1, source_target_pairs={{0,8},{8,16},{16,24},{24,0},{1,9},{9,17},{17,25},{25,1},{2,10},{10... | collective-permute-start | bytes 92168 | tf_op jit(solution)/shard_map/ppermute | solution.py:407
  4.2 3.4 %collective-permute-start.1 = (bf16[5,24,128]{2,1,0:T(8,128)(2,1)S(1)}, bf16[5,24,128]{2,1,0:T(8,128)(2,1)S(1)}, u32[]{:S(2)}, u32[]{:S(2)}) collective-permute-start(bf16[5,24,128]{2,1,0:T(8,128)(2,1)S(1)} %get-tuple-element.23), channel_id=1, source_target_pairs={{8,0},{16,8},{24,16},{0,24},{9,1},{17,9},{25,17},{1,25},{10,2},{18... | collective-permute-start | bytes 92168 | tf_op jit(solution)/shard_map/ppermute | solution.py:408
  7.7 7.3 %collective-permute-start.2 = (bf16[13,24,128]{2,1,0:T(8,128)(2,1)S(1)}, bf16[13,24,128]{2,1,0:T(8,128)(2,1)S(1)}, u32[]{:S(2)}, u32[]{:S(2)}) collective-permute-start(bf16[13,24,128]{2,1,0:T(8,128)(2,1)S(1)} %get-tuple-element.25), channel_id=1, source_target_pairs={{0,2},{1,3},{2,4},{3,5},{4,6},{5,7},{6,0},{7,1},{8,10},{9,11},{10,... | collective-permute-start | bytes 239624 | tf_op jit(solution)/shard_map/ppermute | solution.py:420
  9.0 6.7 %collective-permute-start.3 = (bf16[13,24,128]{2,1,0:T(8,128)(2,1)S(1)}, bf16[13,24,128]{2,1,0:T(8,128)(2,1)S(1)}, u32[]{:S(2)}, u32[]{:S(2)}) collective-permute-start(bf16[13,24,128]{2,1,0:T(8,128)(2,1)S(1)} %get-tuple-element.26), channel_id=1, source_target_pairs={{0,4},{1,5},{2,6},{3,7},{4,0},{5,1},{6,2},{7,3},{8,12},{9,13},{10,... | collective-permute-start | bytes 239624 | tf_op jit(solution)/shard_map/ppermute | solution.py:420
  11.4 5.4 %collective-permute-start.4 = (bf16[13,24,128]{2,1,0:T(8,128)(2,1)S(1)}, bf16[13,24,128]{2,1,0:T(8,128)(2,1)S(1)}, u32[]{:S(2)}, u32[]{:S(2)}) collective-permute-start(bf16[13,24,128]{2,1,0:T(8,128)(2,1)S(1)} %get-tuple-element.27), channel_id=1, source_target_pairs={{0,6},{1,7},{2,0},{3,1},{4,2},{5,3},{6,4},{7,5},{8,14},{9,15},{10,... | collective-permute-start | bytes 239624 | tf_op jit(solution)/shard_map/ppermute | solution.py:420
  12.6 5.4 %collective-permute-start.5 = (bf16[13,24,128]{2,1,0:T(8,128)(2,1)S(1)}, bf16[13,24,128]{2,1,0:T(8,128)(2,1)S(1)}, u32[]{:S(2)}, u32[]{:S(2)}) collective-permute-start(bf16[13,24,128]{2,1,0:T(8,128)(2,1)S(1)} %get-tuple-element.24.refs_0_), channel_id=1, source_target_pairs={{0,1},{1,0},{2,3},{3,2},{4,5},{5,4},{6,7},{7,6},{8,9},{9,8},{10,11... | collective-permute-start | bytes 239624 | tf_op jit(solution)/shard_map/ppermute | solution.py:421
  15.0 3.0 %collective-permute-start.6 = (bf16[13,24,128]{2,1,0:T(8,128)(2,1)S(1)}, bf16[13,24,128]{2,1,0:T(8,128)(2,1)S(1)}, u32[]{:S(2)}, u32[]{:S(2)}) collective-permute-start(bf16[13,24,128]{2,1,0:T(8,128)(2,1)S(1)} %collective-permute-done.2.refs_1_), channel_id=1, source_target_pairs={{0,1},{1,0},{2,3},{3,2},{4,5},{5,4},{6,7},{7,6},{8,9},{9,8},{10,11... | collective-permute-start | bytes 239624 | tf_op jit(solution)/shard_map/ppermute | solution.py:421
  15.6 2.3 %collective-permute-start.7 = (bf16[13,24,128]{2,1,0:T(8,128)(2,1)S(1)}, bf16[13,24,128]{2,1,0:T(8,128)(2,1)S(1)}, u32[]{:S(2)}, u32[]{:S(2)}) collective-permute-start(bf16[13,24,128]{2,1,0:T(8,128)(2,1)S(1)} %collective-permute-done.3.refs_2_), channel_id=1, source_target_pairs={{0,1},{1,0},{2,3},{3,2},{4,5},{5,4},{6,7},{7,6},{8,9},{9,8},{10,11... | collective-permute-start | bytes 239624 | tf_op jit(solution)/shard_map/ppermute | solution.py:421
  16.8 2.1 %collective-permute-start.8 = (bf16[13,24,128]{2,1,0:T(8,128)(2,1)S(1)}, bf16[13,24,128]{2,1,0:T(8,128)(2,1)S(1)}, u32[]{:S(2)}, u32[]{:S(2)}) collective-permute-start(bf16[13,24,128]{2,1,0:T(8,128)(2,1)S(1)} %collective-permute-done.4.refs_3_), channel_id=1, source_target_pairs={{0,1},{1,0},{2,3},{3,2},{4,5},{5,4},{6,7},{7,6},{8,9},{9,8},{10,11... | collective-permute-start | bytes 239624 | tf_op jit(solution)/shard_map/ppermute | solution.py:421
  24.8 9.7 %collective-permute-start.9 = (bf16[8,24,128]{2,1,0:T(8,128)(2,1)S(1)}, bf16[8,24,128]{2,1,0:T(8,128)(2,1)S(1)}, u32[]{:S(2)}, u32[]{:S(2)}) collective-permute-start(bf16[8,24,128]{2,1,0:T(8,128)(2,1)S(1)} %get-tuple-element.30), channel_id=1, source_target_pairs={{0,1},{1,0},{2,3},{3,2},{4,5},{5,4},{6,7},{7,6},{8,9},{9,8},{10,11... | collective-permute-start | bytes 147464 | tf_op jit(solution)/shard_map/ppermute | solution.py:374
  25.2 19.3 %all-to-all-start = ((f32[128,1,256]{2,1,0:T(1,128)}), f32[128,1,256]{2,1,0:T(1,128)S(1)}, u32[]{:S(2)}, u32[]{:S(2)}) async-start(f32[128,1,256]{2,1,0:T(1,128)} %get-tuple-element.33), calls=%async_computation | async-start | bytes 262144 | tf_op jit(solution)/shard_map/all_to_all | solution.py:449
  34.5 6.5 %collective-permute-start.12 = (bf16[4,24,128]{2,1,0:T(8,128)(2,1)S(1)}, bf16[4,24,128]{2,1,0:T(8,128)(2,1)S(1)}, u32[]{:S(2)}, u32[]{:S(2)}) collective-permute-start(bf16[4,24,128]{2,1,0:T(8,128)(2,1)S(1)} %shard_map.88.refs_0_), channel_id=1, source_target_pairs={{0,4},{1,5},{2,6},{3,7},{4,0},{5,1},{6,2},{7,3},{8,12},{9,13},{10,... | collective-permute-start | bytes 73736 | tf_op jit(solution)/shard_map/ppermute | solution.py:453
  37.5 3.5 %collective-permute-start.10 = (bf16[4,24,128]{2,1,0:T(8,128)(2,1)S(1)}, bf16[4,24,128]{2,1,0:T(8,128)(2,1)S(1)}, u32[]{:S(2)}, u32[]{:S(2)}) collective-permute-start(bf16[4,24,128]{2,1,0:T(8,128)(2,1)S(1)} %get-tuple-element.31), channel_id=1, source_target_pairs={{0,2},{1,7},{2,4},{3,1},{4,6},{5,3},{6,0},{7,5},{8,10},{9,15},{10,... | collective-permute-start | bytes 73736 | tf_op jit(solution)/shard_map/ppermute | solution.py:457
  38.3 4.8 %collective-permute-start.11 = (bf16[4,24,128]{2,1,0:T(8,128)(2,1)S(1)}, bf16[4,24,128]{2,1,0:T(8,128)(2,1)S(1)}, u32[]{:S(2)}, u32[]{:S(2)}) collective-permute-start(bf16[4,24,128]{2,1,0:T(8,128)(2,1)S(1)} %get-tuple-element.32), channel_id=1, source_target_pairs={{0,3},{1,6},{2,5},{3,0},{4,7},{5,2},{6,1},{7,4},{8,11},{9,14},{10,... | collective-permute-start | bytes 73736 | tf_op jit(solution)/shard_map/ppermute | solution.py:458
